TPU v7x, 32 devices: a whole 2x2x4 slice. The times are simulated.
32 devices in a mesh: section: 2 (over core), dp: 4 (over z), mp: 4 (over y, x).
Axes of the slice: x: 2, y: 2, z: 4, core: 2. Of those that a mesh axis runs over, the one named last changes fastest.
Arguments:
- patches: bfloat16 [64, 16, 1024], P('mp', 'dp'), may hold values from -6 to 6
- counts: int32 [16], P('dp'), may hold values from 35 to 63
- patch_index: int32 [64, 16], P('mp', 'dp'), may hold values from 0 to 195, as said below
- scale_level: int32 [16], P('dp'), may hold values from 0 to 7
- enc_gain_one: bfloat16 [1024], replicated, may hold values from 0.25 to 1.75
- enc_qkv: bfloat16 [1024, 3, 1024], P(None, None, 'mp'), may hold values from -0.1875 to 0.1875
- enc_out: bfloat16 [1024, 1024], P(None, 'mp'), may hold values from -0.5 to 0.5
- enc_gain_two: bfloat16 [1024], replicated, may hold values from 0.25 to 1.75
- enc_up: bfloat16 [1024, 4096], P(None, 'mp'), may hold values from -0.1875 to 0.1875
- enc_down: bfloat16 [1024, 4096], P(None, 'mp'), may hold values from -0.09375 to 0.09375
- w_proj: bfloat16 [1024, 512], replicated, may hold values from -0.1875 to 0.1875
- mask_token: bfloat16 [512], replicated, may hold values from -4 to 4
- pos_table: bfloat16 [8, 196, 512], replicated, may hold values from -1 to 1
- dec_gain_one: bfloat16 [512], replicated, may hold values from 0.25 to 1.75
- dec_qkv: bfloat16 [512, 3, 512], P(None, None, 'mp'), may hold values from -0.25 to 0.25
- dec_out: bfloat16 [512, 512], P(None, 'mp'), may hold values from -1 to 1
- dec_gain_two: bfloat16 [512], replicated, may hold values from 0.25 to 1.75
- dec_up: bfloat16 [512, 2048], P(None, 'mp'), may hold values from -0.25 to 0.25
- dec_down: bfloat16 [512, 2048], P(None, 'mp'), may hold values from -0.125 to 0.125
- decoded_grad: bfloat16 [196, 16, 512], P('mp', 'dp'), may hold values from -6 to 6
Outputs:
- decoded: float32 [196, 16, 512], P(None, 'dp', ('section', 'mp'))
- patches_grad: float32 [64, 16, 1024], P(None, 'dp', ('section', 'mp'))
- enc_qkv_grad: float32 [1024, 3, 1024], P(('section', 'dp'), None, 'mp')
- enc_out_grad: float32 [1024, 1024], P(('section', 'dp'), 'mp')
- enc_up_grad: float32 [1024, 4096], P(('section', 'dp'), 'mp')
- enc_down_grad: float32 [1024, 4096], P(('section', 'dp'), 'mp')
- dec_qkv_grad: float32 [512, 3, 512], P(('section', 'dp'), None, 'mp')
- dec_out_grad: float32 [512, 512], P(('section', 'dp'), 'mp')
- dec_up_grad: float32 [512, 2048], P(('section', 'dp'), 'mp')
- dec_down_grad: float32 [512, 2048], P(('section', 'dp'), 'mp')
- proj_grad: float32 [1024, 512], replicated
- enc_gain_one_grad: float32 [1024], replicated
- enc_gain_two_grad: float32 [1024], replicated
- dec_gain_one_grad: float32 [512], replicated
- dec_gain_two_grad: float32 [512], replicated
- mask_token_grad: float32 [512], replicated
Inputs may be any that keep to these rules, and one draw needn't show every extreme that they name: `patch_index`: within each image the 64 entries are distinct patch numbers; slots at or past the image's count are padding.
All inputs are finite; a program needn't handle non-finite values.
Results may differ from a plain program's by a relative error of at most 0.035.
Values may be sent and summed in bfloat16 or wider, within the bound.
A program may use at most 320 MiB of HBM per device.

v0:
```python
import math

import jax
import jax.numpy as jnp
from jax import lax
from jax.sharding import PartitionSpec as P

HEAD = 64
DEC_HEAD = 32


eps = 1e-06


def norm_rows(values):
    average = jnp.mean(values, axis=-1, keepdims=True)
    centered = values - average
    variance = jnp.mean(centered * centered, axis=-1, keepdims=True)
    inverse = lax.rsqrt(variance + eps)
    return (centered * inverse, inverse)


def norm_back(normal, inverse, gain_vec, gradient):
    weighted = gradient * gain_vec
    first_term = jnp.mean(weighted, axis=-1, keepdims=True)
    second_term = jnp.mean(weighted * normal, axis=-1, keepdims=True)
    return (
        inverse * (weighted - first_term - normal * second_term),
        jnp.sum(gradient * normal, axis=(0, 1)),
    )


def spread(values):
    return lax.all_gather(values, "mp", axis=0, tiled=True)


def collect(values):
    return lax.psum_scatter(values, "mp", scatter_dimension=0, tiled=True)


def spare_of(work):
    return lambda: jax.tree.map(jnp.zeros_like, work())


def head_view(qkv_rows, head_size):
    return qkv_rows.reshape(
        qkv_rows.shape[0], qkv_rows.shape[1], 3, qkv_rows.shape[3] // head_size, head_size
    )


def score_rows(queries, key_rows, visible, head_size):
    scores = jnp.einsum(
        "sbhe,tbhe->bhst", queries, key_rows, preferred_element_type=jnp.float32
    ) * (1.0 / math.sqrt(head_size))
    return jnp.where(visible[:, None, None, :], scores, -1e30)


def attend(qkv_rows, visible, head_size):
    heads_view = head_view(qkv_rows, head_size)
    scores = score_rows(heads_view[:, :, 0], heads_view[:, :, 1], visible, head_size)
    highest = jnp.max(scores, axis=-1, keepdims=True)
    weights = jnp.exp(scores - highest)
    denominator = jnp.sum(weights, axis=-1, keepdims=True)
    probability = (weights / denominator).astype(jnp.bfloat16)
    context = jnp.einsum(
        "bhst,tbhe->sbhe", probability, heads_view[:, :, 2], preferred_element_type=jnp.float32
    )
    context = context.reshape(qkv_rows.shape[0], qkv_rows.shape[1], qkv_rows.shape[3]).astype(
        jnp.bfloat16
    )
    return (context, highest + jnp.log(denominator))


def attend_back(qkv_rows, visible, logsum, grad_context, head_size):
    heads_view = head_view(qkv_rows, head_size)
    queries = heads_view[:, :, 0]
    key_rows = heads_view[:, :, 1]
    value_rows = heads_view[:, :, 2]
    probability = jnp.exp(score_rows(queries, key_rows, visible, head_size) - logsum)
    grad_heads = grad_context.reshape(queries.shape)
    grad_values = jnp.einsum(
        "bhst,sbhe->tbhe",
        probability.astype(jnp.bfloat16),
        grad_heads,
        preferred_element_type=jnp.float32,
    )
    grad_probs = jnp.einsum(
        "sbhe,tbhe->bhst", grad_heads, value_rows, preferred_element_type=jnp.float32
    )
    row_inner = jnp.sum(grad_probs * probability, axis=-1, keepdims=True)
    grad_scores = (probability * (grad_probs - row_inner)).astype(jnp.bfloat16)
    score_scale = 1.0 / math.sqrt(head_size)
    grad_queries = (
        jnp.einsum("bhst,tbhe->sbhe", grad_scores, key_rows, preferred_element_type=jnp.float32)
        * score_scale
    )
    grad_keys = (
        jnp.einsum("bhst,sbhe->tbhe", grad_scores, queries, preferred_element_type=jnp.float32)
        * score_scale
    )
    stacked = jnp.stack([grad_queries, grad_keys, grad_values], axis=2)
    return stacked.reshape(qkv_rows.shape).astype(jnp.bfloat16)


def attention_local(normed_one, visible, w_qkv, w_out, head_size):
    qkv_rows = jnp.einsum(
        "sbw,wcf->sbcf", normed_one, w_qkv, preferred_element_type=jnp.float32
    ).astype(jnp.bfloat16)
    context, logsum = attend(qkv_rows, visible, head_size)
    mixed_terms = jnp.einsum("sbf,wf->sbw", context, w_out, preferred_element_type=jnp.float32)
    return (qkv_rows, context, logsum, mixed_terms)


def feed_local(normed_two, w_up, w_down):
    upper_in = jnp.einsum("sbw,wf->sbf", normed_two, w_up, preferred_element_type=jnp.float32)
    hidden = jax.nn.gelu(upper_in, approximate=False).astype(jnp.bfloat16)
    return (upper_in, jnp.einsum("sbf,wf->sbw", hidden, w_down, preferred_element_type=jnp.float32))


def feed_back_local(grad_full, normed_two, upper_in, w_up, w_down):
    value_out, gelu_pull = jax.vjp(
        lambda argument: jax.nn.gelu(argument, approximate=False), upper_in
    )
    hidden = value_out.astype(jnp.bfloat16)
    grad_down_w = jnp.einsum("sbw,sbf->wf", grad_full, hidden, preferred_element_type=jnp.float32)
    grad_hidden = jnp.einsum("sbw,wf->sbf", grad_full, w_down, preferred_element_type=jnp.float32)
    grad_upper = gelu_pull(grad_hidden)[0].astype(jnp.bfloat16)
    grad_up_w = jnp.einsum(
        "sbw,sbf->wf", normed_two, grad_upper, preferred_element_type=jnp.float32
    )
    grad_terms = jnp.einsum("sbf,wf->sbw", grad_upper, w_up, preferred_element_type=jnp.float32)
    return (grad_up_w, grad_down_w, grad_terms)


def attention_back_local(
    grad_full, qkv_rows, context, logsum, visible, normed_one, w_qkv, w_out, head_size
):
    grad_out_w = jnp.einsum("sbw,sbf->wf", grad_full, context, preferred_element_type=jnp.float32)
    grad_context = jnp.einsum(
        "sbw,wf->sbf", grad_full, w_out, preferred_element_type=jnp.float32
    ).astype(jnp.bfloat16)
    grad_qkv = attend_back(qkv_rows, visible, logsum, grad_context, head_size)
    grad_qkv_w = jnp.einsum(
        "sbw,sbcf->wcf", normed_one, grad_qkv, preferred_element_type=jnp.float32
    )
    grad_normed = jnp.einsum("sbcf,wcf->sbw", grad_qkv, w_qkv, preferred_element_type=jnp.float32)
    return (grad_qkv_w, grad_out_w, grad_normed)


def on_device(
    patches,
    counts,
    patch_index,
    scale_level,
    enc_gain_one,
    enc_qkv,
    enc_out,
    enc_gain_two,
    enc_up,
    enc_down,
    w_proj,
    mask_token,
    pos_table,
    dec_gain_one,
    dec_qkv,
    dec_out,
    dec_gain_two,
    dec_up,
    dec_down,
    decoded_grad,
):
    data_ways = lax.axis_size("dp")
    model_ways = lax.axis_size("mp")
    slot_rows = patches.shape[0]
    images = patches.shape[1]
    grid_rows = decoded_grad.shape[0]
    dec_width = decoded_grad.shape[2]
    slot_count = slot_rows * model_ways
    grid_count = grid_rows * model_ways
    per_peer = images // data_ways
    slot_start = lax.axis_index("mp") * slot_rows
    grid_start = lax.axis_index("mp") * grid_rows
    is_encoder = lax.axis_index("section") == 0
    visible = jnp.arange(slot_count, dtype=jnp.int32)[None, :] < counts[:, None]
    all_visible = jnp.ones((images, grid_count), dtype=bool)
    enc_g1 = enc_gain_one.astype(jnp.float32)
    enc_g2 = enc_gain_two.astype(jnp.float32)
    dec_g1 = dec_gain_one.astype(jnp.float32)
    dec_g2 = dec_gain_two.astype(jnp.float32)
    token_vec = mask_token.astype(jnp.float32)

    def on_encoder(work):
        return lax.cond(is_encoder, work, spare_of(work))

    def on_decoder(work):
        return lax.cond(is_encoder, spare_of(work), work)

    full_in = spread(patches)

    def enc_attention():
        normal_one, inverse_one = norm_rows(full_in.astype(jnp.float32))
        normed_one = (normal_one * enc_g1).astype(jnp.bfloat16)
        return attention_local(normed_one, visible, enc_qkv, enc_out, HEAD)

    enc_qkv_rows, enc_context, enc_logsum, enc_mixed_terms = on_encoder(enc_attention)
    enc_middle = patches.astype(jnp.float32) + collect(enc_mixed_terms)
    enc_normal_two, enc_inverse_two = norm_rows(enc_middle)
    enc_normed_two = spread((enc_normal_two * enc_g2).astype(jnp.bfloat16))
    enc_upper, enc_down_terms = on_encoder(lambda: feed_local(enc_normed_two, enc_up, enc_down))
    enc_out_low = (enc_middle + collect(enc_down_terms)).astype(jnp.bfloat16)

    def enc_send():
        sent_rows = jnp.einsum(
            "sbw,wf->sbf", enc_out_low, w_proj, preferred_element_type=jnp.float32
        ).astype(jnp.bfloat16)
        live_slot = (slot_start + jnp.arange(slot_rows, dtype=jnp.int32))[:, None] < counts[None, :]
        sent_index = jnp.where(live_slot, patch_index, grid_count)
        packed = (
            sent_rows.reshape(slot_rows, per_peer, data_ways, dec_width),
            sent_index.reshape(slot_rows, per_peer, data_ways),
            scale_level.reshape(1, per_peer, data_ways),
        )
        packed = tuple(
            (jnp.concatenate([jnp.zeros_like(member), member], axis=2) for member in packed)
        )
        return packed

    packed = on_encoder(enc_send)
    received = (
        lax.all_to_all(packed[0], ("section", "dp"), split_axis=2, concat_axis=1, tiled=True),
        lax.all_to_all(packed[1], ("section", "dp"), split_axis=2, concat_axis=1, tiled=True),
        lax.all_to_all(packed[2], ("section", "dp"), split_axis=2, concat_axis=1, tiled=True),
    )
    arrived = (received[0][:, :images, 0], received[1][:, :images, 0], received[2][0, :images, 0])
    arrived_rows, arrived_index, arrived_level = arrived

    def make_onehot():
        return (
            arrived_index[:, :, None] == jnp.arange(grid_count, dtype=jnp.int32)[None, None, :]
        ).astype(jnp.bfloat16)

    def dec_place():
        onehot_low = make_onehot()
        covered = jnp.transpose(jnp.sum(onehot_low.astype(jnp.float32), axis=0))
        placed = jnp.einsum(
            "sbp,sbf->pbf", onehot_low, arrived_rows, preferred_element_type=jnp.float32
        )
        return (placed - covered[:, :, None] * token_vec, covered)

    placed_terms, covered_terms = on_decoder(dec_place)
    placed_rows, covered_rows = collect((placed_terms, covered_terms))
    table_rows = lax.dynamic_slice_in_dim(pos_table, grid_start, grid_rows, 1)
    level_hot = (
        arrived_level[:, None] == jnp.arange(pos_table.shape[0], dtype=jnp.int32)[None, :]
    ).astype(jnp.bfloat16)
    position = jnp.einsum("bl,lpf->pbf", level_hot, table_rows, preferred_element_type=jnp.float32)
    grid_values = placed_rows + token_vec + position
    dec_normal_one, dec_inverse_one = norm_rows(grid_values)
    dec_normed_one = spread((dec_normal_one * dec_g1).astype(jnp.bfloat16))
    dec_qkv_rows, dec_context, dec_logsum, dec_mixed_terms = on_decoder(
        lambda: attention_local(dec_normed_one, all_visible, dec_qkv, dec_out, DEC_HEAD)
    )
    dec_middle = grid_values + collect(dec_mixed_terms)
    dec_normal_two, dec_inverse_two = norm_rows(dec_middle)
    dec_normed_two = spread((dec_normal_two * dec_g2).astype(jnp.bfloat16))

    def dec_feed():
        upper_in, down_terms = feed_local(dec_normed_two, dec_up, dec_down)
        own_rows = lax.dynamic_slice_in_dim(down_terms, grid_start, grid_rows, 0) + dec_middle
        return (upper_in, lax.dynamic_update_slice_in_dim(down_terms, own_rows, grid_start, 0))

    dec_upper, dec_summand = on_decoder(dec_feed)
    decoded = lax.psum_scatter(
        dec_summand.astype(jnp.bfloat16), ("section", "mp"), scatter_dimension=2, tiled=True
    ).astype(jnp.float32)
    dec_grad_full = spread(decoded_grad)
    dec_up_grad, dec_down_grad, dec_two_terms = on_decoder(
        lambda: feed_back_local(dec_grad_full, dec_normed_two, dec_upper, dec_up, dec_down)
    )
    dec_through, dec_gain_two_grad = norm_back(
        dec_normal_two, dec_inverse_two, dec_g2, collect(dec_two_terms)
    )
    dec_grad_middle = decoded_grad.astype(jnp.float32) + dec_through
    dec_middle_full = spread(dec_grad_middle.astype(jnp.bfloat16))
    dec_qkv_grad, dec_out_grad, dec_one_terms = on_decoder(
        lambda: attention_back_local(
            dec_middle_full,
            dec_qkv_rows,
            dec_context,
            dec_logsum,
            all_visible,
            dec_normed_one,
            dec_qkv,
            dec_out,
            DEC_HEAD,
        )
    )
    dec_inner, dec_gain_one_grad = norm_back(
        dec_normal_one, dec_inverse_one, dec_g1, collect(dec_one_terms)
    )
    grad_grid = dec_grad_middle + dec_inner
    grad_token = jnp.sum(grad_grid * (1.0 - covered_rows)[:, :, None], axis=(0, 1))
    grad_grid_full = spread(grad_grid.astype(jnp.bfloat16))

    def dec_return():
        grad_sent = jnp.einsum(
            "sbp,pbf->sbf", make_onehot(), grad_grid_full, preferred_element_type=jnp.float32
        ).astype(jnp.bfloat16)
        return jnp.concatenate([grad_sent, jnp.zeros_like(grad_sent)], axis=1)[:, :, None, :]

    back_rows = on_decoder(dec_return)
    returned = lax.all_to_all(
        back_rows, ("section", "dp"), split_axis=1, concat_axis=2, tiled=True
    )[:, :, data_ways:]
    grad_arrived = returned.reshape(slot_rows, images, dec_width)

    def enc_project_back():
        grad_proj_w = jnp.einsum(
            "sbw,sbf->wf", enc_out_low, grad_arrived, preferred_element_type=jnp.float32
        )
        grad_block = jnp.einsum(
            "sbf,wf->sbw", grad_arrived, w_proj, preferred_element_type=jnp.float32
        )
        return (grad_proj_w, grad_block)

    proj_grad, enc_grad_block = on_encoder(enc_project_back)
    enc_grad_full = spread(enc_grad_block.astype(jnp.bfloat16))
    enc_up_grad, enc_down_grad, enc_two_terms = on_encoder(
        lambda: feed_back_local(enc_grad_full, enc_normed_two, enc_upper, enc_up, enc_down)
    )
    enc_through, enc_gain_two_grad = norm_back(
        enc_normal_two, enc_inverse_two, enc_g2, collect(enc_two_terms)
    )
    enc_grad_middle = enc_grad_block + enc_through
    enc_middle_full = spread(enc_grad_middle.astype(jnp.bfloat16))

    def enc_attention_back():
        normal_one, inverse_one = norm_rows(full_in.astype(jnp.float32))
        normed_one = (normal_one * enc_g1).astype(jnp.bfloat16)
        grad_qkv_w, grad_out_w, grad_normed = attention_back_local(
            enc_middle_full,
            enc_qkv_rows,
            enc_context,
            enc_logsum,
            visible,
            normed_one,
            enc_qkv,
            enc_out,
            HEAD,
        )
        grad_inner, grad_gain_one = norm_back(normal_one, inverse_one, enc_g1, grad_normed)
        own_rows = lax.dynamic_slice_in_dim(grad_inner, slot_start, slot_rows, 0) + enc_grad_middle
        summand = lax.dynamic_update_slice_in_dim(grad_inner, own_rows, slot_start, 0)
        return (grad_qkv_w, grad_out_w, grad_gain_one, summand)

    enc_qkv_grad, enc_out_grad, enc_gain_one_grad, in_summand = on_encoder(enc_attention_back)
    patches_grad = lax.psum_scatter(
        in_summand.astype(jnp.bfloat16), ("section", "mp"), scatter_dimension=2, tiled=True
    ).astype(jnp.float32)
    enc_gain_two_grad = jnp.where(is_encoder, enc_gain_two_grad, 0.0)
    dec_gain_one_grad = jnp.where(is_encoder, 0.0, dec_gain_one_grad)
    dec_gain_two_grad = jnp.where(is_encoder, 0.0, dec_gain_two_grad)
    grad_token = jnp.where(is_encoder, 0.0, grad_token)
    sharded = (
        lax.psum_scatter(enc_qkv_grad, ("section", "dp"), scatter_dimension=0, tiled=True),
        lax.psum_scatter(enc_out_grad, ("section", "dp"), scatter_dimension=0, tiled=True),
        lax.psum_scatter(enc_up_grad, ("section", "dp"), scatter_dimension=0, tiled=True),
        lax.psum_scatter(enc_down_grad, ("section", "dp"), scatter_dimension=0, tiled=True),
        lax.psum_scatter(dec_qkv_grad, ("section", "dp"), scatter_dimension=0, tiled=True),
        lax.psum_scatter(dec_out_grad, ("section", "dp"), scatter_dimension=0, tiled=True),
        lax.psum_scatter(dec_up_grad, ("section", "dp"), scatter_dimension=0, tiled=True),
        lax.psum_scatter(dec_down_grad, ("section", "dp"), scatter_dimension=0, tiled=True),
    )
    shared = lax.psum(
        (
            proj_grad,
            enc_gain_one_grad,
            enc_gain_two_grad,
            dec_gain_one_grad,
            dec_gain_two_grad,
            grad_token,
        ),
        ("section", "dp", "mp"),
    )
    return (
        decoded,
        patches_grad,
        sharded[0],
        sharded[1],
        sharded[2],
        sharded[3],
        sharded[4],
        sharded[5],
        sharded[6],
        sharded[7],
        shared[0],
        shared[1],
        shared[2],
        shared[3],
        shared[4],
        shared[5],
    )


def solution(mesh):
    placed = (
        P("mp", "dp", None),
        P("dp"),
        P("mp", "dp"),
        P("dp"),
        P(),
        P(None, None, "mp"),
        P(None, "mp"),
        P(),
        P(None, "mp"),
        P(None, "mp"),
        P(),
        P(),
        P(),
        P(),
        P(None, None, "mp"),
        P(None, "mp"),
        P(),
        P(None, "mp"),
        P(None, "mp"),
        P("mp", "dp", None),
    )
    return jax.shard_map(
        on_device,
        mesh=mesh,
        in_specs=placed,
        out_specs=(
            P(None, "dp", ("section", "mp")),
            P(None, "dp", ("section", "mp")),
            P(("section", "dp"), None, "mp"),
            P(("section", "dp"), "mp"),
            P(("section", "dp"), "mp"),
            P(("section", "dp"), "mp"),
            P(("section", "dp"), None, "mp"),
            P(("section", "dp"), "mp"),
            P(("section", "dp"), "mp"),
            P(("section", "dp"), "mp"),
            P(),
            P(),
            P(),
            P(),
            P(),
            P(),
        ),
        check_vma=False,
    )
```

profile of v0, /device:TPU:0, one launch (start us, length us, event | category | flops | bytes accessed | tf_op | source)
XLA Modules:
  0.0 1278.2 jit_solution(12715782838565168949)
XLA Ops:
  10.8 11.5 all_gather.27
  22.3 10.2 conditional.12
  33.6 28.1 %reduce-scatter.19.cloned.1.call-done = f32[16,4,1024]{2,0,1:T(8,128)} async-done(((f32[64,4,1024]{2,0,1:T(8,128)}), f32[16,4,1024]{2,0,1:T(8,128)}) %reduce-scatter.19.cloned.1.call-update) | async-done | bytes 262160 | tf_op jit(solution)/shard_map/reduce_scatter | solution.py:38
  63.1 10.6 all_gather.28
  73.7 9.0 conditional.13
  82.7 27.9 %reduce-scatter.21.cloned.1.call-done = f32[16,4,1024]{2,0,1:T(8,128)} async-done(((f32[64,4,1024]{2,0,1:T(8,128)}), f32[16,4,1024]{2,0,1:T(8,128)}) %reduce-scatter.21.cloned.1.call-update) | async-done | bytes 262160 | tf_op jit(solution)/shard_map/reduce_scatter | solution.py:38
  113.7 10.0 all_to_all.48
  149.4 50.2 %all-reduce.18.cloned.1.call-done = f32[196,4,512]{2,1,0:T(4,128)} async-done(((f32[196,4,512]{2,1,0:T(4,128)}), f32[196,4,512]{2,1,0:T(4,128)}) %all-reduce.18.cloned.1.call-update) | async-done | bytes 1605648
  201.6 12.0 all_gather.29
  219.2 14.8 %all_gather.31 = bf16[196,4,512]{2,1,0:T(4,128)(2,1)S(1)} all-gather(bf16[49,4,512]{2,1,0:T(4,128)(2,1)S(1)} %copy-done.20), channel_id=1, replica_groups=mesh['section'=2,'dp'=4,'mp'=4] {'mp'}, dimensions={0}, use_global_device_ids=true | all-gather | bytes 1003520 | tf_op jit(solution)/shard_map/all_gather | solution.py:34
  234.0 52.8 %all-reduce.20.cloned.1.call-done = f32[196,4,512]{2,1,0:T(4,128)} async-done(((f32[196,4,512]{2,1,0:T(4,128)}), f32[196,4,512]{2,1,0:T(4,128)}) %all-reduce.20.cloned.1.call-update) | async-done | bytes 1605648
  288.5 12.0 all_gather.30
  310.3 78.5 %all-reduce.22.cloned.1.call-done = f32[196,4,512]{2,1,0:T(4,128)} async-done(((f32[196,4,512]{2,1,0:T(4,128)}), f32[196,4,512]{2,1,0:T(4,128)}) %all-reduce.22.cloned.1.call-update) | async-done | bytes 1605648
  392.3 11.4 all_gather.32
  419.1 64.3 %all-reduce.24.cloned.1.call-done = f32[196,4,512]{2,1,0:T(4,128)} async-done(((f32[196,4,512]{2,1,0:T(4,128)}), f32[196,4,512]{2,1,0:T(4,128)}) %all-reduce.24.cloned.1.call-update) | async-done | bytes 1605648
  486.2 11.5 all_gather.33
  513.1 9.4 all_gather.34
  522.5 15.7 %conditional.22 = (f32[1024,1024]{0,1:T(8,128)}, f32[1024,1024]{0,1:T(8,128)}, f32[64,4,1024]{2,0,1:T(8,128)S(1)}) conditional(s32[]{:T(128)} %convert_element_type.168, () %tuple.123, (f32[64,4,1024]{2,0,1:T(8,128)}, bf16[64,4,1024]{2,0,1:T(8,128)(2,1)S(1)}, bf16[1024,1024]{1,0:T(8,128)(2,1)}, bf16[64,4,1024]{2,0,1:T(8,128)(2,1)}, ...), branch_computations={%region_45.46_spmd, %region_46.47_spmd} | conditional | flops 2183397376 | bytes 27263028 | solution.py:193
  543.4 21.3 %reduce-scatter.23.cloned.1.call-done = f32[16,4,1024]{2,0,1:T(8,128)} async-done(((f32[64,4,1024]{2,0,1:T(8,128)}), f32[16,4,1024]{2,0,1:T(8,128)}) %reduce-scatter.23.cloned.1.call-update) | async-done | bytes 262160 | tf_op jit(solution)/shard_map/reduce_scatter | solution.py:38
  567.7 9.9 all_gather.35
  577.7 20.5 %conditional.23 = (f32[1024,3,256]{2,0,1:T(8,128)}, f32[1024,256]{1,0:T(8,128)S(1)}, f32[1024]{0:T(1024)S(1)}, f32[64,4,1024]{2,0,1:T(8,128)}) conditional(s32[]{:T(128)} %convert_element_type.168, () %tuple.114, (bf16[64,4,1024]{2,0,1:T(8,128)(2,1)S(1)}, f32[1024]{0:T(1024)}, pred[4,64]{1,0:T(4,128)(4,1)}, bf16[64,4,3,256]{3,0,2,1:T(8,128)(2,1)}, ...), branch_computations={%region_50.51_spmd, %region_51.58_spmd} | conditional | flops 1125644544 | bytes 23512476 | solution.py:193
  599.9 26.8 %copy.420 = bf16[64,4,1024]{1,0,2:T(8,128)(2,1)} copy(bf16[64,4,1024]{2,0,1:T(8,128)(2,1)S(1)} %convert_element_type.188) | data formatting | bytes 1048576
  626.7 32.6 %reshape.287 = bf16[1024,256]{1,0:T(8,128)(2,1)} reshape(bf16[1024,64,4]{2,1,0:T(8,128)(2,1)} %bitcast.286) | data formatting | bytes 1048576
  680.0 40.2 %all-reduce.9 = (f32[1024]{0:T(1024)}, f32[1024]{0:T(1024)}, f32[512]{0:T(512)}, f32[512]{0:T(512)}, f32[512]{0:T(512)}) all-reduce(f32[1024]{0:T(1024)S(1)} %get-tuple-element.261, f32[1024]{0:T(1024)S(1)} %broadcast_select_fusion, f32[512]{0:T(512)S(1)} %get-tuple-element.574, ...), channel_id=1, replica_groups=mesh['section'=2,'dp'=4,'mp'=4] {'section','dp','mp'}, use_global_device_ids=true, to_apply=%region_68.69 | all-reduce | flops 3584 | bytes 28672 | tf_op jit(solution)/shard_map/psum | solution.py:374
  731.7 37.8 %reduce-scatter.39.cloned.1.call-done = f32[64,512]{1,0:T(8,128)} async-done(((f32[512,512]{1,0:T(8,128)}), f32[64,512]{1,0:T(8,128)}) %reduce-scatter.39.cloned.1.call-update) | async-done | bytes 131088 | tf_op jit(solution)/shard_map/reduce_scatter | solution.py:372
  769.4 33.3 %reduce-scatter.35.cloned.1.call-done = f32[64,128]{1,0:T(8,128)} async-done(((f32[512,128]{1,0:T(8,128)}), f32[64,128]{1,0:T(8,128)}) %reduce-scatter.35.cloned.1.call-update) | async-done | bytes 32784 | tf_op jit(solution)/shard_map/reduce_scatter | solution.py:370
  802.8 35.7 %reduce-scatter.33.cloned.1.call-done = f32[64,3,128]{2,0,1:T(8,128)} async-done(((f32[512,3,128]{2,0,1:T(8,128)}), f32[64,3,128]{2,0,1:T(8,128)}) %reduce-scatter.33.cloned.1.call-update) | async-done | bytes 98320 | tf_op jit(solution)/shard_map/reduce_scatter | solution.py:369
  838.4 138.5 %all-reduce.16.cloned.1.call-done = f32[1024,512]{1,0:T(8,128)} async-done(((f32[1024,512]{1,0:T(8,128)}), f32[1024,512]{1,0:T(8,128)}) %all-reduce.16.cloned.1.call-update) | async-done | bytes 2097168 | tf_op jit(solution)/shard_map/psum | solution.py:374
  976.9 37.3 %reduce-scatter.27.cloned.1.call-done = f32[128,256]{1,0:T(8,128)} async-done(((f32[1024,256]{1,0:T(8,128)}), f32[128,256]{1,0:T(8,128)}) %reduce-scatter.27.cloned.1.call-update) | async-done | bytes 131088 | tf_op jit(solution)/shard_map/reduce_scatter | solution.py:366
  1014.3 70.6 %reduce-scatter.25.cloned.1.call-done = f32[128,3,256]{2,0,1:T(8,128)} async-done(((f32[1024,3,256]{2,0,1:T(8,128)}), f32[128,3,256]{2,0,1:T(8,128)}) %reduce-scatter.25.cloned.1.call-update) | async-done | bytes 393232 | tf_op jit(solution)/shard_map/reduce_scatter | solution.py:365
  1084.9 91.2 %reduce-scatter.29.cloned.1.call-done = f32[128,1024]{1,0:T(8,128)} async-done(((f32[1024,1024]{1,0:T(8,128)}), f32[128,1024]{1,0:T(8,128)}) %reduce-scatter.29.cloned.1.call-update) | async-done | bytes 524304 | tf_op jit(solution)/shard_map/reduce_scatter | solution.py:367
  1176.0 91.6 %reduce-scatter.31.cloned.1.call-done = f32[128,1024]{1,0:T(8,128)} async-done(((f32[1024,1024]{1,0:T(8,128)}), f32[128,1024]{1,0:T(8,128)}) %reduce-scatter.31.cloned.1.call-update) | async-done | bytes 524304 | tf_op jit(solution)/shard_map/reduce_scatter | solution.py:368
  (259 shorter events, 205.3 us)
Async XLA Ops:
  7.2 192.4 %copy-start = (bf16[8,196,512]{2,0,1:T(8,128)(2,1)S(1)}, bf16[8,196,512]{2,0,1:T(8,128)(2,1)}, u32[]{:S(2)}) copy-start(bf16[8,196,512]{2,0,1:T(8,128)(2,1)} %param.56) | copy-start | bytes 4816900
  7.2 54.5 %reduce-scatter.19.cloned.1.call-start = ((), (), s32[]{:S(2)}) async-start(), calls=%async_computation.17 | async-start | bytes 1310720 | tf_op jit(solution)/shard_map/reduce_scatter | solution.py:38
  32.5 41.2 %copy-start.34 = (f32[4,4,64,1]{2,1,0,3:T(4,128)}, f32[4,4,64,1]{2,1,0,3:T(4,128)S(1)}, u32[]{:S(2)}) copy-start(f32[4,4,64,1]{2,1,0,3:T(4,128)S(1)} %get-tuple-element.240) | copy-start | bytes 12292
  33.5 77.1 %reduce-scatter.21.cloned.1.call-start = ((), (), s32[]{:S(2)}) async-start(), calls=%async_computation.18 | async-start | bytes 1310720 | tf_op jit(solution)/shard_map/reduce_scatter | solution.py:38
  82.7 29.6 %copy-start.37 = (s32[16,4]{0,1:T(4,128)S(1)}, s32[16,4]{0,1:T(4,128)}, u32[]{:S(2)}) copy-start(s32[16,4]{0,1:T(4,128)} %param.46) | copy-start | bytes 772
  82.7 29.6 %copy-start.41 = (s32[4]{0:T(128)S(1)}, s32[4]{0:T(128)}, u32[]{:S(2)}) copy-start(s32[4]{0:T(128)} %param.45) | copy-start | bytes 52
  82.7 29.6 %copy-start.45 = (s32[4]{0:T(128)S(1)}, s32[4]{0:T(128)}, u32[]{:S(2)}) copy-start(s32[4]{0:T(128)} %param.47) | copy-start | bytes 52
  82.7 44.4 %copy-start.38 = (bf16[512]{0:T(512)(128)(2,1)S(1)}, bf16[512]{0:T(512)(128)(2,1)}, u32[]{:S(2)}) copy-start(bf16[512]{0:T(512)(128)(2,1)} %param.55) | copy-start | bytes 3076
  123.7 10.3 all-to-all-start.1
  127.0 72.6 %all-reduce.18.cloned.1.call-start = ((), (), s32[]{:S(2)}) async-start(), calls=%async_computation.31 | async-start | bytes 3211264
  139.0 74.6 %copy-start.31 = (f32[512]{0:T(512)}, f32[512]{0:T(512)S(1)}, u32[]{:S(2)}) copy-start(f32[512]{0:T(512)S(1)} %convert_element_type.175) | copy-start | bytes 6148
  140.3 8.9 all-to-all-start.2
  143.7 143.1 %all-reduce.20.cloned.1.call-start = ((), (), s32[]{:S(2)}) async-start(), calls=%async_computation.32 | async-start | bytes 3211264
  149.4 64.2 %copy-start.28 = (bf16[512,128]{1,0:T(8,128)(2,1)S(1)}, bf16[512,128]{1,0:T(8,128)(2,1)}, u32[]{:S(2)}) copy-start(bf16[512,128]{1,0:T(8,128)(2,1)} %param.59) | copy-start | bytes 393220
  219.1 169.6 %all-reduce.22.cloned.1.call-start = ((), (), s32[]{:S(2)}) async-start(), calls=%async_computation.33 | async-start | bytes 3211264
  310.3 173.0 %all-reduce.24.cloned.1.call-start = ((), (), s32[]{:S(2)}) async-start(), calls=%async_computation.34 | async-start | bytes 3211264
  409.9 73.4 %copy-start.32 = (f32[512]{0:T(512)S(1)}, f32[512]{0:T(512)}, u32[]{:S(2)}) copy-start(f32[512]{0:T(512)} %copy-done.31) | copy-start | bytes 6148
  498.4 11.6 all-to-all-start.3
  503.0 61.8 %reduce-scatter.23.cloned.1.call-start = ((), (), s32[]{:S(2)}) async-start(), calls=%async_computation.19 | async-start | bytes 1310720 | tf_op jit(solution)/shard_map/reduce_scatter | solution.py:38
  539.3 138.6 %reduce-scatter.41.cloned.1.call-start = ((), (), s32[]{:S(2)}) async-start(), calls=%async_computation.29 | async-start | bytes 1032192
  543.3 34.3 %copy-start.16 = (bf16[1024,256]{1,0:T(8,128)(2,1)S(1)}, bf16[1024,256]{1,0:T(8,128)(2,1)}, u32[]{:S(2)}) copy-start(bf16[1024,256]{1,0:T(8,128)(2,1)} %param.50) | copy-start | bytes 1572868
  543.3 34.3 %copy-start.35 = (f32[4,4,64,1]{2,1,0,3:T(4,128)S(1)}, f32[4,4,64,1]{2,1,0,3:T(4,128)}, u32[]{:S(2)}) copy-start(f32[4,4,64,1]{2,1,0,3:T(4,128)} %copy-done.34) | copy-start | bytes 12292
  543.4 176.9 %reduce-scatter.43.cloned.1.call-start = ((), (), s32[]{:S(2)}) async-start(), calls=%async_computation.30 | async-start | bytes 589824
  659.3 72.4 %reduce-scatter.37.cloned.1.call-start = ((), (), s32[]{:S(2)}) async-start(), calls=%async_computation.26 | async-start | bytes 1179648 | tf_op jit(solution)/shard_map/reduce_scatter | solution.py:371
  662.0 107.4 %reduce-scatter.39.cloned.1.call-start = ((), (), s32[]{:S(2)}) async-start(), calls=%async_computation.27 | async-start | bytes 1179648 | tf_op jit(solution)/shard_map/reduce_scatter | solution.py:372
  663.4 139.3 %reduce-scatter.35.cloned.1.call-start = ((), (), s32[]{:S(2)}) async-start(), calls=%async_computation.25 | async-start | bytes 294912 | tf_op jit(solution)/shard_map/reduce_scatter | solution.py:370
  664.0 174.4 %reduce-scatter.33.cloned.1.call-start = ((), (), s32[]{:S(2)}) async-start(), calls=%async_computation.24 | async-start | bytes 884736 | tf_op jit(solution)/shard_map/reduce_scatter | solution.py:369
  665.2 311.7 %all-reduce.16.cloned.1.call-start = ((), (), s32[]{:S(2)}) async-start(), calls=%async_computation.28 | async-start | bytes 4194304 | tf_op jit(solution)/shard_map/psum | solution.py:374
  665.8 348.5 %reduce-scatter.27.cloned.1.call-start = ((), (), s32[]{:S(2)}) async-start(), calls=%async_computation.21 | async-start | bytes 1179648 | tf_op jit(solution)/shard_map/reduce_scatter | solution.py:366
  666.4 418.5 %reduce-scatter.25.cloned.1.call-start = ((), (), s32[]{:S(2)}) async-start(), calls=%async_computation.20 | async-start | bytes 3538944 | tf_op jit(solution)/shard_map/reduce_scatter | solution.py:365
  667.0 509.1 %reduce-scatter.29.cloned.1.call-start = ((), (), s32[]{:S(2)}) async-start(), calls=%async_computation.22 | async-start | bytes 4718592 | tf_op jit(solution)/shard_map/reduce_scatter | solution.py:367
  672.5 595.1 %reduce-scatter.31.cloned.1.call-start = ((), (), s32[]{:S(2)}) async-start(), calls=%async_computation.23 | async-start | bytes 4718592 | tf_op jit(solution)/shard_map/reduce_scatter | solution.py:368
  (26 other events, 188.2 us)
Sparse Core Ops, SparseCore 0:
  33.6 28.0 reduce-scatter.18
  82.8 27.7 reduce-scatter.20
  139.1 60.4 all-reduce.17
  219.2 67.4 all-reduce.19
  310.4 78.3 all-reduce.21
  410.0 73.2 all-reduce.23
  539.4 25.2 reduce-scatter.22
  568.2 35.4 reduce-scatter.40
  659.4 33.8 reduce-scatter.42
  696.0 35.5 reduce-scatter.36
  734.5 34.8 reduce-scatter.38
  772.1 30.6 reduce-scatter.34
  805.7 32.6 reduce-scatter.32
  844.2 132.6 all-reduce.15
  979.7 34.5 reduce-scatter.26
  1017.1 67.7 reduce-scatter.24
  1087.7 88.2 reduce-scatter.28
  1178.9 88.7 reduce-scatter.30
where the time goes:
time: 1290 us; the launch traced here: 1280 us
  waiting for transfers between devices  883 us (68%)
  blocking collectives  162 us (13%)
  local copies, waits for them, and re-layouts  131 us (10%)
  matrix products  47.2 us (4%)
  other arithmetic  25.6 us (2%)
  between operations  16 us (1%)
    unnamed x24, waiting for transfers between devices  248 us
    psum x1, waiting for transfers between devices, on_device(): lax.psum((proj_grad, enc_gain_one_grad, enc_gain_two_grad, dec_gain_one_g...  138 us
    all_gather x9, blocking collectives, spread(): return lax.all_gather(values, 'mp', axis=0, tiled=True)  103 us
    reduce_scatter x1, waiting for transfers between devices, on_device(): lax.psum_scatter(enc_down_grad, ('section', 'dp'), scatter_dimension=0, t...  91.6 us
    reduce_scatter x1, waiting for transfers between devices, on_device(): lax.psum_scatter(enc_up_grad, ('section', 'dp'), scatter_dimension=0, til...  91.2 us
    unnamed x74, local copies, waits for them, and re-layouts  78.3 us
    reduce_scatter x3, waiting for transfers between devices, collect(): return lax.psum_scatter(values, 'mp', scatter_dimension=0, tiled=True)  77.3 us
    reduce_scatter x1, waiting for transfers between devices, on_device(): lax.psum_scatter(enc_qkv_grad, ('section', 'dp'), scatter_dimension=0, ti...  70.6 us
  transfers between devices with their start and end apart: 21, of which 19 were waited for; matrix products, arithmetic and copies ran while one was open for 9% of the time, Pallas kernels for 0%

commit v1 on v0

--- a/solution.py
+++ b/solution.py
@@ -1,8 +1,11 @@
+import functools
 import math
 
 import jax
 import jax.numpy as jnp
 from jax import lax
+from jax.experimental import pallas as pl
+from jax.experimental.pallas import tpu as pltpu
 from jax.sharding import PartitionSpec as P
 
 HEAD = 64
@@ -402,7 +405,7 @@
     )
 
 
-def solution(mesh):
+def placed_on(mesh, body):
     placed = (
         P("mp", "dp", None),
         P("dp"),
@@ -426,7 +429,7 @@
         P("mp", "dp", None),
     )
     return jax.shard_map(
-        on_device,
+        body,
         mesh=mesh,
         in_specs=placed,
         out_specs=(
@@ -449,3 +452,852 @@
         ),
         check_vma=False,
     )
+
+
+MESH = pl.DeviceIdType.MESH
+F32 = jnp.float32
+BF16 = jnp.bfloat16
+WAYS = 4
+PAIR = 2
+SLOTS = 64
+SHARD = 16
+PATCHES = 49
+ROWS = 64
+WIDTH = 1024
+DEC_WIDTH = 512
+HEADS_HERE = 4
+COPIES = 192
+
+
+def dot(left, right, left_dim, right_dim):
+    return lax.dot_general(
+        left, right, (((left_dim,), (right_dim,)), ((), ())), preferred_element_type=F32
+    )
+
+
+def rows_back(normal, inverse, gain, gradient):
+    weighted = gradient * gain
+    first = jnp.mean(weighted, axis=-1, keepdims=True)
+    second = jnp.mean(weighted * normal, axis=-1, keepdims=True)
+    return inverse * (weighted - first - normal * second)
+
+
+def gelu_both(upper):
+    phi = 0.5 * (1.0 + lax.erf(upper * math.sqrt(0.5)))
+    density = jnp.exp(-0.5 * upper * upper) * (1.0 / math.sqrt(2.0 * math.pi))
+    return upper * phi, phi + upper * density
+
+
+def head_mask(width, head, kind):
+    lane = lax.broadcasted_iota(jnp.int32, (1, width), 1)
+    return [
+        ((lane >= h * head) & (lane < (h + 1) * head)).astype(F32).astype(kind)
+        for h in range(HEADS_HERE)
+    ]
+
+
+def stack_heads(values, masks):
+    return jnp.concatenate([values * mask for mask in masks], axis=0)
+
+
+def fold_heads(stacked, masks, rows):
+    total = None
+    for h, mask in enumerate(masks):
+        part = stacked[h * rows : (h + 1) * rows] * mask
+        total = part if total is None else total + part
+    return total
+
+
+def attention(qkv, keep, rows, width, head, scale):
+    low = head_mask(width, head, BF16)
+    wide = head_mask(width, head, F32)
+    queries = stack_heads(qkv[:, :width], low)
+    scores = dot(queries, qkv[:, width : 2 * width], 1, 1) * scale
+    scores = jnp.where(keep, scores, -1e30)
+    weights = jnp.exp(scores - jnp.max(scores, axis=-1, keepdims=True))
+    probs = weights / jnp.sum(weights, axis=-1, keepdims=True)
+    mixed = dot(probs.astype(BF16), qkv[:, 2 * width :], 1, 0)
+    return probs, fold_heads(mixed, wide, rows).astype(BF16)
+
+
+def attention_back(qkv, probs, grad_context, rows, width, head, scale):
+    low = head_mask(width, head, BF16)
+    wide = head_mask(width, head, F32)
+    queries = stack_heads(qkv[:, :width], low)
+    grads = stack_heads(grad_context, low)
+    grad_probs = dot(grads, qkv[:, 2 * width :], 1, 1)
+    inner = jnp.sum(grad_probs * probs, axis=-1, keepdims=True)
+    grad_scores = (probs * (grad_probs - inner)).astype(BF16)
+    grad_queries = fold_heads(dot(grad_scores, qkv[:, width : 2 * width], 1, 0), wide, rows) * scale
+    grad_keys = dot(grad_scores, queries, 0, 0) * scale
+    grad_values = dot(probs.astype(BF16), grads, 0, 0)
+    return jnp.concatenate([grad_queries, grad_keys, grad_values], axis=1).astype(BF16)
+
+
+IN_NAMES = [
+    "xs",
+    "info",
+    "keep",
+    "gains",
+    "dgrad",
+    "w_qkv",
+    "w_out",
+    "w_up",
+    "w_down",
+    "w_proj",
+    "table",
+    "d_qkv",
+    "d_out",
+    "d_up",
+    "d_down",
+]
+OUT_NAMES = [
+    "o_dec",
+    "o_pat",
+    "o_qkv",
+    "o_out",
+    "o_up",
+    "o_down",
+    "o_dqkv",
+    "o_dout",
+    "o_dup",
+    "o_ddown",
+    "o_proj",
+    "o_vec",
+]
+LOADED = dict(
+    w_qkv=(WIDTH, 768),
+    w_out=(WIDTH, 256),
+    w_up=(WIDTH, 1024),
+    w_down=(WIDTH, 1024),
+    w_proj=(WIDTH, DEC_WIDTH),
+    table=(8, 256, DEC_WIDTH),
+    d_qkv=(DEC_WIDTH, 384),
+    d_out=(DEC_WIDTH, 128),
+    d_up=(DEC_WIDTH, 512),
+    d_down=(DEC_WIDTH, 512),
+)
+BUFFERS = dict(
+    xf=((2, 64, 1024), BF16),
+    qkv=((2, 64, 768), BF16),
+    probs=((2, 256, 64), F32),
+    s1=((2, 64, 1024), BF16),
+    r1=((3, 2, 16, 1024), BF16),
+    mid=((2, 16, 1024), F32),
+    n2=((2, 64, 1024), BF16),
+    gp=((128, 1024), F32),
+    s2=((2, 64, 1024), BF16),
+    r2=((3, 2, 16, 1024), BF16),
+    eo=((2, 16, 1024), BF16),
+    eom=((2, 64, 256), BF16),
+    sent=((2, 16, 512), BF16),
+    arr=((2, 64, 512), BF16),
+    meta=((2, 4, 8, 128), jnp.int32),
+    dgf=((2, 256, 512), BF16),
+    hot=((2, 256, 64), BF16),
+    free=((2, 256, 1), F32),
+    grid=((2, 256, 512), F32),
+    dn1=((512, 512), BF16),
+    dqkv=((512, 384), BF16),
+    dprobs=((2, 1024, 256), F32),
+    dctx=((512, 128), BF16),
+    s3=((2, 256, 512), BF16),
+    r3=((3, 2, 64, 512), BF16),
+    dmid=((2, 64, 512), F32),
+    dn2=((2, 256, 512), BF16),
+    dhid=((512, 512), BF16),
+    dgh=((512, 512), F32),
+    dgu=((512, 512), BF16),
+    s4=((2, 256, 512), BF16),
+    r4=((3, 2, 64, 512), BF16),
+    ds=((8, 256, 128), BF16),
+    dr=((8, 256, 128), BF16),
+    dgm=((2, 256, 512), BF16),
+    dgq=((512, 384), BF16),
+    s5=((2, 64, 512), BF16),
+    r5=((3, 2, 16, 512), BF16),
+    sg=((2, 16, 512), BF16),
+    sgf=((2, 64, 512), BF16),
+    wds=((256, 1536), BF16),
+    wdr=((256, 1536), BF16),
+    wdo=((256, 1536), F32),
+    wzs=((4, 64, 1536), BF16),
+    wzr=((3, 64, 1536), BF16),
+    s6=((2, 64, 1024), BF16),
+    r6=((3, 2, 16, 1024), BF16),
+    gy=((128, 1024), BF16),
+    gyo=((2, 16, 512), BF16),
+    gm=((2, 64, 1024), BF16),
+    fs=((8, 128, 128), BF16),
+    fr=((8, 128, 128), BF16),
+    hz=((4, 128, 1024), BF16),
+    cz=((4, 128, 256), BF16),
+    uz=((4, 128, 1024), BF16),
+    qz=((4, 128, 768), BF16),
+    xb=((4, 2, 4, 128, 128), BF16),
+    xz=((4, 4, 2, 128, 128), BF16),
+    wes=((128, 3072), BF16),
+    wer=((128, 3072), BF16),
+    ps=((2, 128, 512), BF16),
+    pr=((128, 512), BF16),
+    po=((128, 512), F32),
+    pzs=((4, 32, 512), BF16),
+    pzr=((3, 32, 512), BF16),
+    pz=((4, 32, 512), BF16),
+    pa=((4, 2, 128, 512), BF16),
+    vec=((8, 512), F32),
+    vr=((8, 8, 512), F32),
+    vz=((4, 8, 512), F32),
+)
+
+
+class Refs:
+    pass
+
+
+def kernel(*refs):
+    r = Refs()
+    names = IN_NAMES + OUT_NAMES + list(BUFFERS) + ["v_" + n for n in LOADED]
+    for name, ref in zip(names, refs):
+        setattr(r, name, ref)
+    load_sem, send_sem, recv_sem = refs[len(names) :]
+    s, d, m = (lax.axis_index(a) for a in ("section", "dp", "mp"))
+    used = [0]
+    started = []
+
+    def take(count):
+        used[0] += count
+        return used[0] - count
+
+    def copy(src, dst, device, at, land=None):
+        return pltpu.make_async_remote_copy(
+            src_ref=src,
+            dst_ref=dst,
+            send_sem=send_sem.at[at],
+            recv_sem=recv_sem.at[at if land is None else land],
+            device_id=device,
+            device_id_type=MESH,
+        )
+
+    def send(src, dst, device):
+        made = copy(src, dst, device, take(1))
+        made.start()
+        started.append(made)
+        return made
+
+    def arrive(copies):
+        for made in copies:
+            made.wait_recv()
+
+    def model(k):
+        return lax.rem(m + k, WAYS)
+
+    def data(k):
+        return lax.rem(d + k, WAYS)
+
+    def gather(ref, rows):
+        own = ref.at[:, pl.ds(pl.multiple_of(m * rows, rows), rows)]
+        return [send(own, own, {"mp": model(k)}) for k in (1, 2, 3)]
+
+    def scatter(src, dst, rows):
+        copies = []
+        for k in (1, 2, 3):
+            to = model(k)
+            part = src.at[:, pl.ds(pl.multiple_of(to * rows, rows), rows)]
+            copies.append(send(part, dst.at[k - 1], {"mp": to}))
+        return copies
+
+    def summed(src, dst, rows):
+        total = src[:, pl.ds(pl.multiple_of(m * rows, rows), rows), :].astype(F32)
+        for k in range(3):
+            total = total + dst[k].astype(F32)
+        return total
+
+    def along(ref):
+        return [send(ref.at[d], ref.at[d], {"dp": data(k)}) for k in (1, 2, 3)]
+
+    def cuts(which, values):
+        for block in range(8):
+            r.xb[which, block // 4, block % 4] = values[:, block * 128 : (block + 1) * 128]
+        r.xz[which, d] = r.xb[which, :, d]
+        return [
+            send(r.xb.at[which, :, data(k)], r.xz.at[which, d], {"dp": data(k)}) for k in (1, 2, 3)
+        ]
+
+    plane = [(a, k) for a in (0, 1) for k in range(4) if (a, k) != (0, 0)]
+
+    def to_plane(a, k):
+        return {"section": lax.rem(s + a, 2), "mp": model(k)}
+
+    half = d // 2
+    place = lax.rem(d, 2)
+
+    def across(i, k):
+        return {"section": half, "dp": 2 * s + i, "mp": model(k)}
+
+    def mine(i):
+        return (half == s) & (2 * s + i == d)
+
+    def exchange(src_of, dst_of, own):
+        at = take(8)
+        for i in range(PAIR):
+            for k in range(4):
+                made = copy(
+                    src_of(i), dst_of(place, m), across(i, k), at + 4 * i + k, at + 4 * place + k
+                )
+                if k:
+                    made.start()
+                else:
+                    pl.when(jnp.logical_not(mine(i)))(made.start)
+                    pl.when(mine(i))(functools.partial(own, i))
+
+        def landed():
+            for i in range(PAIR):
+                for k in range(4):
+                    made = copy(src_of(i), dst_of(i, model(4 - k)), across(i, k), at + 4 * i + k)
+                    if k:
+                        made.wait_recv()
+                    else:
+                        pl.when(jnp.logical_not(mine(i)))(made.wait_recv)
+
+        def left():
+            for i in range(PAIR):
+                for k in range(4):
+                    made = copy(src_of(i), dst_of(place, m), across(i, k), at + 4 * i + k)
+                    if k:
+                        made.wait_send()
+                    else:
+                        pl.when(jnp.logical_not(mine(i)))(made.wait_send)
+
+        return landed, left
+
+    loads = {}
+    for at, name in enumerate(LOADED):
+        loads[name] = pltpu.make_async_copy(
+            getattr(r, name), getattr(r, "v_" + name), load_sem.at[at]
+        )
+        loads[name].start()
+
+    barrier = pltpu.get_barrier_semaphore()
+    for a, k in plane:
+        pl.semaphore_signal(barrier, inc=1, device_id=to_plane(a, k), device_id_type=MESH)
+    for k in (1, 2, 3):
+        pl.semaphore_signal(barrier, inc=1, device_id={"dp": data(k)}, device_id_type=MESH)
+    for i in range(PAIR):
+        for k in range(4):
+            signal = functools.partial(
+                pl.semaphore_signal, barrier, inc=1, device_id=across(i, k), device_id_type=MESH
+            )
+            if k:
+                signal()
+            else:
+                pl.when(jnp.logical_not(mine(i)))(signal)
+    pl.semaphore_wait(barrier, 7 + 3 + 8 - (half == s).astype(jnp.int32))
+
+    gain = [r.gains[i : i + 1, :] for i in range(5)]
+    e_g1, e_g2 = gain[0], gain[1]
+    d_g1, d_g2, token = (g[:, :DEC_WIDTH] for g in gain[2:5])
+
+    own16 = pl.ds(pl.multiple_of(m * SHARD, SHARD), SHARD)
+    own64 = pl.ds(pl.multiple_of(m * ROWS, ROWS), ROWS)
+    r.xf[:, own16, :] = r.xs[...]
+    got = gather(r.xf, SHARD)
+
+    def own_info(i):
+        r.meta[place, m] = r.info[i]
+
+    info_landed, info_left = exchange(
+        lambda i: r.info.at[i], lambda i, at: r.meta.at[i, at], own_info
+    )
+    r.dgf[:, own64, :] = r.dgrad[...]
+    got_dg = gather(r.dgf, ROWS)
+    arrive(got)
+    normal, _ = norm_rows(r.xf[...].reshape(128, WIDTH).astype(F32))
+    normed = (normal * e_g1).astype(BF16)
+    loads["w_qkv"].wait()
+    qkv = dot(normed, r.v_w_qkv[...], 1, 0).astype(BF16)
+    contexts = []
+    for i in range(PAIR):
+        part = qkv[i * 64 : (i + 1) * 64]
+        r.qkv[i] = part
+        keep = r.keep[i, 0:1, 0:64] > 0.0
+        probs, context = attention(part, keep, 64, 256, HEAD, 1.0 / math.sqrt(HEAD))
+        r.probs[i] = probs
+        contexts.append(context)
+    context = jnp.concatenate(contexts, axis=0)
+    loads["w_out"].wait()
+    r.s1[...] = dot(context, r.v_w_out[...], 1, 1).astype(BF16).reshape(2, 64, WIDTH)
+    got = scatter(r.s1, r.r1, SHARD)
+    r.cz[d] = context
+    got_c = along(r.cz)
+    got_x1 = cuts(0, normed)
+
+    info_landed()
+    loads["table"].wait()
+    row = lax.broadcasted_iota(jnp.int32, (256, 1), 0)
+    real = (lax.rem(row, ROWS) < PATCHES).astype(F32)
+    for i in range(PAIR):
+        facts = r.meta[i, 0] + r.meta[i, 1] + r.meta[i, 2] + r.meta[i, 3]
+        index = facts[0:1, 0:64]
+        hot = (lax.broadcasted_iota(jnp.int32, (256, 64), 0) == index).astype(F32)
+        free = real - jnp.sum(hot, axis=1, keepdims=True)
+        r.hot[i] = hot.astype(BF16)
+        r.free[i] = free
+        r.grid[i] = free * token
+        level = facts[1:2, 0:1]
+
+        def add_level(l, carry):
+            chosen = (level == l).astype(F32)
+            r.grid[i] += chosen * r.v_table[l].astype(F32)
+            return carry
+
+        lax.fori_loop(0, 8, add_level, 0)
+
+    arrive(got)
+    middle = r.xs[...].astype(F32) + summed(r.s1, r.r1, SHARD)
+    r.mid[...] = middle
+    normal, _ = norm_rows(middle)
+    r.n2[:, own16, :] = (normal * e_g2).astype(BF16)
+    got = gather(r.n2, SHARD)
+    arrive(got_dg)
+    loads["d_down"].wait()
+    r.dgh[...] = dot(r.dgf[...].reshape(512, 512), r.v_d_down[...], 1, 0)
+    loads["w_up"].wait()
+    loads["w_down"].wait()
+    arrive(got)
+    normed = r.n2[...].reshape(128, WIDTH)
+    hidden, slope = gelu_both(dot(normed, r.v_w_up[...], 1, 0))
+    r.gp[...] = slope
+    hidden = hidden.astype(BF16)
+    r.s2[...] = dot(hidden, r.v_w_down[...], 1, 1).astype(BF16).reshape(2, 64, WIDTH)
+    got = scatter(r.s2, r.r2, SHARD)
+    r.hz[d] = hidden
+    got_h = along(r.hz)
+    got_x2 = cuts(1, normed)
+    loads["w_proj"].wait()
+    arrive(got)
+    out_low = (r.mid[...] + summed(r.s2, r.r2, SHARD)).astype(BF16)
+    r.eo[...] = out_low
+    r.sent[...] = (
+        dot(out_low.reshape(32, WIDTH), r.v_w_proj[...], 1, 0).astype(BF16).reshape(2, 16, 512)
+    )
+
+    def own_sent(i):
+        r.arr[place, own16, :] = r.sent[i]
+
+    def slot_rows(ref):
+        return lambda i, at: ref.at[i, pl.ds(pl.multiple_of(at * SHARD, SHARD), SHARD)]
+
+    sent_landed, sent_left = exchange(lambda i: r.sent.at[i], slot_rows(r.arr), own_sent)
+    r.eom[:, own16, :] = r.eo[:, :, pl.ds(pl.multiple_of(m * 256, 256), 256)]
+    got_eo = []
+    for k in (1, 2, 3):
+        columns = pl.ds(pl.multiple_of(model(k) * 256, 256), 256)
+        got_eo.append(send(r.eo.at[:, :, columns], r.eom.at[:, own16], {"mp": model(k)}))
+
+    loads["d_qkv"].wait()
+    loads["d_out"].wait()
+    sent_landed()
+    cols = lax.broadcasted_iota(jnp.int32, (1, 256), 1)
+    d_keep = lax.rem(cols, ROWS) < PATCHES
+    d_scale = 1.0 / math.sqrt(DEC_HEAD)
+    for i in range(PAIR):
+        values = r.grid[i] + dot(r.hot[i], r.arr[i], 1, 0)
+        r.grid[i] = values
+        normal, _ = norm_rows(values)
+        normed = (normal * d_g1).astype(BF16)
+        at = slice(i * 256, (i + 1) * 256)
+        r.dn1[at, :] = normed
+        part = dot(normed, r.v_d_qkv[...], 1, 0).astype(BF16)
+        r.dqkv[at, :] = part
+        probs, context = attention(part, d_keep, 256, 128, DEC_HEAD, d_scale)
+        r.dprobs[i] = probs
+        r.dctx[at, :] = context
+        r.s3[i] = dot(context, r.v_d_out[...], 1, 1).astype(BF16)
+    got = scatter(r.s3, r.r3, ROWS)
+    loads["d_up"].wait()
+    arrive(got)
+    middle = r.grid[:, own64, :] + summed(r.s3, r.r3, ROWS)
+    r.dmid[...] = middle
+    normal, _ = norm_rows(middle)
+    r.dn2[:, own64, :] = (normal * d_g2).astype(BF16)
+    got = gather(r.dn2, ROWS)
+    arrive(got)
+    hidden, slope = gelu_both(dot(r.dn2[...].reshape(512, 512), r.v_d_up[...], 1, 0))
+    grad_upper = (r.dgh[...] * slope).astype(BF16)
+    r.dhid[...] = hidden.astype(BF16)
+    r.dgu[...] = grad_upper
+
+    r.s4[...] = dot(grad_upper, r.v_d_up[...], 1, 1).astype(BF16).reshape(2, 256, 512)
+    got = scatter(r.s4, r.r4, ROWS)
+    r.grid_out = dot(r.dhid[...], r.v_d_down[...], 1, 1).reshape(2, 256, 512)
+    shard = lax.broadcasted_iota(jnp.int32, (256, 1), 0) // ROWS
+    here = (shard == m).astype(F32)
+    parts = []
+    for i in range(PAIR):
+        whole = jnp.concatenate([r.dmid[i]] * 4, axis=0)
+        parts.append((r.grid_out[i] + whole * here).astype(F32))
+    for block in range(8):
+        at = slice(block * 64, (block + 1) * 64)
+        r.ds[block] = jnp.concatenate([parts[0][:, at], parts[1][:, at]], axis=1).astype(BF16)
+    rank = s * 4 + m
+    got_dec = []
+    for a, k in plane:
+        to = lax.rem(s + a, 2) * 4 + model(k)
+        got_dec.append(send(r.ds.at[to], r.dr.at[rank], to_plane(a, k)))
+    r.dr[rank] = r.ds[rank]
+
+    def dec_weights(left, right, first, size):
+        for a in (0, 1):
+            rows = pl.ds(pl.multiple_of(lax.rem(s + a, 2) * 256, 256), 256)
+            value = dot(left[:, rows], right[...], 0, 0)
+            if a == 0:
+                r.wdo[:, first : first + size] = value
+            else:
+                r.wds[:, first : first + size] = value.astype(BF16)
+
+    flat = lambda ref, rows, width: ref.reshape(rows, width)
+    dec_weights(flat(r.dn2, 512, 512), r.dgu, 512, 512)
+    arrive(got)
+    total = summed(r.s4, r.r4, ROWS)
+    normal, inverse = norm_rows(r.dmid[...])
+    grad = r.dgrad[...].astype(F32) + rows_back(normal, inverse, d_g2, total)
+    r.vec[...] = jnp.zeros((8, 512), F32)
+    r.vec[5:6, :] = jnp.sum((total * normal).reshape(128, 512), axis=0, keepdims=True)
+    r.dgm[:, own64, :] = grad.astype(BF16)
+    got = gather(r.dgm, ROWS)
+    dec_weights(flat(r.dgf, 512, 512), r.dhid, 1024, 512)
+    arrive(got)
+    gain_sum = jnp.zeros((1, 512), F32)
+    token_sum = jnp.zeros((1, 512), F32)
+    for i in range(PAIR):
+        at = slice(i * 256, (i + 1) * 256)
+        grad_low = r.dgm[i]
+        grad_context = dot(grad_low, r.v_d_out[...], 1, 0).astype(BF16)
+        part = attention_back(
+            r.dqkv[at, :], r.dprobs[i], grad_context, 256, 128, DEC_HEAD, d_scale
+        )
+        r.dgq[at, :] = part
+        terms = dot(part, r.v_d_qkv[...], 1, 1)
+        normal, inverse = norm_rows(r.grid[i])
+        gain_sum += jnp.sum(terms * normal, axis=0, keepdims=True)
+        back = rows_back(normal, inverse, d_g1, terms) + 0.25 * grad_low.astype(F32)
+        token_sum += jnp.sum(back * r.free[i], axis=0, keepdims=True)
+        r.s5[i] = dot(r.hot[i], back.astype(BF16), 0, 0).astype(BF16)
+    got = scatter(r.s5, r.r5, SHARD)
+    r.vec[4:5, :] = gain_sum
+    r.vec[6:7, :] = token_sum
+    dec_weights(flat(r.dgm, 512, 512), r.dctx, 384, 128)
+    dec_weights(r.dn1, r.dgq, 0, 384)
+    got_wd = [send(r.wds, r.wdr, to_plane(1, 0))]
+    arrive(got)
+    r.sg[...] = summed(r.s5, r.r5, SHARD).astype(BF16)
+
+    def own_back(i):
+        r.sgf[place, own16, :] = r.sg[i]
+
+    back_landed, back_left = exchange(lambda i: r.sg.at[i], slot_rows(r.sgf), own_back)
+    arrive(got_dec)
+    for a in (0, 1):
+        total = r.dr[4 * a].astype(F32)
+        for k in (1, 2, 3):
+            total = total + r.dr[4 * a + k].astype(F32)
+        r.o_dec[a] = total
+    arrive(got_wd)
+    for block in range(4):
+        at = slice(block * 64, (block + 1) * 64)
+        r.wdo[at, :] = r.wdo[at, :] + r.wdr[at, :].astype(F32)
+        r.wzs[block] = r.wdo[at, :].astype(BF16)
+    got_wz = [
+        send(r.wzs.at[data(k)], r.wzr.at[k - 1], {"dp": data(k)}) for k in (1, 2, 3)
+    ]
+
+    back_landed()
+    grad_sent = r.sgf[...].reshape(128, 512)
+    grad_low = dot(grad_sent, r.v_w_proj[...], 1, 1).astype(BF16)
+    r.gy[...] = grad_low
+    grad_upper = (dot(grad_low, r.v_w_down[...], 1, 0) * r.gp[...]).astype(BF16)
+    r.s6[...] = dot(grad_upper, r.v_w_up[...], 1, 1).astype(BF16).reshape(2, 64, WIDTH)
+    got = scatter(r.s6, r.r6, SHARD)
+    r.uz[d] = grad_upper
+    got_u = along(r.uz)
+    got_x3 = cuts(2, grad_low)
+    arrive(got_eo)
+    product = dot(r.eom[...].reshape(128, 256), grad_sent, 0, 0)
+    for a in (0, 1):
+        r.ps[a] = product[a * 128 : (a + 1) * 128].astype(BF16)
+    other = lax.rem(s + 1, 2)
+    got_p = [send(r.ps.at[other], r.pr, to_plane(1, 0))]
+    arrive(got)
+    total = summed(r.s6, r.r6, SHARD)
+    normal, inverse = norm_rows(r.mid[...])
+    own_sent_grad = r.sgf[:, own16, :].reshape(32, 512)
+    own_grad = dot(own_sent_grad, r.v_w_proj[...], 1, 1).reshape(2, 16, WIDTH)
+    grad = own_grad + rows_back(normal, inverse, e_g2, total)
+    r.gm[:, own16, :] = grad.astype(BF16)
+    got = gather(r.gm, SHARD)
+    gain_two = jnp.sum((total * normal).reshape(32, WIDTH), axis=0, keepdims=True)
+    r.vec[2:3, :] = gain_two[:, :512]
+    r.vec[3:4, :] = gain_two[:, 512:]
+
+    arrive(got_p)
+    kept = r.ps[s].astype(F32) + r.pr[...].astype(F32)
+    r.po[...] = kept
+    for block in range(4):
+        r.pzs[block] = kept[block * 32 : (block + 1) * 32].astype(BF16)
+    got_pz = [send(r.pzs.at[data(k)], r.pzr.at[k - 1], {"dp": data(k)}) for k in (1, 2, 3)]
+
+    arrive(got)
+    grad_low = r.gm[...].reshape(128, WIDTH)
+    grad_context = dot(grad_low, r.v_w_out[...], 1, 0).astype(BF16)
+    parts = []
+    for i in range(PAIR):
+        parts.append(
+            attention_back(
+                r.qkv[i],
+                r.probs[i],
+                grad_context[i * 64 : (i + 1) * 64],
+                64,
+                256,
+                HEAD,
+                1.0 / math.sqrt(HEAD),
+            )
+        )
+    part = jnp.concatenate(parts, axis=0)
+    r.qz[d] = part
+    got_q = along(r.qz)
+    got_x4 = cuts(3, grad_low)
+    terms = dot(part, r.v_w_qkv[...], 1, 1)
+    normal, inverse = norm_rows(r.xf[...].reshape(128, WIDTH).astype(F32))
+    gain_one = jnp.sum(terms * normal, axis=0, keepdims=True)
+    r.vec[0:1, :] = gain_one[:, :512]
+    r.vec[1:2, :] = gain_one[:, 512:]
+    back = rows_back(normal, inverse, e_g1, terms) + 0.25 * grad_low.astype(F32)
+    for block in range(8):
+        r.fs[block] = back[:, block * 128 : (block + 1) * 128].astype(BF16)
+    got_f = []
+    for a, k in plane:
+        to = lax.rem(s + a, 2) * 4 + model(k)
+        got_f.append(send(r.fs.at[to], r.fr.at[rank], to_plane(a, k)))
+    r.fr[rank] = r.fs[rank]
+    r.vr[rank] = r.vec[...]
+    got_v = [send(r.vec, r.vr.at[rank], to_plane(a, k)) for a, k in plane]
+
+    arrive(got_pz)
+    mine32 = pl.ds(pl.multiple_of(d * 32, 32), 32)
+    total = r.po[mine32, :]
+    for k in range(3):
+        total = total + r.pzr[k].astype(F32)
+    r.pz[d] = total.astype(BF16)
+    got_pg = along(r.pz)
+
+    def enc_weights(which, right, first, size, out):
+        lefts = [
+            r.xz[which, :, lax.rem(s + a, 2), :, :].reshape(512, 128) for a in (0, 1)
+        ]
+        value = right[...].reshape(512, size)
+        r.wes[:, first : first + size] = dot(lefts[1], value, 0, 0).astype(BF16)
+        made = send(
+            r.wes.at[:, first : first + size], r.wer.at[:, first : first + size], to_plane(1, 0)
+        )
+        out[...] = dot(lefts[0], value, 0, 0)
+        return made
+
+    arrive(got_h)
+    arrive(got_x3)
+    got_w = [enc_weights(2, r.hz, 2048, 1024, r.o_down)]
+    arrive(got_x2)
+    arrive(got_u)
+    got_w.append(enc_weights(1, r.uz, 1024, 1024, r.o_up))
+    arrive(got_wz)
+    total = r.wdo[pl.ds(pl.multiple_of(d * 64, 64), 64), :]
+    for k in range(3):
+        total = total + r.wzr[k].astype(F32)
+    r.o_dqkv[...] = total[:, :384]
+    r.o_dout[...] = total[:, 384:512]
+    r.o_dup[...] = total[:, 512:1024]
+    r.o_ddown[...] = total[:, 1024:]
+    arrive(got_v)
+    total = r.vr[0]
+    for k in range(1, 8):
+        total = total + r.vr[k]
+    r.vz[d] = total
+    got_vz = along(r.vz)
+    arrive(got_pg)
+    r.pa[m, s] = r.pz[...].reshape(128, 512)
+    got_pa = [send(r.pa.at[m, s], r.pa.at[m, s], {"mp": model(k)}) for k in (1, 2, 3)]
+    arrive(got_f)
+    for a in (0, 1):
+        total = r.fr[4 * a].astype(F32)
+        for k in (1, 2, 3):
+            total = total + r.fr[4 * a + k].astype(F32)
+        r.o_pat[a] = total
+    arrive(got_pa)
+    got_ps = [send(r.pa.at[:, s], r.pa.at[:, s], to_plane(1, 0))]
+    arrive(got_c)
+    arrive(got_x4)
+    got_w.append(enc_weights(3, r.cz, 768, 256, r.o_out))
+    arrive(got_x1)
+    arrive(got_q)
+    got_w.append(enc_weights(0, r.qz, 0, 768, r.o_qkv))
+    arrive(got_vz)
+    r.o_vec[...] = r.vz[0] + r.vz[1] + r.vz[2] + r.vz[3]
+    arrive(got_ps)
+    for a in range(4):
+        for b in range(2):
+            at = a * 256 + b * 128
+            r.o_proj[at : at + 128, :] = r.pa[a, b].astype(F32)
+    firsts = [(2048, 1024, r.o_down), (1024, 1024, r.o_up), (768, 256, r.o_out), (0, 768, r.o_qkv)]
+    for made, (first, size, out) in zip(got_w, firsts):
+        made.wait_recv()
+        out[...] += r.wer[:, first : first + size].astype(F32)
+    for made in started:
+        made.wait_send()
+    for leave in (info_left, sent_left, back_left):
+        leave()
+    assert used[0] <= COPIES
+
+
+def with_kernel(
+    patches,
+    counts,
+    patch_index,
+    scale_level,
+    enc_gain_one,
+    enc_qkv,
+    enc_out,
+    enc_gain_two,
+    enc_up,
+    enc_down,
+    w_proj,
+    mask_token,
+    pos_table,
+    dec_gain_one,
+    dec_qkv,
+    dec_out,
+    dec_gain_two,
+    dec_up,
+    dec_down,
+    decoded_grad,
+):
+    s, m = lax.axis_index("section"), lax.axis_index("mp")
+
+    def own_pair(values, axis):
+        return lax.dynamic_slice_in_dim(values, PAIR * s, PAIR, axis)
+
+    rows = jnp.swapaxes(own_pair(patches, 1), 0, 1)
+    grads = jnp.swapaxes(own_pair(decoded_grad, 1), 0, 1)
+    grads = jnp.pad(grads, ((0, 0), (0, ROWS - PATCHES), (0, 0)))
+    seen = own_pair(counts, 0)
+    keep = (jnp.arange(128, dtype=jnp.int32)[None, :] < seen[:, None]).astype(F32)
+    keep = jnp.broadcast_to(keep[:, None, :], (PAIR, 8, 128))
+    index = jnp.swapaxes(own_pair(patch_index, 1), 0, 1)
+    grid_row = (index // PATCHES) * ROWS + index % PATCHES
+    slot = m * SHARD + jnp.arange(SHARD, dtype=jnp.int32)
+    grid_row = jnp.where(slot[None, :] < seen[:, None], grid_row, -1)
+    lanes = jnp.zeros((PAIR, 128), jnp.int32)
+    lanes = lax.dynamic_update_slice(lanes, grid_row, (0, m * SHARD))
+    level = jnp.where(m == 0, own_pair(scale_level, 0), 0)
+    info = jnp.concatenate(
+        [
+            lanes[:, None, :],
+            jnp.broadcast_to(level[:, None, None], (PAIR, 1, 128)),
+            jnp.zeros((PAIR, 6, 128), jnp.int32),
+        ],
+        axis=1,
+    )
+    wide = lambda v: jnp.pad(v.astype(F32), (0, WIDTH - v.shape[0]))[None, :]
+    gains = jnp.concatenate(
+        [wide(v) for v in (enc_gain_one, enc_gain_two, dec_gain_one, dec_gain_two, mask_token)]
+        + [jnp.zeros((3, WIDTH), F32)],
+        axis=0,
+    )
+    table = pos_table.reshape(8, WAYS, PATCHES, DEC_WIDTH)
+    table = jnp.pad(table, ((0, 0), (0, 0), (0, ROWS - PATCHES), (0, 0))).reshape(8, 256, DEC_WIDTH)
+    inputs = (
+        rows,
+        info,
+        keep,
+        gains,
+        grads,
+        enc_qkv.reshape(WIDTH, 768),
+        enc_out,
+        enc_up,
+        enc_down,
+        w_proj,
+        table,
+        dec_qkv.reshape(DEC_WIDTH, 384),
+        dec_out,
+        dec_up,
+        dec_down,
+    )
+    shapes = (
+        (2, 256, 128),
+        (2, 128, 128),
+        (128, 768),
+        (128, 256),
+        (128, 1024),
+        (128, 1024),
+        (64, 384),
+        (64, 128),
+        (64, 512),
+        (64, 512),
+        (1024, 512),
+        (8, 512),
+    )
+    vmem = pl.BlockSpec(memory_space=pltpu.VMEM)
+    outs = pl.pallas_call(
+        kernel,
+        out_shape=[jax.ShapeDtypeStruct(shape, F32) for shape in shapes],
+        in_specs=[vmem] * 5 + [pl.BlockSpec(memory_space=pl.ANY)] * 10,
+        out_specs=[vmem] * len(shapes),
+        scratch_shapes=[pltpu.VMEM(shape, kind) for shape, kind in BUFFERS.values()]
+        + [pltpu.VMEM(shape, BF16) for shape in LOADED.values()]
+        + [
+            pltpu.SemaphoreType.DMA((len(LOADED),)),
+            pltpu.SemaphoreType.DMA((COPIES,)),
+            pltpu.SemaphoreType.DMA((COPIES,)),
+        ],
+        compiler_params=pltpu.CompilerParams(
+            collective_id=0, has_side_effects=True, vmem_limit_bytes=60 * 2**20
+        ),
+        name="layer_pair",
+    )(*inputs)
+    dec, pat, qkv, out, up, down, dqkv, dout, dup, ddown, proj, vec = outs
+    dec = dec.reshape(2, WAYS, ROWS, PAIR, 64)[:, :, :PATCHES]
+    dec = jnp.transpose(dec, (1, 2, 0, 3, 4)).reshape(WAYS * PATCHES, 4, 64)
+    pat = jnp.transpose(pat.reshape(2, PAIR, SLOTS, 128), (2, 0, 1, 3)).reshape(SLOTS, 4, 128)
+    return (
+        dec,
+        pat,
+        qkv.reshape(128, 3, 256),
+        out,
+        up,
+        down,
+        dqkv.reshape(64, 3, 128),
+        dout,
+        dup,
+        ddown,
+        proj,
+        vec[0:2].reshape(WIDTH),
+        vec[2:4].reshape(WIDTH),
+        vec[4],
+        vec[5],
+        vec[6],
+    )
+
+
+def fits_kernel(mesh, shapes):
+    ways = (mesh.shape["section"], mesh.shape["dp"], mesh.shape["mp"])
+    wanted = {0: (64, 16, 1024), 5: (1024, 3, 1024), 8: (1024, 4096), 10: (1024, 512)}
+    wanted.update({12: (8, 196, 512), 14: (512, 3, 512), 17: (512, 2048), 19: (196, 16, 512)})
+    return ways == (2, 4, 4) and all(shapes[i] == shape for i, shape in wanted.items())
+
+
+def solution(mesh):
+    def program(*arrays):
+        shapes = [array.shape for array in arrays]
+        body = with_kernel if fits_kernel(mesh, shapes) else on_device
+        return placed_on(mesh, body)(*arrays)
+
+    return program

time: 1290 us -> 226 us (0.18)
  waiting for transfers between devices: 883 us -> 0 us
  Pallas kernels: 0 us -> 187 us
  blocking collectives: 162 us -> 0 us
  local copies, waits for them, and re-layouts: 131 us -> 30.2 us
  matrix products: 47.2 us -> 0 us
  other arithmetic: 25.6 us -> 5.77 us
  between operations: 16 us -> 0.81 us
    reduce_scatter x11 -> x0, waiting for transfers between devices: 478 us -> none  [the longest x1 91.6 us: on_device(): lax.psum_scatter(enc_down_grad, ('section', 'dp'), scatter_dimension=0, t...]
    unnamed x24 -> x0, waiting for transfers between devices: 248 us -> none
    pallas_call x0 -> x1, Pallas kernels: none -> 187 us  [with_kernel(): pl.pallas_call(kernel, out_shape=[jax.ShapeDtypeStruct(shape, F32) for sh...]
    psum x1 -> x0, waiting for transfers between devices: 138 us -> none  [on_device(): lax.psum((proj_grad, enc_gain_one_grad, enc_gain_two_grad, dec_gain_one_g...]
    all_gather x9 -> x0, blocking collectives: 103 us -> none  [spread(): return lax.all_gather(values, 'mp', axis=0, tiled=True)]
    unnamed x74 -> x33, local copies, waits for them, and re-layouts: 78.3 us -> 14.9 us
    dot_general x23 -> x0, matrix products: 47.2 us -> none  [the longest x1 6.05 us: feed_back_local(): jnp.einsum('sbw,sbf->wf', grad_full, hidden, preferred_element_type=jnp.f...]
    psum x1 -> x0, blocking collectives: 40.2 us -> none  [on_device(): lax.psum((proj_grad, enc_gain_one_grad, enc_gain_two_grad, dec_gain_one_g...]
  transfers between devices with their start and end apart: 21 -> 0, of which waited for: 19 -> 0; matrix products, arithmetic and copies ran while one was open for 9% -> 0% of each run, Pallas kernels for 0% -> 0%
where the time goes in v1:
time: 226 us; the launch traced here: 224 us
  Pallas kernels  187 us (83%)
  local copies, waits for them, and re-layouts  30.2 us (13%)
  other arithmetic  5.77 us (3%)
    pallas_call x1, Pallas kernels, with_kernel(): pl.pallas_call(kernel, out_shape=[jax.ShapeDtypeStruct(shape, F32) for sh...  187 us
    unnamed x33, local copies, waits for them, and re-layouts  14.9 us

profile of v1, /device:TPU:0, one launch (start us, length us, event | category | flops | bytes accessed | tf_op | source)
XLA Modules:
  0.0 224.1 jit_solution(15074611507263785380)
XLA Ops:
  0.7 0.9 broadcast_select_fusion
  1.6 0.7 dynamic_slice.16
  2.3 0.8 compare_select_fusion
  3.4 0.7 broadcast_in_dim.81
  4.0 0.7 broadcast_in_dim.82
  4.7 0.7 pad_convert_fusion
  5.4 0.7 pad_convert_fusion.2
  6.1 0.7 pad_convert_fusion.1
  6.8 0.7 add_add_fusion.refs_1_
  8.0 0.7 concatenate.7.refs_3_
  8.7 1.0 constant_dynamic-slice_fusion.1
  10.5 0.7 pad.24.refs_4_
  11.1 1.2 copy.51
  12.3 0.9 copy.53.refs_11_
  13.2 0.9 copy.49
  14.1 1.6 copy.52.refs_5_
  16.3 1.6 pad.25
  17.9 187.4 %layer_pair.1 = (f32[2,256,128]{2,1,0:T(8,128)}, f32[2,128,128]{2,1,0:T(8,128)}, f32[128,768]{1,0:T(8,128)}, f32[128,256]{1,0:T(8,128)}, f32[128,1024]{1,0:T(8,1...) custom-call(bf16[2,16,1024]{2,1,0:T(8,128)(2,1)} %bitcast.65, ...), custom_call_target="tpu_custom_call" | custom-call | tf_op jit(solution)/shard_map/layer_pair/pallas_call | solution.py:1249
  205.2 1.7 copy.55
  206.9 1.4 fusion.3
  208.3 0.8 slice_bitcast_fusion
  210.3 1.5 copy_bitcast_fusion.1
  211.8 1.3 reshape.98
  213.4 1.0 reshape.99
  214.4 1.3 copy.56
  215.7 0.9 copy.57
  216.6 1.6 copy.78
  218.2 1.9 copy.79
  220.1 0.8 copy.80
  221.5 0.7 copy.82
  222.2 0.7 copy.83
  222.8 1.3 copy.84
  (34 shorter events, 4.4 us)
Async XLA Ops:
  0.6 9.7 %copy-start = (bf16[49,4,512]{2,1,0:T(4,128)(2,1)S(1)}, bf16[49,4,512]{2,1,0:T(4,128)(2,1)}, u32[]{:S(2)}) copy-start(bf16[49,4,512]{2,1,0:T(4,128)(2,1)} %param.39) | copy-start | bytes 602116
  0.7 12.6 %copy-start.3 = (bf16[1024,3,256]{2,0,1:T(8,128)(2,1)S(1)}, bf16[1024,3,256]{2,0,1:T(8,128)(2,1)}, u32[]{:S(2)}) copy-start(bf16[1024,3,256]{2,0,1:T(8,128)(2,1)} %param.25) | copy-start | bytes 4718596
  14.1 1.6 copy-start.2
  213.2 6.9 %copy-start.4 = (f32[128,1024]{1,0:T(8,128)S(1)}, f32[128,1024]{1,0:T(8,128)}, u32[]{:S(2)}) copy-start(f32[128,1024]{1,0:T(8,128)} %get-tuple-element.98) | copy-start | bytes 1572868
  214.4 6.5 %copy-start.7 = (f32[64,128]{1,0:T(8,128)S(1)}, f32[64,128]{1,0:T(8,128)}, u32[]{:S(2)}) copy-start(f32[64,128]{1,0:T(8,128)} %get-tuple-element.100) | copy-start | bytes 98308
  214.4 7.1 %copy-start.6 = (f32[64,512]{1,0:T(8,128)S(1)}, f32[64,512]{1,0:T(8,128)}, u32[]{:S(2)}) copy-start(f32[64,512]{1,0:T(8,128)} %get-tuple-element.101) | copy-start | bytes 393220
  214.4 7.8 %copy-start.5 = (f32[64,512]{1,0:T(8,128)S(1)}, f32[64,512]{1,0:T(8,128)}, u32[]{:S(2)}) copy-start(f32[64,512]{1,0:T(8,128)} %get-tuple-element.102) | copy-start | bytes 393220
  214.4 8.4 %copy-start.1 = (f32[1024,512]{1,0:T(8,128)S(1)}, f32[1024,512]{1,0:T(8,128)}, u32[]{:S(2)}) copy-start(f32[1024,512]{1,0:T(8,128)} %get-tuple-element.103) | copy-start | bytes 6291460

commit v2 on v1

--- a/solution.py
+++ b/solution.py
@@ -466,7 +466,7 @@
 WIDTH = 1024
 DEC_WIDTH = 512
 HEADS_HERE = 4
-COPIES = 192
+COPIES = 256
 
 
 def dot(left, right, left_dim, right_dim):
@@ -582,14 +582,13 @@
     qkv=((2, 64, 768), BF16),
     probs=((2, 256, 64), F32),
     s1=((2, 64, 1024), BF16),
-    r1=((3, 2, 16, 1024), BF16),
+    r1=((2, 3, 16, 1024), BF16),
     mid=((2, 16, 1024), F32),
     n2=((2, 64, 1024), BF16),
-    gp=((128, 1024), F32),
+    gp=((2, 64, 1024), F32),
     s2=((2, 64, 1024), BF16),
-    r2=((3, 2, 16, 1024), BF16),
+    r2=((2, 3, 16, 1024), BF16),
     eo=((2, 16, 1024), BF16),
-    eom=((2, 64, 256), BF16),
     sent=((2, 16, 512), BF16),
     arr=((2, 64, 512), BF16),
     meta=((2, 4, 8, 128), jnp.int32),
@@ -602,48 +601,49 @@
     dprobs=((2, 1024, 256), F32),
     dctx=((512, 128), BF16),
     s3=((2, 256, 512), BF16),
-    r3=((3, 2, 64, 512), BF16),
+    r3=((2, 3, 64, 512), BF16),
     dmid=((2, 64, 512), F32),
     dn2=((2, 256, 512), BF16),
     dhid=((512, 512), BF16),
     dgh=((512, 512), F32),
     dgu=((512, 512), BF16),
     s4=((2, 256, 512), BF16),
-    r4=((3, 2, 64, 512), BF16),
+    r4=((2, 3, 64, 512), BF16),
     ds=((8, 256, 128), BF16),
     dr=((8, 256, 128), BF16),
     dgm=((2, 256, 512), BF16),
     dgq=((512, 384), BF16),
     s5=((2, 64, 512), BF16),
-    r5=((3, 2, 16, 512), BF16),
+    r5=((2, 3, 16, 512), BF16),
     sg=((2, 16, 512), BF16),
-    sgf=((2, 64, 512), BF16),
-    wds=((256, 1536), BF16),
-    wdr=((256, 1536), BF16),
-    wdo=((256, 1536), F32),
-    wzs=((4, 64, 1536), BF16),
-    wzr=((3, 64, 1536), BF16),
+    w1s=((256, 1024), BF16),
+    w1r=((256, 1024), BF16),
+    w1o=((256, 1024), F32),
+    z1s=((4, 64, 1024), BF16),
+    z1r=((3, 64, 1024), BF16),
+    w2s=((256, 512), BF16),
+    w2r=((256, 512), BF16),
+    w2o=((256, 512), F32),
+    z2s=((4, 64, 512), BF16),
+    z2r=((3, 64, 512), BF16),
     s6=((2, 64, 1024), BF16),
-    r6=((3, 2, 16, 1024), BF16),
-    gy=((128, 1024), BF16),
-    gyo=((2, 16, 512), BF16),
+    r6=((2, 3, 16, 1024), BF16),
     gm=((2, 64, 1024), BF16),
-    fs=((8, 128, 128), BF16),
-    fr=((8, 128, 128), BF16),
-    hz=((4, 128, 1024), BF16),
-    cz=((4, 128, 256), BF16),
-    uz=((4, 128, 1024), BF16),
-    qz=((4, 128, 768), BF16),
-    xb=((4, 2, 4, 128, 128), BF16),
-    xz=((4, 4, 2, 128, 128), BF16),
+    fs=((8, 2, 64, 128), BF16),
+    fr=((8, 2, 64, 128), BF16),
+    cz=((4, 2, 64, 256), BF16),
+    uz=((4, 2, 64, 1024), BF16),
+    qz=((4, 2, 64, 768), BF16),
+    ez=((4, 2, 64, 256), BF16),
+    sz=((4, 2, 4, 16, 512), BF16),
+    xb=((3, 2, 4, 2, 64, 128), BF16),
+    xz=((3, 4, 2, 2, 64, 128), BF16),
+    ha=((512, 1024), BF16),
+    ga=((512, 1024), BF16),
     wes=((128, 3072), BF16),
     wer=((128, 3072), BF16),
-    ps=((2, 128, 512), BF16),
-    pr=((128, 512), BF16),
-    po=((128, 512), F32),
-    pzs=((4, 32, 512), BF16),
-    pzr=((3, 32, 512), BF16),
-    pz=((4, 32, 512), BF16),
+    ps=((256, 512), BF16),
+    pr=((256, 512), BF16),
     pa=((4, 2, 128, 512), BF16),
     vec=((8, 512), F32),
     vr=((8, 8, 512), F32),
@@ -696,6 +696,10 @@
         return lax.rem(d + k, WAYS)
 
     def gather(ref, rows):
+        own = ref.at[pl.ds(pl.multiple_of(m * rows, rows), rows)]
+        return [send(own, own, {"mp": model(k)}) for k in (1, 2, 3)]
+
+    def gather_all(ref, rows):
         own = ref.at[:, pl.ds(pl.multiple_of(m * rows, rows), rows)]
         return [send(own, own, {"mp": model(k)}) for k in (1, 2, 3)]
 
@@ -703,12 +707,12 @@
         copies = []
         for k in (1, 2, 3):
             to = model(k)
-            part = src.at[:, pl.ds(pl.multiple_of(to * rows, rows), rows)]
+            part = src.at[pl.ds(pl.multiple_of(to * rows, rows), rows)]
             copies.append(send(part, dst.at[k - 1], {"mp": to}))
         return copies
 
     def summed(src, dst, rows):
-        total = src[:, pl.ds(pl.multiple_of(m * rows, rows), rows), :].astype(F32)
+        total = src[pl.ds(pl.multiple_of(m * rows, rows), rows), :].astype(F32)
         for k in range(3):
             total = total + dst[k].astype(F32)
         return total
@@ -717,8 +721,10 @@
         return [send(ref.at[d], ref.at[d], {"dp": data(k)}) for k in (1, 2, 3)]
 
     def cuts(which, values):
-        for block in range(8):
-            r.xb[which, block // 4, block % 4] = values[:, block * 128 : (block + 1) * 128]
+        for i, value in enumerate(values):
+            for block in range(8):
+                at = slice(block * 128, (block + 1) * 128)
+                r.xb[which, block // 4, block % 4, i] = value[:, at]
         r.xz[which, d] = r.xb[which, :, d]
         return [
             send(r.xb.at[which, :, data(k)], r.xz.at[which, d], {"dp": data(k)}) for k in (1, 2, 3)
@@ -738,38 +744,55 @@
     def mine(i):
         return (half == s) & (2 * s + i == d)
 
-    def exchange(src_of, dst_of, own):
-        at = take(8)
-        for i in range(PAIR):
-            for k in range(4):
-                made = copy(
-                    src_of(i), dst_of(place, m), across(i, k), at + 4 * i + k, at + 4 * place + k
-                )
-                if k:
-                    made.start()
-                else:
-                    pl.when(jnp.logical_not(mine(i)))(made.start)
-                    pl.when(mine(i))(functools.partial(own, i))
-
-        def landed():
+    def to_dp():
+        return sending[0] if sending else d
+
+    sending = []
+
+    class exchange:
+        def __init__(self, src_of, dst_of, own):
+            self.src_of, self.dst_of, self.own = src_of, dst_of, own
+            self.at = take(8)
+
+        def out(self, i, k):
+            sending.append(2 * s + i)
+            land = self.dst_of(place, m)
+            sending.clear()
+            at = self.at
+            return copy(self.src_of(i), land, across(i, k), at + 4 * i + k, at + 4 * place + k)
+
+        def come(self, i, k):
+            at = self.at + 4 * i + k
+            return copy(self.src_of(i), self.dst_of(i, model(4 - k)), across(i, k), at)
+
+        def start(self, i):
+            for k in (1, 2, 3):
+                self.out(i, k).start()
+            pl.when(jnp.logical_not(mine(i)))(self.out(i, 0).start)
+            pl.when(mine(i))(functools.partial(self.own, i))
+
+        def landed(self, i):
+            pl.when(jnp.logical_not(mine(i)))(self.come(i, 0).wait_recv)
+            for k in (1, 2, 3):
+                self.come(i, k).wait_recv()
+
+        def left(self):
             for i in range(PAIR):
-                for k in range(4):
-                    made = copy(src_of(i), dst_of(i, model(4 - k)), across(i, k), at + 4 * i + k)
-                    if k:
-                        made.wait_recv()
-                    else:
-                        pl.when(jnp.logical_not(mine(i)))(made.wait_recv)
-
-        def left():
-            for i in range(PAIR):
-                for k in range(4):
-                    made = copy(src_of(i), dst_of(place, m), across(i, k), at + 4 * i + k)
-                    if k:
-                        made.wait_send()
-                    else:
-                        pl.when(jnp.logical_not(mine(i)))(made.wait_send)
-
-        return landed, left
+                for k in (1, 2, 3):
+                    self.out(i, k).wait_send()
+                pl.when(jnp.logical_not(mine(i)))(self.out(i, 0).wait_send)
+
+    def slot_rows(ref):
+        return lambda i, at: ref.at[i, pl.ds(pl.multiple_of(at * SHARD, SHARD), SHARD)]
+
+    def put_info(i):
+        r.meta[place, m] = r.info[i]
+
+    def put_rows(ref):
+        def put(i):
+            ref[place, pl.ds(pl.multiple_of(m * SHARD, SHARD), SHARD), :] = r.sent[i]
+
+        return put
 
     loads = {}
     for at, name in enumerate(LOADED):
@@ -800,43 +823,44 @@
 
     own16 = pl.ds(pl.multiple_of(m * SHARD, SHARD), SHARD)
     own64 = pl.ds(pl.multiple_of(m * ROWS, ROWS), ROWS)
+    e_scale = 1.0 / math.sqrt(HEAD)
+    d_scale = 1.0 / math.sqrt(DEC_HEAD)
+    other = lax.rem(s + 1, 2)
+    rank = s * 4 + m
+    pair = range(PAIR)
+
     r.xf[:, own16, :] = r.xs[...]
-    got = gather(r.xf, SHARD)
-
-    def own_info(i):
-        r.meta[place, m] = r.info[i]
-
-    info_landed, info_left = exchange(
-        lambda i: r.info.at[i], lambda i, at: r.meta.at[i, at], own_info
-    )
+    got = [gather(r.xf.at[i], SHARD) for i in pair]
+    info = exchange(lambda i: r.info.at[i], lambda i, at: r.meta.at[i, at], put_info)
+    for i in pair:
+        info.start(i)
     r.dgf[:, own64, :] = r.dgrad[...]
-    got_dg = gather(r.dgf, ROWS)
-    arrive(got)
-    normal, _ = norm_rows(r.xf[...].reshape(128, WIDTH).astype(F32))
-    normed = (normal * e_g1).astype(BF16)
     loads["w_qkv"].wait()
-    qkv = dot(normed, r.v_w_qkv[...], 1, 0).astype(BF16)
-    contexts = []
-    for i in range(PAIR):
-        part = qkv[i * 64 : (i + 1) * 64]
+    loads["w_out"].wait()
+    sent_on = []
+    contexts, normeds = [], []
+    for i in pair:
+        arrive(got[i])
+        normal, _ = norm_rows(r.xf[i].astype(F32))
+        normed = (normal * e_g1).astype(BF16)
+        part = dot(normed, r.v_w_qkv[...], 1, 0).astype(BF16)
         r.qkv[i] = part
         keep = r.keep[i, 0:1, 0:64] > 0.0
-        probs, context = attention(part, keep, 64, 256, HEAD, 1.0 / math.sqrt(HEAD))
+        probs, context = attention(part, keep, 64, 256, HEAD, e_scale)
         r.probs[i] = probs
-        contexts.append(context)
-    context = jnp.concatenate(contexts, axis=0)
-    loads["w_out"].wait()
-    r.s1[...] = dot(context, r.v_w_out[...], 1, 1).astype(BF16).reshape(2, 64, WIDTH)
-    got = scatter(r.s1, r.r1, SHARD)
-    r.cz[d] = context
+        r.s1[i] = dot(context, r.v_w_out[...], 1, 1).astype(BF16)
+        sent_on.append(scatter(r.s1.at[i], r.r1.at[i], SHARD))
+        r.cz[d, i] = context
+        normeds.append(normed)
     got_c = along(r.cz)
-    got_x1 = cuts(0, normed)
-
-    info_landed()
+    got_x1 = cuts(0, normeds)
+    got_dg = gather_all(r.dgf, ROWS)
+
     loads["table"].wait()
     row = lax.broadcasted_iota(jnp.int32, (256, 1), 0)
     real = (lax.rem(row, ROWS) < PATCHES).astype(F32)
-    for i in range(PAIR):
+    for i in pair:
+        info.landed(i)
         facts = r.meta[i, 0] + r.meta[i, 1] + r.meta[i, 2] + r.meta[i, 3]
         index = facts[0:1, 0:64]
         hot = (lax.broadcasted_iota(jnp.int32, (256, 64), 0) == index).astype(F32)
@@ -853,55 +877,50 @@
 
         lax.fori_loop(0, 8, add_level, 0)
 
-    arrive(got)
-    middle = r.xs[...].astype(F32) + summed(r.s1, r.r1, SHARD)
-    r.mid[...] = middle
-    normal, _ = norm_rows(middle)
-    r.n2[:, own16, :] = (normal * e_g2).astype(BF16)
-    got = gather(r.n2, SHARD)
+    got = []
+    for i in pair:
+        arrive(sent_on[i])
+        middle = r.xs[i].astype(F32) + summed(r.s1.at[i], r.r1.at[i], SHARD)
+        r.mid[i] = middle
+        normal, _ = norm_rows(middle)
+        r.n2[i, own16, :] = (normal * e_g2).astype(BF16)
+        got.append(gather(r.n2.at[i], SHARD))
+    loads["w_up"].wait()
+    loads["w_down"].wait()
+    loads["w_proj"].wait()
+    sent_on = []
+    for i in pair:
+        arrive(got[i])
+        upper = dot(r.n2[i], r.v_w_up[...], 1, 0)
+        r.uz[d, i] = upper.astype(BF16)
+        hidden, slope = gelu_both(upper)
+        r.gp[i] = slope
+        r.s2[i] = dot(hidden.astype(BF16), r.v_w_down[...], 1, 1).astype(BF16)
+        sent_on.append(scatter(r.s2.at[i], r.r2.at[i], SHARD))
     arrive(got_dg)
     loads["d_down"].wait()
     r.dgh[...] = dot(r.dgf[...].reshape(512, 512), r.v_d_down[...], 1, 0)
-    loads["w_up"].wait()
-    loads["w_down"].wait()
-    arrive(got)
-    normed = r.n2[...].reshape(128, WIDTH)
-    hidden, slope = gelu_both(dot(normed, r.v_w_up[...], 1, 0))
-    r.gp[...] = slope
-    hidden = hidden.astype(BF16)
-    r.s2[...] = dot(hidden, r.v_w_down[...], 1, 1).astype(BF16).reshape(2, 64, WIDTH)
-    got = scatter(r.s2, r.r2, SHARD)
-    r.hz[d] = hidden
-    got_h = along(r.hz)
-    got_x2 = cuts(1, normed)
-    loads["w_proj"].wait()
-    arrive(got)
-    out_low = (r.mid[...] + summed(r.s2, r.r2, SHARD)).astype(BF16)
-    r.eo[...] = out_low
-    r.sent[...] = (
-        dot(out_low.reshape(32, WIDTH), r.v_w_proj[...], 1, 0).astype(BF16).reshape(2, 16, 512)
-    )
-
-    def own_sent(i):
-        r.arr[place, own16, :] = r.sent[i]
-
-    def slot_rows(ref):
-        return lambda i, at: ref.at[i, pl.ds(pl.multiple_of(at * SHARD, SHARD), SHARD)]
-
-    sent_landed, sent_left = exchange(lambda i: r.sent.at[i], slot_rows(r.arr), own_sent)
-    r.eom[:, own16, :] = r.eo[:, :, pl.ds(pl.multiple_of(m * 256, 256), 256)]
+    sent = exchange(lambda i: r.sent.at[i], slot_rows(r.arr), put_rows(r.arr))
+    for i in pair:
+        arrive(sent_on[i])
+        out_low = (r.mid[i] + summed(r.s2.at[i], r.r2.at[i], SHARD)).astype(BF16)
+        r.eo[i] = out_low
+        r.sent[i] = dot(out_low, r.v_w_proj[...], 1, 0).astype(BF16)
+        sent.start(i)
+    r.ez[d, :, own16] = r.eo[:, :, pl.ds(pl.multiple_of(m * 256, 256), 256)]
     got_eo = []
     for k in (1, 2, 3):
         columns = pl.ds(pl.multiple_of(model(k) * 256, 256), 256)
-        got_eo.append(send(r.eo.at[:, :, columns], r.eom.at[:, own16], {"mp": model(k)}))
+        got_eo.append(send(r.eo.at[:, :, columns], r.ez.at[d, :, own16], {"mp": model(k)}))
 
     loads["d_qkv"].wait()
     loads["d_out"].wait()
-    sent_landed()
+    loads["d_up"].wait()
     cols = lax.broadcasted_iota(jnp.int32, (1, 256), 1)
     d_keep = lax.rem(cols, ROWS) < PATCHES
-    d_scale = 1.0 / math.sqrt(DEC_HEAD)
-    for i in range(PAIR):
+    sent_on = []
+    for i in pair:
+        sent.landed(i)
         values = r.grid[i] + dot(r.hot[i], r.arr[i], 1, 0)
         r.grid[i] = values
         normal, _ = norm_rows(values)
@@ -914,63 +933,85 @@
         r.dprobs[i] = probs
         r.dctx[at, :] = context
         r.s3[i] = dot(context, r.v_d_out[...], 1, 1).astype(BF16)
-    got = scatter(r.s3, r.r3, ROWS)
-    loads["d_up"].wait()
-    arrive(got)
-    middle = r.grid[:, own64, :] + summed(r.s3, r.r3, ROWS)
-    r.dmid[...] = middle
-    normal, _ = norm_rows(middle)
-    r.dn2[:, own64, :] = (normal * d_g2).astype(BF16)
-    got = gather(r.dn2, ROWS)
-    arrive(got)
-    hidden, slope = gelu_both(dot(r.dn2[...].reshape(512, 512), r.v_d_up[...], 1, 0))
-    grad_upper = (r.dgh[...] * slope).astype(BF16)
-    r.dhid[...] = hidden.astype(BF16)
-    r.dgu[...] = grad_upper
-
-    r.s4[...] = dot(grad_upper, r.v_d_up[...], 1, 1).astype(BF16).reshape(2, 256, 512)
-    got = scatter(r.s4, r.r4, ROWS)
-    r.grid_out = dot(r.dhid[...], r.v_d_down[...], 1, 1).reshape(2, 256, 512)
+        sent_on.append(scatter(r.s3.at[i], r.r3.at[i], ROWS))
+    got_u = along(r.uz)
+    got_x2 = cuts(1, [r.n2[0], r.n2[1]])
+    arrive(got_eo)
+    got_ez = along(r.ez)
+    got = []
+    for i in pair:
+        arrive(sent_on[i])
+        middle = r.grid[i, own64, :] + summed(r.s3.at[i], r.r3.at[i], ROWS)
+        r.dmid[i] = middle
+        normal, _ = norm_rows(middle)
+        r.dn2[i, own64, :] = (normal * d_g2).astype(BF16)
+        got.append(gather(r.dn2.at[i], ROWS))
+    sent_on = []
+    for i in pair:
+        arrive(got[i])
+        at = slice(i * 256, (i + 1) * 256)
+        hidden, slope = gelu_both(dot(r.dn2[i], r.v_d_up[...], 1, 0))
+        grad_upper = (r.dgh[at, :] * slope).astype(BF16)
+        r.dhid[at, :] = hidden.astype(BF16)
+        r.dgu[at, :] = grad_upper
+        r.s4[i] = dot(grad_upper, r.v_d_up[...], 1, 1).astype(BF16)
+        sent_on.append(scatter(r.s4.at[i], r.r4.at[i], ROWS))
+
+    def dec_weights(left, right, own, away, first):
+        size = right.shape[1]
+        for a in (0, 1):
+            rows = pl.ds(pl.multiple_of(lax.rem(s + a, 2) * 256, 256), 256)
+            value = dot(left[:, rows], right[...], 0, 0)
+            if a == 0:
+                own[:, first : first + size] = value
+            else:
+                away[:, first : first + size] = value.astype(BF16)
+
+    def dec_sums(own, arrived, away, landing):
+        for block in range(4):
+            at = slice(block * 64, (block + 1) * 64)
+            own[at, :] = own[at, :] + arrived[at, :].astype(F32)
+            away[block] = own[at, :].astype(BF16)
+        return [send(away.at[data(k)], landing.at[k - 1], {"dp": data(k)}) for k in (1, 2, 3)]
+
+    dec_weights(r.dn2.reshape(512, 512), r.dgu, r.w1o, r.w1s, 0)
+    dec_weights(r.dgf.reshape(512, 512), r.dhid, r.w1o, r.w1s, 512)
+    got_w1 = [send(r.w1s, r.w1r, to_plane(1, 0))]
+    r.vec[...] = jnp.zeros((8, 512), F32)
+    got = []
+    gain_sum = jnp.zeros((1, 512), F32)
+    for i in pair:
+        arrive(sent_on[i])
+        total = summed(r.s4.at[i], r.r4.at[i], ROWS)
+        normal, inverse = norm_rows(r.dmid[i])
+        grad = r.dgrad[i].astype(F32) + rows_back(normal, inverse, d_g2, total)
+        gain_sum += jnp.sum(total * normal, axis=0, keepdims=True)
+        r.dgm[i, own64, :] = grad.astype(BF16)
+        got.append(gather(r.dgm.at[i], ROWS))
+    r.vec[5:6, :] = gain_sum
     shard = lax.broadcasted_iota(jnp.int32, (256, 1), 0) // ROWS
     here = (shard == m).astype(F32)
     parts = []
-    for i in range(PAIR):
+    for i in pair:
         whole = jnp.concatenate([r.dmid[i]] * 4, axis=0)
-        parts.append((r.grid_out[i] + whole * here).astype(F32))
+        value = dot(r.dhid[i * 256 : (i + 1) * 256, :], r.v_d_down[...], 1, 1)
+        parts.append(value + whole * here)
     for block in range(8):
         at = slice(block * 64, (block + 1) * 64)
         r.ds[block] = jnp.concatenate([parts[0][:, at], parts[1][:, at]], axis=1).astype(BF16)
-    rank = s * 4 + m
     got_dec = []
     for a, k in plane:
         to = lax.rem(s + a, 2) * 4 + model(k)
         got_dec.append(send(r.ds.at[to], r.dr.at[rank], to_plane(a, k)))
     r.dr[rank] = r.ds[rank]
-
-    def dec_weights(left, right, first, size):
-        for a in (0, 1):
-            rows = pl.ds(pl.multiple_of(lax.rem(s + a, 2) * 256, 256), 256)
-            value = dot(left[:, rows], right[...], 0, 0)
-            if a == 0:
-                r.wdo[:, first : first + size] = value
-            else:
-                r.wds[:, first : first + size] = value.astype(BF16)
-
-    flat = lambda ref, rows, width: ref.reshape(rows, width)
-    dec_weights(flat(r.dn2, 512, 512), r.dgu, 512, 512)
-    arrive(got)
-    total = summed(r.s4, r.r4, ROWS)
-    normal, inverse = norm_rows(r.dmid[...])
-    grad = r.dgrad[...].astype(F32) + rows_back(normal, inverse, d_g2, total)
-    r.vec[...] = jnp.zeros((8, 512), F32)
-    r.vec[5:6, :] = jnp.sum((total * normal).reshape(128, 512), axis=0, keepdims=True)
-    r.dgm[:, own64, :] = grad.astype(BF16)
-    got = gather(r.dgm, ROWS)
-    dec_weights(flat(r.dgf, 512, 512), r.dhid, 1024, 512)
-    arrive(got)
+    arrive(got_w1)
+    got_z1 = dec_sums(r.w1o, r.w1r, r.z1s, r.z1r)
+
     gain_sum = jnp.zeros((1, 512), F32)
     token_sum = jnp.zeros((1, 512), F32)
-    for i in range(PAIR):
+    sent_on = []
+    for i in pair:
+        arrive(got[i])
         at = slice(i * 256, (i + 1) * 256)
         grad_low = r.dgm[i]
         grad_context = dot(grad_low, r.v_d_out[...], 1, 0).astype(BF16)
@@ -984,162 +1025,153 @@
         back = rows_back(normal, inverse, d_g1, terms) + 0.25 * grad_low.astype(F32)
         token_sum += jnp.sum(back * r.free[i], axis=0, keepdims=True)
         r.s5[i] = dot(r.hot[i], back.astype(BF16), 0, 0).astype(BF16)
-    got = scatter(r.s5, r.r5, SHARD)
+        sent_on.append(scatter(r.s5.at[i], r.r5.at[i], SHARD))
     r.vec[4:5, :] = gain_sum
     r.vec[6:7, :] = token_sum
-    dec_weights(flat(r.dgm, 512, 512), r.dctx, 384, 128)
-    dec_weights(r.dn1, r.dgq, 0, 384)
-    got_wd = [send(r.wds, r.wdr, to_plane(1, 0))]
-    arrive(got)
-    r.sg[...] = summed(r.s5, r.r5, SHARD).astype(BF16)
-
-    def own_back(i):
-        r.sgf[place, own16, :] = r.sg[i]
-
-    back_landed, back_left = exchange(lambda i: r.sg.at[i], slot_rows(r.sgf), own_back)
+
+    def put_back(i):
+        r.sz[d, place, m] = r.sg[i]
+
+    back = exchange(
+        lambda i: r.sg.at[i], lambda i, at: r.sz.at[to_dp(), i, at], put_back
+    )
+    for i in pair:
+        arrive(sent_on[i])
+        r.sg[i] = summed(r.s5.at[i], r.r5.at[i], SHARD).astype(BF16)
+        back.start(i)
+    dec_weights(r.dn1, r.dgq, r.w2o, r.w2s, 0)
+    dec_weights(r.dgm.reshape(512, 512), r.dctx, r.w2o, r.w2s, 384)
+    got_w2 = [send(r.w2s, r.w2r, to_plane(1, 0))]
+
+    sent_on = []
+    for i in pair:
+        back.landed(i)
+        grad_low = dot(r.sz[d, i].reshape(64, 512), r.v_w_proj[...], 1, 1).astype(BF16)
+        grad_upper = (dot(grad_low, r.v_w_down[...], 1, 0) * r.gp[i]).astype(BF16)
+        r.s6[i] = dot(grad_upper, r.v_w_up[...], 1, 1).astype(BF16)
+        sent_on.append(scatter(r.s6.at[i], r.r6.at[i], SHARD))
+    got_sz = [
+        send(r.sz.at[d, :, m], r.sz.at[d, :, m], {"dp": data(k)}) for k in (1, 2, 3)
+    ]
+    arrive(got_w2)
+    got_z2 = dec_sums(r.w2o, r.w2r, r.z2s, r.z2r)
+    got = []
+    gain_two = jnp.zeros((1, WIDTH), F32)
+    for i in pair:
+        arrive(sent_on[i])
+        total = summed(r.s6.at[i], r.r6.at[i], SHARD)
+        normal, inverse = norm_rows(r.mid[i])
+        own_grad = dot(r.sz[d, i, m], r.v_w_proj[...], 1, 1)
+        grad = own_grad + rows_back(normal, inverse, e_g2, total)
+        gain_two += jnp.sum(total * normal, axis=0, keepdims=True)
+        r.gm[i, own16, :] = grad.astype(BF16)
+        got.append(gather(r.gm.at[i], SHARD))
+    r.vec[2:3, :] = gain_two[:, :512]
+    r.vec[3:4, :] = gain_two[:, 512:]
+    arrive(got_sz)
+    got_sm = []
+    for k in (1, 2, 3):
+        for j in (1, 2, 3):
+            part = r.sz.at[data(k), :, m]
+            got_sm.append(send(part, r.sz.at[data(k), :, m], {"mp": model(j)}))
+    gain_one = jnp.zeros((1, WIDTH), F32)
+    got_f, got_q = [], []
+    for i in pair:
+        arrive(got[i])
+        grad_low = r.gm[i]
+        grad_context = dot(grad_low, r.v_w_out[...], 1, 0).astype(BF16)
+        part = attention_back(r.qkv[i], r.probs[i], grad_context, 64, 256, HEAD, e_scale)
+        r.qz[d, i] = part
+        got_q += [send(r.qz.at[d, i], r.qz.at[d, i], {"dp": data(k)}) for k in (1, 2, 3)]
+        terms = dot(part, r.v_w_qkv[...], 1, 1)
+        normal, inverse = norm_rows(r.xf[i].astype(F32))
+        gain_one += jnp.sum(terms * normal, axis=0, keepdims=True)
+        grad = rows_back(normal, inverse, e_g1, terms) + 0.25 * grad_low.astype(F32)
+        for block in range(8):
+            r.fs[block, i] = grad[:, block * 128 : (block + 1) * 128].astype(BF16)
+        for a, k in plane:
+            to = lax.rem(s + a, 2) * 4 + model(k)
+            got_f.append(send(r.fs.at[to, i], r.fr.at[rank, i], to_plane(a, k)))
+        r.fr[rank, i] = r.fs[rank, i]
+    got_x4 = cuts(2, [r.gm[0], r.gm[1]])
+    r.vec[0:1, :] = gain_one[:, :512]
+    r.vec[1:2, :] = gain_one[:, 512:]
+    r.vr[rank] = r.vec[...]
+    got_v = [send(r.vec, r.vr.at[rank], to_plane(a, k)) for a, k in plane]
+
+    def enc_weights(lefts, value, first, out):
+        size = value.shape[1]
+        r.wes[:, first : first + size] = dot(lefts[1], value, 0, 0).astype(BF16)
+        made = send(
+            r.wes.at[:, first : first + size], r.wer.at[:, first : first + size], to_plane(1, 0)
+        )
+        out[...] = dot(lefts[0], value, 0, 0)
+        return made
+
+    def cut_rows(which):
+        return [r.xz[which, :, lax.rem(s + a, 2)].reshape(512, 128) for a in (0, 1)]
+
+    arrive(got_u)
+    hidden, slope = gelu_both(r.uz[...].reshape(512, WIDTH).astype(F32))
+    r.ha[...] = hidden.astype(BF16)
+    arrive(got_sm)
+    grad_all = r.sz[...].reshape(512, 512)
+    r.ga[...] = dot(grad_all, r.v_w_proj[...], 1, 1).astype(BF16)
+    grad_upper = (dot(r.ga[...], r.v_w_down[...], 1, 0) * slope).astype(BF16)
+    lefts = []
+    for a in (0, 1):
+        block = lax.rem(s + a, 2) * 4 + d
+        lefts.append(r.ga[:, pl.ds(pl.multiple_of(block * 128, 128), 128)])
+    got_w = [enc_weights(lefts, r.ha[...], 2048, r.o_down)]
+    arrive(got_x2)
+    got_w.append(enc_weights(cut_rows(1), grad_upper, 1024, r.o_up))
+
+    arrive(got_ez)
+    r.ps[...] = dot(r.ez[...].reshape(512, 256), grad_all, 0, 0).astype(BF16)
+    got_p = [send(r.ps, r.pr, to_plane(1, 0))]
+    arrive(got_z1)
+    mine64 = pl.ds(pl.multiple_of(d * 64, 64), 64)
+    total = r.w1o[mine64, :]
+    for k in range(3):
+        total = total + r.z1r[k].astype(F32)
+    r.o_dup[...] = total[:, :512]
+    r.o_ddown[...] = total[:, 512:]
+    arrive(got_z2)
+    total = r.w2o[mine64, :]
+    for k in range(3):
+        total = total + r.z2r[k].astype(F32)
+    r.o_dqkv[...] = total[:, :384]
+    r.o_dout[...] = total[:, 384:]
+    arrive(got_p)
+    half_rows = pl.ds(pl.multiple_of(s * 128, 128), 128)
+    r.pa[m, s] = (r.ps[half_rows, :].astype(F32) + r.pr[half_rows, :].astype(F32)).astype(BF16)
+    got_pa = [send(r.pa.at[m, s], r.pa.at[m, s], {"mp": model(k)}) for k in (1, 2, 3)]
+    arrive(got_v)
+    total = r.vr[0]
+    for k in range(1, 8):
+        total = total + r.vr[k]
+    r.vz[d] = total
+    got_vz = along(r.vz)
     arrive(got_dec)
     for a in (0, 1):
         total = r.dr[4 * a].astype(F32)
         for k in (1, 2, 3):
             total = total + r.dr[4 * a + k].astype(F32)
         r.o_dec[a] = total
-    arrive(got_wd)
-    for block in range(4):
-        at = slice(block * 64, (block + 1) * 64)
-        r.wdo[at, :] = r.wdo[at, :] + r.wdr[at, :].astype(F32)
-        r.wzs[block] = r.wdo[at, :].astype(BF16)
-    got_wz = [
-        send(r.wzs.at[data(k)], r.wzr.at[k - 1], {"dp": data(k)}) for k in (1, 2, 3)
-    ]
-
-    back_landed()
-    grad_sent = r.sgf[...].reshape(128, 512)
-    grad_low = dot(grad_sent, r.v_w_proj[...], 1, 1).astype(BF16)
-    r.gy[...] = grad_low
-    grad_upper = (dot(grad_low, r.v_w_down[...], 1, 0) * r.gp[...]).astype(BF16)
-    r.s6[...] = dot(grad_upper, r.v_w_up[...], 1, 1).astype(BF16).reshape(2, 64, WIDTH)
-    got = scatter(r.s6, r.r6, SHARD)
-    r.uz[d] = grad_upper
-    got_u = along(r.uz)
-    got_x3 = cuts(2, grad_low)
-    arrive(got_eo)
-    product = dot(r.eom[...].reshape(128, 256), grad_sent, 0, 0)
-    for a in (0, 1):
-        r.ps[a] = product[a * 128 : (a + 1) * 128].astype(BF16)
-    other = lax.rem(s + 1, 2)
-    got_p = [send(r.ps.at[other], r.pr, to_plane(1, 0))]
-    arrive(got)
-    total = summed(r.s6, r.r6, SHARD)
-    normal, inverse = norm_rows(r.mid[...])
-    own_sent_grad = r.sgf[:, own16, :].reshape(32, 512)
-    own_grad = dot(own_sent_grad, r.v_w_proj[...], 1, 1).reshape(2, 16, WIDTH)
-    grad = own_grad + rows_back(normal, inverse, e_g2, total)
-    r.gm[:, own16, :] = grad.astype(BF16)
-    got = gather(r.gm, SHARD)
-    gain_two = jnp.sum((total * normal).reshape(32, WIDTH), axis=0, keepdims=True)
-    r.vec[2:3, :] = gain_two[:, :512]
-    r.vec[3:4, :] = gain_two[:, 512:]
-
-    arrive(got_p)
-    kept = r.ps[s].astype(F32) + r.pr[...].astype(F32)
-    r.po[...] = kept
-    for block in range(4):
-        r.pzs[block] = kept[block * 32 : (block + 1) * 32].astype(BF16)
-    got_pz = [send(r.pzs.at[data(k)], r.pzr.at[k - 1], {"dp": data(k)}) for k in (1, 2, 3)]
-
-    arrive(got)
-    grad_low = r.gm[...].reshape(128, WIDTH)
-    grad_context = dot(grad_low, r.v_w_out[...], 1, 0).astype(BF16)
-    parts = []
-    for i in range(PAIR):
-        parts.append(
-            attention_back(
-                r.qkv[i],
-                r.probs[i],
-                grad_context[i * 64 : (i + 1) * 64],
-                64,
-                256,
-                HEAD,
-                1.0 / math.sqrt(HEAD),
-            )
-        )
-    part = jnp.concatenate(parts, axis=0)
-    r.qz[d] = part
-    got_q = along(r.qz)
-    got_x4 = cuts(3, grad_low)
-    terms = dot(part, r.v_w_qkv[...], 1, 1)
-    normal, inverse = norm_rows(r.xf[...].reshape(128, WIDTH).astype(F32))
-    gain_one = jnp.sum(terms * normal, axis=0, keepdims=True)
-    r.vec[0:1, :] = gain_one[:, :512]
-    r.vec[1:2, :] = gain_one[:, 512:]
-    back = rows_back(normal, inverse, e_g1, terms) + 0.25 * grad_low.astype(F32)
-    for block in range(8):
-        r.fs[block] = back[:, block * 128 : (block + 1) * 128].astype(BF16)
-    got_f = []
-    for a, k in plane:
-        to = lax.rem(s + a, 2) * 4 + model(k)
-        got_f.append(send(r.fs.at[to], r.fr.at[rank], to_plane(a, k)))
-    r.fr[rank] = r.fs[rank]
-    r.vr[rank] = r.vec[...]
-    got_v = [send(r.vec, r.vr.at[rank], to_plane(a, k)) for a, k in plane]
-
-    arrive(got_pz)
-    mine32 = pl.ds(pl.multiple_of(d * 32, 32), 32)
-    total = r.po[mine32, :]
-    for k in range(3):
-        total = total + r.pzr[k].astype(F32)
-    r.pz[d] = total.astype(BF16)
-    got_pg = along(r.pz)
-
-    def enc_weights(which, right, first, size, out):
-        lefts = [
-            r.xz[which, :, lax.rem(s + a, 2), :, :].reshape(512, 128) for a in (0, 1)
-        ]
-        value = right[...].reshape(512, size)
-        r.wes[:, first : first + size] = dot(lefts[1], value, 0, 0).astype(BF16)
-        made = send(
-            r.wes.at[:, first : first + size], r.wer.at[:, first : first + size], to_plane(1, 0)
-        )
-        out[...] = dot(lefts[0], value, 0, 0)
-        return made
-
-    arrive(got_h)
-    arrive(got_x3)
-    got_w = [enc_weights(2, r.hz, 2048, 1024, r.o_down)]
-    arrive(got_x2)
-    arrive(got_u)
-    got_w.append(enc_weights(1, r.uz, 1024, 1024, r.o_up))
-    arrive(got_wz)
-    total = r.wdo[pl.ds(pl.multiple_of(d * 64, 64), 64), :]
-    for k in range(3):
-        total = total + r.wzr[k].astype(F32)
-    r.o_dqkv[...] = total[:, :384]
-    r.o_dout[...] = total[:, 384:512]
-    r.o_dup[...] = total[:, 512:1024]
-    r.o_ddown[...] = total[:, 1024:]
-    arrive(got_v)
-    total = r.vr[0]
-    for k in range(1, 8):
-        total = total + r.vr[k]
-    r.vz[d] = total
-    got_vz = along(r.vz)
-    arrive(got_pg)
-    r.pa[m, s] = r.pz[...].reshape(128, 512)
-    got_pa = [send(r.pa.at[m, s], r.pa.at[m, s], {"mp": model(k)}) for k in (1, 2, 3)]
     arrive(got_f)
     for a in (0, 1):
         total = r.fr[4 * a].astype(F32)
         for k in (1, 2, 3):
             total = total + r.fr[4 * a + k].astype(F32)
-        r.o_pat[a] = total
+        r.o_pat[a] = total.reshape(128, 128)
     arrive(got_pa)
     got_ps = [send(r.pa.at[:, s], r.pa.at[:, s], to_plane(1, 0))]
     arrive(got_c)
     arrive(got_x4)
-    got_w.append(enc_weights(3, r.cz, 768, 256, r.o_out))
+    got_w.append(enc_weights(cut_rows(2), r.cz[...].reshape(512, 256), 768, r.o_out))
     arrive(got_x1)
     arrive(got_q)
-    got_w.append(enc_weights(0, r.qz, 0, 768, r.o_qkv))
+    got_w.append(enc_weights(cut_rows(0), r.qz[...].reshape(512, 768), 0, r.o_qkv))
     arrive(got_vz)
     r.o_vec[...] = r.vz[0] + r.vz[1] + r.vz[2] + r.vz[3]
     arrive(got_ps)
@@ -1153,8 +1185,8 @@
         out[...] += r.wer[:, first : first + size].astype(F32)
     for made in started:
         made.wait_send()
-    for leave in (info_left, sent_left, back_left):
-        leave()
+    for leave in (info, sent, back):
+        leave.left()
     assert used[0] <= COPIES
 
 

time: 226 us -> 168 us (0.74)
  Pallas kernels: 187 us -> 130 us
    pallas_call x1, Pallas kernels: 187 us -> 130 us  [with_kernel(): pl.pallas_call(kernel, out_shape=[jax.ShapeDtypeStruct(shape, F32) for sh...]
where the time goes in v2:
time: 168 us; the launch traced here: 167 us
  Pallas kernels  130 us (77%)
  local copies, waits for them, and re-layouts  30.2 us (18%)
  other arithmetic  5.77 us (3%)
    pallas_call x1, Pallas kernels, with_kernel(): pl.pallas_call(kernel, out_shape=[jax.ShapeDtypeStruct(shape, F32) for sh...  130 us
    unnamed x33, local copies, waits for them, and re-layouts  14.9 us
    broadcast_in_dim x5, other arithmetic, with_kernel(): wide = lambda v: jnp.pad(v.astype(F32), (0, WIDTH - v.shape[0]))[None, :]  3.41 us

profile of v2, /device:TPU:0, one launch (start us, length us, event | category | flops | bytes accessed | tf_op | source)
XLA Modules:
  0.0 167.0 jit_solution(2970711484795383812)
XLA Ops:
  0.7 0.9 broadcast_select_fusion
  1.6 0.7 dynamic_slice.16
  2.3 0.8 compare_select_fusion
  3.4 0.7 broadcast_in_dim.81
  4.0 0.7 broadcast_in_dim.82
  4.7 0.7 pad_convert_fusion
  5.4 0.7 pad_convert_fusion.2
  6.1 0.7 pad_convert_fusion.1
  6.8 0.7 add_add_fusion.refs_1_
  8.0 0.7 concatenate.7.refs_3_
  8.7 1.0 constant_dynamic-slice_fusion.1
  10.5 0.7 pad.24.refs_4_
  11.1 1.2 copy.51
  12.3 0.9 copy.53.refs_11_
  13.2 0.9 copy.49
  14.1 1.6 copy.52.refs_5_
  16.3 1.6 pad.25
  17.9 130.2 %layer_pair.1 = (f32[2,256,128]{2,1,0:T(8,128)}, f32[2,128,128]{2,1,0:T(8,128)}, f32[128,768]{1,0:T(8,128)}, f32[128,256]{1,0:T(8,128)}, f32[128,1024]{1,0:T(8,1...) custom-call(bf16[2,16,1024]{2,1,0:T(8,128)(2,1)} %bitcast.65, ...), custom_call_target="tpu_custom_call" | custom-call | tf_op jit(solution)/shard_map/layer_pair/pallas_call | solution.py:1281
  148.1 1.7 copy.55
  149.8 1.4 fusion.3
  151.2 0.8 slice_bitcast_fusion
  153.2 1.5 copy_bitcast_fusion.1
  154.7 1.3 reshape.98
  156.3 1.0 reshape.99
  157.3 1.3 copy.56
  158.6 0.9 copy.57
  159.5 1.6 copy.78
  161.1 1.9 %copy.79 = f32[128,1024]{1,0:T(8,128)} copy(f32[128,1024]{1,0:T(8,128)} %get-tuple-element.97) | data formatting | bytes 1048576
  163.0 0.8 copy.80
  164.4 0.7 copy.82
  165.1 0.7 copy.83
  165.7 1.3 copy.84
  (34 shorter events, 4.4 us)
Async XLA Ops:
  0.6 9.7 %copy-start = (bf16[49,4,512]{2,1,0:T(4,128)(2,1)S(1)}, bf16[49,4,512]{2,1,0:T(4,128)(2,1)}, u32[]{:S(2)}) copy-start(bf16[49,4,512]{2,1,0:T(4,128)(2,1)} %param.39) | copy-start | bytes 602116
  0.7 12.6 %copy-start.3 = (bf16[1024,3,256]{2,0,1:T(8,128)(2,1)S(1)}, bf16[1024,3,256]{2,0,1:T(8,128)(2,1)}, u32[]{:S(2)}) copy-start(bf16[1024,3,256]{2,0,1:T(8,128)(2,1)} %param.25) | copy-start | bytes 4718596
  14.1 1.6 copy-start.2
  156.0 6.9 %copy-start.4 = (f32[128,1024]{1,0:T(8,128)S(1)}, f32[128,1024]{1,0:T(8,128)}, u32[]{:S(2)}) copy-start(f32[128,1024]{1,0:T(8,128)} %get-tuple-element.98) | copy-start | bytes 1572868
  157.3 6.5 %copy-start.7 = (f32[64,128]{1,0:T(8,128)S(1)}, f32[64,128]{1,0:T(8,128)}, u32[]{:S(2)}) copy-start(f32[64,128]{1,0:T(8,128)} %get-tuple-element.100) | copy-start | bytes 98308
  157.3 7.1 %copy-start.6 = (f32[64,512]{1,0:T(8,128)S(1)}, f32[64,512]{1,0:T(8,128)}, u32[]{:S(2)}) copy-start(f32[64,512]{1,0:T(8,128)} %get-tuple-element.101) | copy-start | bytes 393220
  157.3 7.8 %copy-start.5 = (f32[64,512]{1,0:T(8,128)S(1)}, f32[64,512]{1,0:T(8,128)}, u32[]{:S(2)}) copy-start(f32[64,512]{1,0:T(8,128)} %get-tuple-element.102) | copy-start | bytes 393220
  157.3 8.4 %copy-start.1 = (f32[1024,512]{1,0:T(8,128)S(1)}, f32[1024,512]{1,0:T(8,128)}, u32[]{:S(2)}) copy-start(f32[1024,512]{1,0:T(8,128)} %get-tuple-element.103) | copy-start | bytes 6291460

commit v3 on v2

--- a/solution.py
+++ b/solution.py
@@ -469,6 +469,11 @@
 COPIES = 256
 
 
+def padded_row(patch):
+    shard = sum((patch >= k * PATCHES).astype(jnp.int32) for k in (1, 2, 3))
+    return patch + (ROWS - PATCHES) * shard
+
+
 def dot(left, right, left_dim, right_dim):
     return lax.dot_general(
         left, right, (((left_dim,), (right_dim,)), ((), ())), preferred_element_type=F32
@@ -536,9 +541,14 @@
 
 IN_NAMES = [
     "xs",
-    "info",
-    "keep",
-    "gains",
+    "counts",
+    "index",
+    "levels",
+    "g1",
+    "g2",
+    "g3",
+    "g4",
+    "g5",
     "dgrad",
     "w_qkv",
     "w_out",
@@ -563,7 +573,11 @@
     "o_dup",
     "o_ddown",
     "o_proj",
-    "o_vec",
+    "o_v1",
+    "o_v2",
+    "o_v3",
+    "o_v4",
+    "o_v5",
 ]
 LOADED = dict(
     w_qkv=(WIDTH, 768),
@@ -571,13 +585,27 @@
     w_up=(WIDTH, 1024),
     w_down=(WIDTH, 1024),
     w_proj=(WIDTH, DEC_WIDTH),
-    table=(8, 256, DEC_WIDTH),
+    table=(196, 8, DEC_WIDTH),
     d_qkv=(DEC_WIDTH, 384),
     d_out=(DEC_WIDTH, 128),
     d_up=(DEC_WIDTH, 512),
     d_down=(DEC_WIDTH, 512),
 )
+STORED = dict(
+    o_dec=(4, 64, 196),
+    o_qkv=(3, 128, 256),
+    o_out=(128, 256),
+    o_up=(128, 1024),
+    o_down=(128, 1024),
+    o_dqkv=(3, 64, 128),
+    o_dout=(64, 128),
+    o_dup=(64, 512),
+    o_ddown=(64, 512),
+    o_proj=(1024, 512),
+)
 BUFFERS = dict(
+    info=((2, 8, 128), jnp.int32),
+    flat=((1568, 512), BF16),
     xf=((2, 64, 1024), BF16),
     qkv=((2, 64, 768), BF16),
     probs=((2, 256, 64), F32),
@@ -642,6 +670,7 @@
     ga=((512, 1024), BF16),
     wes=((128, 3072), BF16),
     wer=((128, 3072), BF16),
+    own_qkv=((128, 768), F32),
     ps=((256, 512), BF16),
     pr=((256, 512), BF16),
     pa=((4, 2, 128, 512), BF16),
@@ -657,10 +686,10 @@
 
 def kernel(*refs):
     r = Refs()
-    names = IN_NAMES + OUT_NAMES + list(BUFFERS) + ["v_" + n for n in LOADED]
+    names = IN_NAMES + OUT_NAMES + list(BUFFERS) + ["v_" + n for n in (*LOADED, *STORED)]
     for name, ref in zip(names, refs):
         setattr(r, name, ref)
-    load_sem, send_sem, recv_sem = refs[len(names) :]
+    load_sem, store_sem, send_sem, recv_sem = refs[len(names) :]
     s, d, m = (lax.axis_index(a) for a in ("section", "dp", "mp"))
     used = [0]
     started = []
@@ -795,11 +824,36 @@
         return put
 
     loads = {}
-    for at, name in enumerate(LOADED):
-        loads[name] = pltpu.make_async_copy(
-            getattr(r, name), getattr(r, "v_" + name), load_sem.at[at]
-        )
-        loads[name].start()
+
+    def load(name, parts):
+        src, dst = getattr(r, name), getattr(r, "v_" + name)
+        if not parts:
+            return [(src, dst)]
+        width = dst.shape[1] // parts
+        return [(src.at[c], dst.at[:, c * width : (c + 1) * width]) for c in range(parts)]
+
+    at = 0
+    for name in LOADED:
+        loads[name] = []
+        for src, dst in load(name, 3 if name in ("w_qkv", "d_qkv") else 0):
+            loads[name].append(pltpu.make_async_copy(src, dst, load_sem.at[at]))
+            at += 1
+        for made in loads[name]:
+            made.start()
+
+    def loaded(*which):
+        for name in which:
+            for made in loads[name]:
+                made.wait()
+
+    stores = []
+
+    def store(*which):
+        for name in which:
+            at = list(STORED).index(name)
+            made = pltpu.make_async_copy(getattr(r, "v_" + name), getattr(r, name), store_sem.at[at])
+            made.start()
+            stores.append(made)
 
     barrier = pltpu.get_barrier_semaphore()
     for a, k in plane:
@@ -817,9 +871,8 @@
                 pl.when(jnp.logical_not(mine(i)))(signal)
     pl.semaphore_wait(barrier, 7 + 3 + 8 - (half == s).astype(jnp.int32))
 
-    gain = [r.gains[i : i + 1, :] for i in range(5)]
-    e_g1, e_g2 = gain[0], gain[1]
-    d_g1, d_g2, token = (g[:, :DEC_WIDTH] for g in gain[2:5])
+    e_g1, e_g2 = (g[...].astype(F32).reshape(1, WIDTH) for g in (r.g1, r.g2))
+    d_g1, d_g2, token = (g[...].astype(F32).reshape(1, DEC_WIDTH) for g in (r.g3, r.g4, r.g5))
 
     own16 = pl.ds(pl.multiple_of(m * SHARD, SHARD), SHARD)
     own64 = pl.ds(pl.multiple_of(m * ROWS, ROWS), ROWS)
@@ -829,14 +882,29 @@
     rank = s * 4 + m
     pair = range(PAIR)
 
-    r.xf[:, own16, :] = r.xs[...]
-    got = [gather(r.xf.at[i], SHARD) for i in pair]
+    def own_images(ref):
+        values = ref[...].astype(F32)
+        return [jnp.where(s == 0, values[:, i], values[:, PAIR + i]) for i in pair]
+
+    got = []
+    for i, rows in enumerate(own_images(r.xs)):
+        r.xf[i, own16, :] = rows.astype(BF16)
+        got.append(gather(r.xf.at[i], SHARD))
+    slot = m * SHARD + lax.broadcasted_iota(jnp.int32, (1, SHARD), 1)
+    r.info[...] = jnp.zeros((2, 8, 128), jnp.int32)
+    for i in pair:
+        patch = r.index[pl.ds(PAIR * s + i, 1), :]
+        live = slot < r.counts[PAIR * s + i]
+        r.info[i, 0:1, 0:SHARD] = jnp.where(live, padded_row(patch), -1)
+        r.info[i, 1:2, :] = jnp.zeros((1, 128), jnp.int32) + r.levels[PAIR * s + i]
     info = exchange(lambda i: r.info.at[i], lambda i, at: r.meta.at[i, at], put_info)
     for i in pair:
         info.start(i)
-    r.dgf[:, own64, :] = r.dgrad[...]
-    loads["w_qkv"].wait()
-    loads["w_out"].wait()
+    for i, rows in enumerate(own_images(r.dgrad)):
+        rows = jnp.concatenate([rows, jnp.zeros((ROWS - PATCHES, DEC_WIDTH), F32)], axis=0)
+        r.dgf[i, own64, :] = rows.astype(BF16)
+    loaded("w_qkv")
+    loaded("w_out")
     sent_on = []
     contexts, normeds = [], []
     for i in pair:
@@ -845,7 +913,7 @@
         normed = (normal * e_g1).astype(BF16)
         part = dot(normed, r.v_w_qkv[...], 1, 0).astype(BF16)
         r.qkv[i] = part
-        keep = r.keep[i, 0:1, 0:64] > 0.0
+        keep = lax.broadcasted_iota(jnp.int32, (1, SLOTS), 1) < r.counts[PAIR * s + i]
         probs, context = attention(part, keep, 64, 256, HEAD, e_scale)
         r.probs[i] = probs
         r.s1[i] = dot(context, r.v_w_out[...], 1, 1).astype(BF16)
@@ -856,38 +924,38 @@
     got_x1 = cuts(0, normeds)
     got_dg = gather_all(r.dgf, ROWS)
 
-    loads["table"].wait()
     row = lax.broadcasted_iota(jnp.int32, (256, 1), 0)
-    real = (lax.rem(row, ROWS) < PATCHES).astype(F32)
-    for i in pair:
+    is_real = lax.rem(row, ROWS) < PATCHES
+    real = is_real.astype(F32)
+    entry = jnp.where(is_real, (row - (ROWS - PATCHES) * (row // ROWS)) * 8, -8)
+
+    def start_grid(i):
         info.landed(i)
-        facts = r.meta[i, 0] + r.meta[i, 1] + r.meta[i, 2] + r.meta[i, 3]
-        index = facts[0:1, 0:64]
+        index = jnp.concatenate([r.meta[i, k, 0:1, 0:SHARD] for k in range(4)], axis=1)
         hot = (lax.broadcasted_iota(jnp.int32, (256, 64), 0) == index).astype(F32)
         free = real - jnp.sum(hot, axis=1, keepdims=True)
         r.hot[i] = hot.astype(BF16)
         r.free[i] = free
-        r.grid[i] = free * token
-        level = facts[1:2, 0:1]
-
-        def add_level(l, carry):
-            chosen = (level == l).astype(F32)
-            r.grid[i] += chosen * r.v_table[l].astype(F32)
-            return carry
-
-        lax.fori_loop(0, 8, add_level, 0)
+        level = r.meta[i, 0, 1:2, 0:1]
+        chosen = lax.broadcasted_iota(jnp.int32, (256, 196 * 8), 1) == entry + level
+        r.grid[i] = free * token + dot(chosen.astype(F32).astype(BF16), r.flat[...], 1, 0)
+
+    loaded("table")
+    r.flat[...] = r.v_table[...].astype(F32).reshape(196 * 8, DEC_WIDTH).astype(BF16)
+    start_grid(0)
 
     got = []
     for i in pair:
         arrive(sent_on[i])
-        middle = r.xs[i].astype(F32) + summed(r.s1.at[i], r.r1.at[i], SHARD)
+        middle = r.xf[i, own16, :].astype(F32) + summed(r.s1.at[i], r.r1.at[i], SHARD)
         r.mid[i] = middle
         normal, _ = norm_rows(middle)
         r.n2[i, own16, :] = (normal * e_g2).astype(BF16)
         got.append(gather(r.n2.at[i], SHARD))
-    loads["w_up"].wait()
-    loads["w_down"].wait()
-    loads["w_proj"].wait()
+    start_grid(1)
+    loaded("w_up")
+    loaded("w_down")
+    loaded("w_proj")
     sent_on = []
     for i in pair:
         arrive(got[i])
@@ -898,7 +966,7 @@
         r.s2[i] = dot(hidden.astype(BF16), r.v_w_down[...], 1, 1).astype(BF16)
         sent_on.append(scatter(r.s2.at[i], r.r2.at[i], SHARD))
     arrive(got_dg)
-    loads["d_down"].wait()
+    loaded("d_down")
     r.dgh[...] = dot(r.dgf[...].reshape(512, 512), r.v_d_down[...], 1, 0)
     sent = exchange(lambda i: r.sent.at[i], slot_rows(r.arr), put_rows(r.arr))
     for i in pair:
@@ -913,9 +981,9 @@
         columns = pl.ds(pl.multiple_of(model(k) * 256, 256), 256)
         got_eo.append(send(r.eo.at[:, :, columns], r.ez.at[d, :, own16], {"mp": model(k)}))
 
-    loads["d_qkv"].wait()
-    loads["d_out"].wait()
-    loads["d_up"].wait()
+    loaded("d_qkv")
+    loaded("d_out")
+    loaded("d_up")
     cols = lax.broadcasted_iota(jnp.int32, (1, 256), 1)
     d_keep = lax.rem(cols, ROWS) < PATCHES
     sent_on = []
@@ -984,7 +1052,7 @@
         arrive(sent_on[i])
         total = summed(r.s4.at[i], r.r4.at[i], ROWS)
         normal, inverse = norm_rows(r.dmid[i])
-        grad = r.dgrad[i].astype(F32) + rows_back(normal, inverse, d_g2, total)
+        grad = r.dgf[i, own64, :].astype(F32) + rows_back(normal, inverse, d_g2, total)
         gain_sum += jnp.sum(total * normal, axis=0, keepdims=True)
         r.dgm[i, own64, :] = grad.astype(BF16)
         got.append(gather(r.dgm.at[i], ROWS))
@@ -1122,9 +1190,9 @@
     for a in (0, 1):
         block = lax.rem(s + a, 2) * 4 + d
         lefts.append(r.ga[:, pl.ds(pl.multiple_of(block * 128, 128), 128)])
-    got_w = [enc_weights(lefts, r.ha[...], 2048, r.o_down)]
+    got_w = [enc_weights(lefts, r.ha[...], 2048, r.v_o_down)]
     arrive(got_x2)
-    got_w.append(enc_weights(cut_rows(1), grad_upper, 1024, r.o_up))
+    got_w.append(enc_weights(cut_rows(1), grad_upper, 1024, r.v_o_up))
 
     arrive(got_ez)
     r.ps[...] = dot(r.ez[...].reshape(512, 256), grad_all, 0, 0).astype(BF16)
@@ -1134,14 +1202,17 @@
     total = r.w1o[mine64, :]
     for k in range(3):
         total = total + r.z1r[k].astype(F32)
-    r.o_dup[...] = total[:, :512]
-    r.o_ddown[...] = total[:, 512:]
+    r.v_o_dup[...] = total[:, :512]
+    r.v_o_ddown[...] = total[:, 512:]
+    store("o_dup", "o_ddown")
     arrive(got_z2)
     total = r.w2o[mine64, :]
     for k in range(3):
         total = total + r.z2r[k].astype(F32)
-    r.o_dqkv[...] = total[:, :384]
-    r.o_dout[...] = total[:, 384:]
+    for c in range(3):
+        r.v_o_dqkv[c] = total[:, c * 128 : (c + 1) * 128]
+    r.v_o_dout[...] = total[:, 384:]
+    store("o_dqkv", "o_dout")
     arrive(got_p)
     half_rows = pl.ds(pl.multiple_of(s * 128, 128), 128)
     r.pa[m, s] = (r.ps[half_rows, :].astype(F32) + r.pr[half_rows, :].astype(F32)).astype(BF16)
@@ -1153,40 +1224,60 @@
     r.vz[d] = total
     got_vz = along(r.vz)
     arrive(got_dec)
+    token_at = padded_row(lax.broadcasted_iota(jnp.int32, (1024, 196), 1))
+    row_at = lax.rem(lax.broadcasted_iota(jnp.int32, (1024, 1), 0), 256)
+    kept = (row_at == token_at).astype(F32).astype(BF16)
     for a in (0, 1):
-        total = r.dr[4 * a].astype(F32)
-        for k in (1, 2, 3):
-            total = total + r.dr[4 * a + k].astype(F32)
-        r.o_dec[a] = total
+        total = dot(r.dr[4 * a : 4 * a + 4].reshape(1024, 128), kept, 0, 0)
+        for i in pair:
+            r.v_o_dec[PAIR * a + i] = total[i * 64 : (i + 1) * 64]
+    store("o_dec")
     arrive(got_f)
     for a in (0, 1):
         total = r.fr[4 * a].astype(F32)
         for k in (1, 2, 3):
             total = total + r.fr[4 * a + k].astype(F32)
-        r.o_pat[a] = total.reshape(128, 128)
+        for i in pair:
+            r.o_pat[:, PAIR * a + i, :] = total[i]
     arrive(got_pa)
     got_ps = [send(r.pa.at[:, s], r.pa.at[:, s], to_plane(1, 0))]
     arrive(got_c)
     arrive(got_x4)
-    got_w.append(enc_weights(cut_rows(2), r.cz[...].reshape(512, 256), 768, r.o_out))
+    got_w.append(enc_weights(cut_rows(2), r.cz[...].reshape(512, 256), 768, r.v_o_out))
     arrive(got_x1)
     arrive(got_q)
-    got_w.append(enc_weights(cut_rows(0), r.qz[...].reshape(512, 768), 0, r.o_qkv))
-    arrive(got_vz)
-    r.o_vec[...] = r.vz[0] + r.vz[1] + r.vz[2] + r.vz[3]
+    got_w.append(enc_weights(cut_rows(0), r.qz[...].reshape(512, 768), 0, r.own_qkv))
     arrive(got_ps)
     for a in range(4):
         for b in range(2):
             at = a * 256 + b * 128
-            r.o_proj[at : at + 128, :] = r.pa[a, b].astype(F32)
-    firsts = [(2048, 1024, r.o_down), (1024, 1024, r.o_up), (768, 256, r.o_out), (0, 768, r.o_qkv)]
-    for made, (first, size, out) in zip(got_w, firsts):
+            r.v_o_proj[at : at + 128, :] = r.pa[a, b].astype(F32)
+    store("o_proj")
+    arrive(got_vz)
+    total = r.vz[0] + r.vz[1] + r.vz[2] + r.vz[3]
+    r.o_v1[...] = jnp.concatenate([total[0:1], total[1:2]], axis=1).reshape(WIDTH)
+    r.o_v2[...] = jnp.concatenate([total[2:3], total[3:4]], axis=1).reshape(WIDTH)
+    for at, out in ((4, r.o_v3), (5, r.o_v4), (6, r.o_v5)):
+        out[...] = total[at : at + 1].reshape(DEC_WIDTH)
+    firsts = [(2048, 1024), (1024, 1024), (768, 256), (0, 768)]
+    names = ["o_down", "o_up", "o_out", "o_qkv"]
+    for made, (first, size), name in zip(got_w, firsts, names):
         made.wait_recv()
-        out[...] += r.wer[:, first : first + size].astype(F32)
+        more = r.wer[:, first : first + size].astype(F32)
+        if name == "o_qkv":
+            for c in range(3):
+                at = slice(c * 256, (c + 1) * 256)
+                r.v_o_qkv[c] = r.own_qkv[:, at] + more[:, at]
+        else:
+            out = getattr(r, "v_" + name)
+            out[...] = out[...] + more
+        store(name)
     for made in started:
         made.wait_send()
     for leave in (info, sent, back):
         leave.left()
+    for made in stores:
+        made.wait()
     assert used[0] <= COPIES
 
 
@@ -1212,81 +1303,45 @@
     dec_down,
     decoded_grad,
 ):
-    s, m = lax.axis_index("section"), lax.axis_index("mp")
-
-    def own_pair(values, axis):
-        return lax.dynamic_slice_in_dim(values, PAIR * s, PAIR, axis)
-
-    rows = jnp.swapaxes(own_pair(patches, 1), 0, 1)
-    grads = jnp.swapaxes(own_pair(decoded_grad, 1), 0, 1)
-    grads = jnp.pad(grads, ((0, 0), (0, ROWS - PATCHES), (0, 0)))
-    seen = own_pair(counts, 0)
-    keep = (jnp.arange(128, dtype=jnp.int32)[None, :] < seen[:, None]).astype(F32)
-    keep = jnp.broadcast_to(keep[:, None, :], (PAIR, 8, 128))
-    index = jnp.swapaxes(own_pair(patch_index, 1), 0, 1)
-    grid_row = (index // PATCHES) * ROWS + index % PATCHES
-    slot = m * SHARD + jnp.arange(SHARD, dtype=jnp.int32)
-    grid_row = jnp.where(slot[None, :] < seen[:, None], grid_row, -1)
-    lanes = jnp.zeros((PAIR, 128), jnp.int32)
-    lanes = lax.dynamic_update_slice(lanes, grid_row, (0, m * SHARD))
-    level = jnp.where(m == 0, own_pair(scale_level, 0), 0)
-    info = jnp.concatenate(
-        [
-            lanes[:, None, :],
-            jnp.broadcast_to(level[:, None, None], (PAIR, 1, 128)),
-            jnp.zeros((PAIR, 6, 128), jnp.int32),
-        ],
-        axis=1,
-    )
-    wide = lambda v: jnp.pad(v.astype(F32), (0, WIDTH - v.shape[0]))[None, :]
-    gains = jnp.concatenate(
-        [wide(v) for v in (enc_gain_one, enc_gain_two, dec_gain_one, dec_gain_two, mask_token)]
-        + [jnp.zeros((3, WIDTH), F32)],
-        axis=0,
-    )
-    table = pos_table.reshape(8, WAYS, PATCHES, DEC_WIDTH)
-    table = jnp.pad(table, ((0, 0), (0, 0), (0, ROWS - PATCHES), (0, 0))).reshape(8, 256, DEC_WIDTH)
     inputs = (
-        rows,
-        info,
-        keep,
-        gains,
-        grads,
-        enc_qkv.reshape(WIDTH, 768),
+        patches,
+        counts,
+        patch_index.T,
+        scale_level,
+        enc_gain_one,
+        enc_gain_two,
+        dec_gain_one,
+        dec_gain_two,
+        mask_token,
+        decoded_grad,
+        jnp.swapaxes(enc_qkv, 0, 1),
         enc_out,
         enc_up,
         enc_down,
         w_proj,
-        table,
-        dec_qkv.reshape(DEC_WIDTH, 384),
+        jnp.swapaxes(pos_table, 0, 1),
+        jnp.swapaxes(dec_qkv, 0, 1),
         dec_out,
         dec_up,
         dec_down,
     )
-    shapes = (
-        (2, 256, 128),
-        (2, 128, 128),
-        (128, 768),
-        (128, 256),
-        (128, 1024),
-        (128, 1024),
-        (64, 384),
-        (64, 128),
-        (64, 512),
-        (64, 512),
-        (1024, 512),
-        (8, 512),
-    )
+    shapes = dict(STORED, o_pat=(SLOTS, 4, 128), o_v1=(WIDTH,), o_v2=(WIDTH,))
+    shapes.update(o_v3=(DEC_WIDTH,), o_v4=(DEC_WIDTH,), o_v5=(DEC_WIDTH,))
+    shapes = [jax.ShapeDtypeStruct(shapes[name], F32) for name in OUT_NAMES]
     vmem = pl.BlockSpec(memory_space=pltpu.VMEM)
+    smem = pl.BlockSpec(memory_space=pltpu.SMEM)
+    hbm = pl.BlockSpec(memory_space=pl.ANY)
     outs = pl.pallas_call(
         kernel,
-        out_shape=[jax.ShapeDtypeStruct(shape, F32) for shape in shapes],
-        in_specs=[vmem] * 5 + [pl.BlockSpec(memory_space=pl.ANY)] * 10,
-        out_specs=[vmem] * len(shapes),
+        out_shape=shapes,
+        in_specs=[vmem, smem, vmem, smem] + [vmem] * 6 + [hbm] * len(LOADED),
+        out_specs=[hbm if name in STORED else vmem for name in OUT_NAMES],
         scratch_shapes=[pltpu.VMEM(shape, kind) for shape, kind in BUFFERS.values()]
         + [pltpu.VMEM(shape, BF16) for shape in LOADED.values()]
+        + [pltpu.VMEM(shape, F32) for shape in STORED.values()]
         + [
-            pltpu.SemaphoreType.DMA((len(LOADED),)),
+            pltpu.SemaphoreType.DMA((len(LOADED) + 4,)),
+            pltpu.SemaphoreType.DMA((len(STORED),)),
             pltpu.SemaphoreType.DMA((COPIES,)),
             pltpu.SemaphoreType.DMA((COPIES,)),
         ],
@@ -1295,28 +1350,37 @@
         ),
         name="layer_pair",
     )(*inputs)
-    dec, pat, qkv, out, up, down, dqkv, dout, dup, ddown, proj, vec = outs
-    dec = dec.reshape(2, WAYS, ROWS, PAIR, 64)[:, :, :PATCHES]
-    dec = jnp.transpose(dec, (1, 2, 0, 3, 4)).reshape(WAYS * PATCHES, 4, 64)
-    pat = jnp.transpose(pat.reshape(2, PAIR, SLOTS, 128), (2, 0, 1, 3)).reshape(SLOTS, 4, 128)
-    return (
-        dec,
-        pat,
-        qkv.reshape(128, 3, 256),
-        out,
-        up,
-        down,
-        dqkv.reshape(64, 3, 128),
-        dout,
-        dup,
-        ddown,
-        proj,
-        vec[0:2].reshape(WIDTH),
-        vec[2:4].reshape(WIDTH),
-        vec[4],
-        vec[5],
-        vec[6],
-    )
+    outs = list(
+        pl.pallas_call(
+            hand_over,
+            out_shape=shapes,
+            in_specs=[hbm] * len(shapes),
+            out_specs=[hbm] * len(shapes),
+            scratch_shapes=[pltpu.VMEM(shape.shape, F32) for shape in shapes]
+            + [pltpu.SemaphoreType.DMA((len(shapes),))] * 2,
+            compiler_params=pltpu.CompilerParams(vmem_limit_bytes=60 * 2**20),
+            name="hand_over",
+        )(*outs)
+    )
+    outs[0] = jnp.transpose(outs[0], (2, 0, 1))
+    outs[2] = jnp.swapaxes(outs[2], 0, 1)
+    outs[6] = jnp.swapaxes(outs[6], 0, 1)
+    return tuple(outs)
+
+
+def hand_over(*refs):
+    count = len(OUT_NAMES)
+    given, returned, held = (refs[i * count : (i + 1) * count] for i in range(3))
+    come, go = refs[3 * count :]
+    arriving = [pltpu.make_async_copy(given[i], held[i], come.at[i]) for i in range(count)]
+    leaving = [pltpu.make_async_copy(held[i], returned[i], go.at[i]) for i in range(count)]
+    for made in arriving:
+        made.start()
+    for first, second in zip(arriving, leaving):
+        first.wait()
+        second.start()
+    for made in leaving:
+        made.wait()
 
 
 def fits_kernel(mesh, shapes):

time: 168 us -> 135 us (0.80)
  local copies, waits for them, and re-layouts: 30.2 us -> 0 us
  other arithmetic: 5.77 us -> 0 us
  Pallas kernels: 130 us -> 134 us
    unnamed x33 -> x0, local copies, waits for them, and re-layouts: 14.9 us -> none
    reshape x5 -> x0, local copies, waits for them, and re-layouts: 5.29 us -> none  [the longest x1 1.58 us: with_kernel(): enc_qkv.reshape(WIDTH, 768)]
    pallas_call x1 -> x2, Pallas kernels: 130 us -> 134 us  [the longest x1 130 us: with_kernel(): pl.pallas_call(kernel, out_shape=shapes, in_specs=[vmem, smem, vmem, smem...]
    broadcast_in_dim x5 -> x0, other arithmetic: 3.41 us -> none  [with_kernel(): wide = lambda v: jnp.pad(v.astype(F32), (0, WIDTH - v.shape[0]))[None, :]]
    pad x2 -> x0, local copies, waits for them, and re-layouts: 2.27 us -> none  [the longest x1 1.61 us: with_kernel(): jnp.pad(table, ((0, 0), (0, 0), (0, ROWS - PATCHES), (0, 0)))]
    dynamic_slice x3 -> x0, local copies, waits for them, and re-layouts: 1.81 us -> none  [own_pair(): return lax.dynamic_slice_in_dim(values, PAIR * s, PAIR, axis)]
where the time goes in v3:
time: 135 us
  Pallas kernels  134 us (99%)
    pallas_call x1, Pallas kernels, with_kernel(): pl.pallas_call(kernel, out_shape=shapes, in_specs=[vmem, smem, vmem, smem...  130 us
    pallas_call x1, Pallas kernels, with_kernel(): pl.pallas_call(hand_over, out_shape=shapes, in_specs=[hbm] * len(shapes),...  4.85 us

profile of v3, /device:TPU:0, one launch (start us, length us, event | category | flops | bytes accessed | tf_op | source)
XLA Modules:
  0.0 135.2 jit_solution(12270230776196512720)
XLA Ops:
  0.7 129.5 %layer_pair.1 = (f32[4,64,196]{2,1,0:T(8,128)}, f32[64,4,128]{2,1,0:T(4,128)}, f32[3,128,256]{2,1,0:T(8,128)}, f32[128,256]{1,0:T(8,128)}, f32[128,1024]{1,0:T(8...) custom-call(bf16[16,4,1024]{2,1,0:T(4,128)(2,1)} %refs_0_.1, ...), custom_call_target="tpu_custom_call" | custom-call | tf_op jit(solution)/shard_map/layer_pair/pallas_call | solution.py:1334
  130.2 4.9 %hand_over.1 = (f32[4,64,196]{2,1,0:T(8,128)}, f32[64,4,128]{2,1,0:T(4,128)}, f32[3,128,256]{2,1,0:T(8,128)}, f32[128,256]{1,0:T(8,128)}, f32[128,1024]{1,0:T(8,...) custom-call(f32[4,64,196]{2,1,0:T(8,128)} %get-tuple-element.48.refs, ...), custom_call_target="tpu_custom_call" | custom-call | tf_op jit(solution)/shard_map/hand_over/pallas_call | solution.py:1354

commit v4 on v3

--- a/solution.py
+++ b/solution.py
@@ -660,13 +660,14 @@
     fs=((8, 2, 64, 128), BF16),
     fr=((8, 2, 64, 128), BF16),
     cz=((4, 2, 64, 256), BF16),
-    uz=((4, 2, 64, 1024), BF16),
+    nz=((4, 2, 4, 16, 1024), BF16),
     qz=((4, 2, 64, 768), BF16),
     ez=((4, 2, 64, 256), BF16),
     sz=((4, 2, 4, 16, 512), BF16),
-    xb=((3, 2, 4, 2, 64, 128), BF16),
-    xz=((3, 4, 2, 2, 64, 128), BF16),
+    xb=((2, 2, 4, 2, 64, 128), BF16),
+    xz=((2, 4, 2, 2, 64, 128), BF16),
     ha=((512, 1024), BF16),
+    sa=((512, 1024), BF16),
     ga=((512, 1024), BF16),
     wes=((128, 3072), BF16),
     wer=((128, 3072), BF16),
@@ -728,10 +729,6 @@
         own = ref.at[pl.ds(pl.multiple_of(m * rows, rows), rows)]
         return [send(own, own, {"mp": model(k)}) for k in (1, 2, 3)]
 
-    def gather_all(ref, rows):
-        own = ref.at[:, pl.ds(pl.multiple_of(m * rows, rows), rows)]
-        return [send(own, own, {"mp": model(k)}) for k in (1, 2, 3)]
-
     def scatter(src, dst, rows):
         copies = []
         for k in (1, 2, 3):
@@ -746,15 +743,24 @@
             total = total + dst[k].astype(F32)
         return total
 
+    def relay(ref, i):
+        copies = []
+        for k in (1, 2, 3):
+            part = ref.at[data(k), i, m]
+            copies += [send(part, part, {"mp": model(j)}) for j in (1, 2, 3)]
+        return copies
+
     def along(ref):
         return [send(ref.at[d], ref.at[d], {"dp": data(k)}) for k in (1, 2, 3)]
 
-    def cuts(which, values):
+    def block_columns(which, values):
         for i, value in enumerate(values):
             for block in range(8):
                 at = slice(block * 128, (block + 1) * 128)
                 r.xb[which, block // 4, block % 4, i] = value[:, at]
         r.xz[which, d] = r.xb[which, :, d]
+
+    def send_columns(which):
         return [
             send(r.xb.at[which, :, data(k)], r.xz.at[which, d], {"dp": data(k)}) for k in (1, 2, 3)
         ]
@@ -909,6 +915,9 @@
     contexts, normeds = [], []
     for i in pair:
         arrive(got[i])
+    got_dg = []
+    for i in pair:
+        got_dg += gather(r.dgf.at[i], ROWS)
         normal, _ = norm_rows(r.xf[i].astype(F32))
         normed = (normal * e_g1).astype(BF16)
         part = dot(normed, r.v_w_qkv[...], 1, 0).astype(BF16)
@@ -920,9 +929,7 @@
         sent_on.append(scatter(r.s1.at[i], r.r1.at[i], SHARD))
         r.cz[d, i] = context
         normeds.append(normed)
-    got_c = along(r.cz)
-    got_x1 = cuts(0, normeds)
-    got_dg = gather_all(r.dgf, ROWS)
+    block_columns(0, normeds)
 
     row = lax.broadcasted_iota(jnp.int32, (256, 1), 0)
     is_real = lax.rem(row, ROWS) < PATCHES
@@ -952,6 +959,9 @@
         normal, _ = norm_rows(middle)
         r.n2[i, own16, :] = (normal * e_g2).astype(BF16)
         got.append(gather(r.n2.at[i], SHARD))
+    got_nz = [
+        send(r.n2.at[:, own16], r.nz.at[d, :, m], {"dp": data(k)}) for k in (1, 2, 3)
+    ]
     start_grid(1)
     loaded("w_up")
     loaded("w_down")
@@ -960,7 +970,6 @@
     for i in pair:
         arrive(got[i])
         upper = dot(r.n2[i], r.v_w_up[...], 1, 0)
-        r.uz[d, i] = upper.astype(BF16)
         hidden, slope = gelu_both(upper)
         r.gp[i] = slope
         r.s2[i] = dot(hidden.astype(BF16), r.v_w_down[...], 1, 1).astype(BF16)
@@ -989,6 +998,10 @@
     sent_on = []
     for i in pair:
         sent.landed(i)
+    arrive(got_nz)
+    got_nm = []
+    for i in pair:
+        got_nm += relay(r.nz, i)
         values = r.grid[i] + dot(r.hot[i], r.arr[i], 1, 0)
         r.grid[i] = values
         normal, _ = norm_rows(values)
@@ -1002,10 +1015,11 @@
         r.dctx[at, :] = context
         r.s3[i] = dot(context, r.v_d_out[...], 1, 1).astype(BF16)
         sent_on.append(scatter(r.s3.at[i], r.r3.at[i], ROWS))
-    got_u = along(r.uz)
-    got_x2 = cuts(1, [r.n2[0], r.n2[1]])
+    r.nz[d] = r.n2[...].reshape(2, 4, 16, WIDTH)
     arrive(got_eo)
     got_ez = along(r.ez)
+    got_c = along(r.cz)
+    got_x1 = send_columns(0)
     got = []
     for i in pair:
         arrive(sent_on[i])
@@ -1014,6 +1028,15 @@
         normal, _ = norm_rows(middle)
         r.dn2[i, own64, :] = (normal * d_g2).astype(BF16)
         got.append(gather(r.dn2.at[i], ROWS))
+
+    def upper_of(j):
+        at = slice(j * 128, (j + 1) * 128)
+        hidden, slope = gelu_both(dot(r.nz[j].reshape(128, WIDTH), r.v_w_up[...], 1, 0))
+        r.ha[at, :] = hidden.astype(BF16)
+        r.sa[at, :] = slope.astype(BF16)
+
+    arrive(got_nm)
+    upper_of(0)
     sent_on = []
     for i in pair:
         arrive(got[i])
@@ -1045,6 +1068,7 @@
     dec_weights(r.dn2.reshape(512, 512), r.dgu, r.w1o, r.w1s, 0)
     dec_weights(r.dgf.reshape(512, 512), r.dhid, r.w1o, r.w1s, 512)
     got_w1 = [send(r.w1s, r.w1r, to_plane(1, 0))]
+    upper_of(1)
     r.vec[...] = jnp.zeros((8, 512), F32)
     got = []
     gain_sum = jnp.zeros((1, 512), F32)
@@ -1067,19 +1091,21 @@
     for block in range(8):
         at = slice(block * 64, (block + 1) * 64)
         r.ds[block] = jnp.concatenate([parts[0][:, at], parts[1][:, at]], axis=1).astype(BF16)
-    got_dec = []
-    for a, k in plane:
-        to = lax.rem(s + a, 2) * 4 + model(k)
-        got_dec.append(send(r.ds.at[to], r.dr.at[rank], to_plane(a, k)))
-    r.dr[rank] = r.ds[rank]
+    upper_of(2)
     arrive(got_w1)
     got_z1 = dec_sums(r.w1o, r.w1r, r.z1s, r.z1r)
 
     gain_sum = jnp.zeros((1, 512), F32)
     token_sum = jnp.zeros((1, 512), F32)
     sent_on = []
+    got_dec = []
     for i in pair:
         arrive(got[i])
+        if i == 1:
+            for a, k in plane:
+                to = lax.rem(s + a, 2) * 4 + model(k)
+                got_dec.append(send(r.ds.at[to], r.dr.at[rank], to_plane(a, k)))
+            r.dr[rank] = r.ds[rank]
         at = slice(i * 256, (i + 1) * 256)
         grad_low = r.dgm[i]
         grad_context = dot(grad_low, r.v_d_out[...], 1, 0).astype(BF16)
@@ -1110,6 +1136,7 @@
     dec_weights(r.dn1, r.dgq, r.w2o, r.w2s, 0)
     dec_weights(r.dgm.reshape(512, 512), r.dctx, r.w2o, r.w2s, 384)
     got_w2 = [send(r.w2s, r.w2r, to_plane(1, 0))]
+    upper_of(3)
 
     sent_on = []
     for i in pair:
@@ -1137,15 +1164,14 @@
     r.vec[2:3, :] = gain_two[:, :512]
     r.vec[3:4, :] = gain_two[:, 512:]
     arrive(got_sz)
-    got_sm = []
-    for k in (1, 2, 3):
-        for j in (1, 2, 3):
-            part = r.sz.at[data(k), :, m]
-            got_sm.append(send(part, r.sz.at[data(k), :, m], {"mp": model(j)}))
+    got_sm = relay(r.sz, 0) + relay(r.sz, 1)
     gain_one = jnp.zeros((1, WIDTH), F32)
     got_f, got_q = [], []
     for i in pair:
         arrive(got[i])
+        if i == 1:
+            block_columns(1, [r.gm[0], r.gm[1]])
+            got_x4 = send_columns(1)
         grad_low = r.gm[i]
         grad_context = dot(grad_low, r.v_w_out[...], 1, 0).astype(BF16)
         part = attention_back(r.qkv[i], r.probs[i], grad_context, 64, 256, HEAD, e_scale)
@@ -1161,7 +1187,6 @@
             to = lax.rem(s + a, 2) * 4 + model(k)
             got_f.append(send(r.fs.at[to, i], r.fr.at[rank, i], to_plane(a, k)))
         r.fr[rank, i] = r.fs[rank, i]
-    got_x4 = cuts(2, [r.gm[0], r.gm[1]])
     r.vec[0:1, :] = gain_one[:, :512]
     r.vec[1:2, :] = gain_one[:, 512:]
     r.vr[rank] = r.vec[...]
@@ -1179,24 +1204,27 @@
     def cut_rows(which):
         return [r.xz[which, :, lax.rem(s + a, 2)].reshape(512, 128) for a in (0, 1)]
 
-    arrive(got_u)
-    hidden, slope = gelu_both(r.uz[...].reshape(512, WIDTH).astype(F32))
-    r.ha[...] = hidden.astype(BF16)
     arrive(got_sm)
     grad_all = r.sz[...].reshape(512, 512)
-    r.ga[...] = dot(grad_all, r.v_w_proj[...], 1, 1).astype(BF16)
-    grad_upper = (dot(r.ga[...], r.v_w_down[...], 1, 0) * slope).astype(BF16)
-    lefts = []
-    for a in (0, 1):
-        block = lax.rem(s + a, 2) * 4 + d
-        lefts.append(r.ga[:, pl.ds(pl.multiple_of(block * 128, 128), 128)])
-    got_w = [enc_weights(lefts, r.ha[...], 2048, r.v_o_down)]
-    arrive(got_x2)
-    got_w.append(enc_weights(cut_rows(1), grad_upper, 1024, r.v_o_up))
-
     arrive(got_ez)
     r.ps[...] = dot(r.ez[...].reshape(512, 256), grad_all, 0, 0).astype(BF16)
     got_p = [send(r.ps, r.pr, to_plane(1, 0))]
+
+    r.ga[...] = dot(grad_all, r.v_w_proj[...], 1, 1).astype(BF16)
+    grad_upper = (dot(r.ga[...], r.v_w_down[...], 1, 0) * r.sa[...].astype(F32)).astype(BF16)
+    columns = []
+    for a in (0, 1):
+        block = lax.rem(s + a, 2) * 4 + d
+        columns.append(pl.ds(pl.multiple_of(block * 128, 128), 128))
+    lefts = [r.ga[:, at] for at in columns]
+    arrive(got_p)
+    half_rows = pl.ds(pl.multiple_of(s * 128, 128), 128)
+    r.pa[m, s] = (r.ps[half_rows, :].astype(F32) + r.pr[half_rows, :].astype(F32)).astype(BF16)
+    got_pa = [send(r.pa.at[m, s], r.pa.at[m, s], {"mp": model(k)}) for k in (1, 2, 3)]
+    got_w = [enc_weights(lefts, r.ha[...], 2048, r.v_o_down)]
+    lefts = [r.nz[:, :, :, :, at].reshape(512, 128) for at in columns]
+    got_w.append(enc_weights(lefts, grad_upper, 1024, r.v_o_up))
+
     arrive(got_z1)
     mine64 = pl.ds(pl.multiple_of(d * 64, 64), 64)
     total = r.w1o[mine64, :]
@@ -1213,16 +1241,14 @@
         r.v_o_dqkv[c] = total[:, c * 128 : (c + 1) * 128]
     r.v_o_dout[...] = total[:, 384:]
     store("o_dqkv", "o_dout")
-    arrive(got_p)
-    half_rows = pl.ds(pl.multiple_of(s * 128, 128), 128)
-    r.pa[m, s] = (r.ps[half_rows, :].astype(F32) + r.pr[half_rows, :].astype(F32)).astype(BF16)
-    got_pa = [send(r.pa.at[m, s], r.pa.at[m, s], {"mp": model(k)}) for k in (1, 2, 3)]
     arrive(got_v)
     total = r.vr[0]
     for k in range(1, 8):
         total = total + r.vr[k]
     r.vz[d] = total
     got_vz = along(r.vz)
+    arrive(got_pa)
+    got_ps = [send(r.pa.at[:, s], r.pa.at[:, s], to_plane(1, 0))]
     arrive(got_dec)
     token_at = padded_row(lax.broadcasted_iota(jnp.int32, (1024, 196), 1))
     row_at = lax.rem(lax.broadcasted_iota(jnp.int32, (1024, 1), 0), 256)
@@ -1239,20 +1265,18 @@
             total = total + r.fr[4 * a + k].astype(F32)
         for i in pair:
             r.o_pat[:, PAIR * a + i, :] = total[i]
-    arrive(got_pa)
-    got_ps = [send(r.pa.at[:, s], r.pa.at[:, s], to_plane(1, 0))]
-    arrive(got_c)
-    arrive(got_x4)
-    got_w.append(enc_weights(cut_rows(2), r.cz[...].reshape(512, 256), 768, r.v_o_out))
-    arrive(got_x1)
-    arrive(got_q)
-    got_w.append(enc_weights(cut_rows(0), r.qz[...].reshape(512, 768), 0, r.own_qkv))
     arrive(got_ps)
     for a in range(4):
         for b in range(2):
             at = a * 256 + b * 128
             r.v_o_proj[at : at + 128, :] = r.pa[a, b].astype(F32)
     store("o_proj")
+    arrive(got_c)
+    arrive(got_x4)
+    got_w.append(enc_weights(cut_rows(1), r.cz[...].reshape(512, 256), 768, r.v_o_out))
+    arrive(got_x1)
+    arrive(got_q)
+    got_w.append(enc_weights(cut_rows(0), r.qz[...].reshape(512, 768), 0, r.own_qkv))
     arrive(got_vz)
     total = r.vz[0] + r.vz[1] + r.vz[2] + r.vz[3]
     r.o_v1[...] = jnp.concatenate([total[0:1], total[1:2]], axis=1).reshape(WIDTH)

time: 135 us -> 126 us (0.933)
  Pallas kernels: 134 us -> 125 us
    pallas_call x1, Pallas kernels: 130 us -> 120 us  [with_kernel(): pl.pallas_call(kernel, out_shape=shapes, in_specs=[vmem, smem, vmem, smem...]
where the time goes in v4:
time: 126 us
  Pallas kernels  125 us (99%)
    pallas_call x1, Pallas kernels, with_kernel(): pl.pallas_call(kernel, out_shape=shapes, in_specs=[vmem, smem, vmem, smem...  120 us
    pallas_call x1, Pallas kernels, with_kernel(): pl.pallas_call(hand_over, out_shape=shapes, in_specs=[hbm] * len(shapes),...  4.85 us

profile of v4, /device:TPU:0, one launch (start us, length us, event | category | flops | bytes accessed | tf_op | source)
XLA Modules:
  0.0 125.5 jit_solution(17375711064815606779)
XLA Ops:
  0.7 119.8 %layer_pair.1 = (f32[4,64,196]{2,1,0:T(8,128)}, f32[64,4,128]{2,1,0:T(4,128)}, f32[3,128,256]{2,1,0:T(8,128)}, f32[128,256]{1,0:T(8,128)}, f32[128,1024]{1,0:T(8...) custom-call(bf16[16,4,1024]{2,1,0:T(4,128)(2,1)} %refs_0_.1, ...), custom_call_target="tpu_custom_call" | custom-call | tf_op jit(solution)/shard_map/layer_pair/pallas_call | solution.py:1358
  120.5 4.9 %hand_over.1 = (f32[4,64,196]{2,1,0:T(8,128)}, f32[64,4,128]{2,1,0:T(4,128)}, f32[3,128,256]{2,1,0:T(8,128)}, f32[128,256]{1,0:T(8,128)}, f32[128,1024]{1,0:T(8,...) custom-call(f32[4,64,196]{2,1,0:T(8,128)} %get-tuple-element.48.refs, ...), custom_call_target="tpu_custom_call" | custom-call | tf_op jit(solution)/shard_map/hand_over/pallas_call | solution.py:1378

commit v5 on v4

--- a/solution.py
+++ b/solution.py
@@ -513,16 +513,18 @@
     return total
 
 
-def attention(qkv, keep, rows, width, head, scale):
-    low = head_mask(width, head, BF16)
-    wide = head_mask(width, head, F32)
-    queries = stack_heads(qkv[:, :width], low)
+def probabilities(qkv, keep, width, head, scale):
+    queries = stack_heads(qkv[:, :width], head_mask(width, head, BF16))
     scores = dot(queries, qkv[:, width : 2 * width], 1, 1) * scale
     scores = jnp.where(keep, scores, -1e30)
     weights = jnp.exp(scores - jnp.max(scores, axis=-1, keepdims=True))
-    probs = weights / jnp.sum(weights, axis=-1, keepdims=True)
+    return weights / jnp.sum(weights, axis=-1, keepdims=True)
+
+
+def attention(qkv, keep, rows, width, head, scale):
+    probs = probabilities(qkv, keep, width, head, scale)
     mixed = dot(probs.astype(BF16), qkv[:, 2 * width :], 1, 0)
-    return probs, fold_heads(mixed, wide, rows).astype(BF16)
+    return probs, fold_heads(mixed, head_mask(width, head, F32), rows).astype(BF16)
 
 
 def attention_back(qkv, probs, grad_context, rows, width, head, scale):
@@ -607,7 +609,6 @@
     info=((2, 8, 128), jnp.int32),
     flat=((1568, 512), BF16),
     xf=((2, 64, 1024), BF16),
-    qkv=((2, 64, 768), BF16),
     probs=((2, 256, 64), F32),
     s1=((2, 64, 1024), BF16),
     r1=((2, 3, 16, 1024), BF16),
@@ -661,13 +662,17 @@
     fr=((8, 2, 64, 128), BF16),
     cz=((4, 2, 64, 256), BF16),
     nz=((4, 2, 4, 16, 1024), BF16),
-    qz=((4, 2, 64, 768), BF16),
+    kz=((4, 2, 64, 768), BF16),
+    gz=((4, 2, 64, 256), BF16),
+    qa=((4, 2, 64, 768), BF16),
+    pz=((3, 2, 256, 64), F32),
+    seen=((4, 8, 128), jnp.int32),
     ez=((4, 2, 64, 256), BF16),
     sz=((4, 2, 4, 16, 512), BF16),
     xb=((2, 2, 4, 2, 64, 128), BF16),
     xz=((2, 4, 2, 2, 64, 128), BF16),
-    ha=((512, 1024), BF16),
-    sa=((512, 1024), BF16),
+    ha=((4, 2, 64, 1024), BF16),
+    sa=((4, 2, 64, 1024), BF16),
     ga=((512, 1024), BF16),
     wes=((128, 3072), BF16),
     wer=((128, 3072), BF16),
@@ -693,7 +698,6 @@
     load_sem, store_sem, send_sem, recv_sem = refs[len(names) :]
     s, d, m = (lax.axis_index(a) for a in ("section", "dp", "mp"))
     used = [0]
-    started = []
 
     def take(count):
         used[0] += count
@@ -712,11 +716,11 @@
     def send(src, dst, device):
         made = copy(src, dst, device, take(1))
         made.start()
-        started.append(made)
         return made
 
     def arrive(copies):
         for made in copies:
+            made.wait_send()
             made.wait_recv()
 
     def model(k):
@@ -903,6 +907,9 @@
         live = slot < r.counts[PAIR * s + i]
         r.info[i, 0:1, 0:SHARD] = jnp.where(live, padded_row(patch), -1)
         r.info[i, 1:2, :] = jnp.zeros((1, 128), jnp.int32) + r.levels[PAIR * s + i]
+        r.info[i, 2:3, :] = jnp.zeros((1, 128), jnp.int32) + r.counts[PAIR * s + i]
+    r.seen[d] = jnp.concatenate([r.info[0, 2:3, :]] * 4 + [r.info[1, 2:3, :]] * 4, axis=0)
+    got_seen = along(r.seen)
     info = exchange(lambda i: r.info.at[i], lambda i, at: r.meta.at[i, at], put_info)
     for i in pair:
         info.start(i)
@@ -921,7 +928,7 @@
         normal, _ = norm_rows(r.xf[i].astype(F32))
         normed = (normal * e_g1).astype(BF16)
         part = dot(normed, r.v_w_qkv[...], 1, 0).astype(BF16)
-        r.qkv[i] = part
+        r.kz[d, i] = part
         keep = lax.broadcasted_iota(jnp.int32, (1, SLOTS), 1) < r.counts[PAIR * s + i]
         probs, context = attention(part, keep, 64, 256, HEAD, e_scale)
         r.probs[i] = probs
@@ -930,6 +937,8 @@
         r.cz[d, i] = context
         normeds.append(normed)
     block_columns(0, normeds)
+    got_c = along(r.cz)
+    got_x1 = send_columns(0)
 
     row = lax.broadcasted_iota(jnp.int32, (256, 1), 0)
     is_real = lax.rem(row, ROWS) < PATCHES
@@ -998,10 +1007,10 @@
     sent_on = []
     for i in pair:
         sent.landed(i)
+    info.left()
     arrive(got_nz)
-    got_nm = []
-    for i in pair:
-        got_nm += relay(r.nz, i)
+    got_nm = [relay(r.nz, 0)]
+    for i in pair:
         values = r.grid[i] + dot(r.hot[i], r.arr[i], 1, 0)
         r.grid[i] = values
         normal, _ = norm_rows(values)
@@ -1018,8 +1027,7 @@
     r.nz[d] = r.n2[...].reshape(2, 4, 16, WIDTH)
     arrive(got_eo)
     got_ez = along(r.ez)
-    got_c = along(r.cz)
-    got_x1 = send_columns(0)
+    got_k = along(r.kz)
     got = []
     for i in pair:
         arrive(sent_on[i])
@@ -1029,13 +1037,15 @@
         r.dn2[i, own64, :] = (normal * d_g2).astype(BF16)
         got.append(gather(r.dn2.at[i], ROWS))
 
-    def upper_of(j):
-        at = slice(j * 128, (j + 1) * 128)
-        hidden, slope = gelu_both(dot(r.nz[j].reshape(128, WIDTH), r.v_w_up[...], 1, 0))
-        r.ha[at, :] = hidden.astype(BF16)
-        r.sa[at, :] = slope.astype(BF16)
-
-    arrive(got_nm)
+    sent.left()
+
+    def upper_of(i):
+        arrive(got_nm[i])
+        rows = r.nz[:, i].reshape(256, WIDTH)
+        hidden, slope = gelu_both(dot(rows, r.v_w_up[...], 1, 0))
+        r.ha[:, i] = hidden.astype(BF16).reshape(4, 64, WIDTH)
+        r.sa[:, i] = slope.astype(BF16).reshape(4, 64, WIDTH)
+
     upper_of(0)
     sent_on = []
     for i in pair:
@@ -1068,7 +1078,6 @@
     dec_weights(r.dn2.reshape(512, 512), r.dgu, r.w1o, r.w1s, 0)
     dec_weights(r.dgf.reshape(512, 512), r.dhid, r.w1o, r.w1s, 512)
     got_w1 = [send(r.w1s, r.w1r, to_plane(1, 0))]
-    upper_of(1)
     r.vec[...] = jnp.zeros((8, 512), F32)
     got = []
     gain_sum = jnp.zeros((1, 512), F32)
@@ -1091,21 +1100,24 @@
     for block in range(8):
         at = slice(block * 64, (block + 1) * 64)
         r.ds[block] = jnp.concatenate([parts[0][:, at], parts[1][:, at]], axis=1).astype(BF16)
-    upper_of(2)
+    arrive(got_seen)
+    arrive(got_k)
+
+    def probs_of(k):
+        for i in pair:
+            keep = lax.broadcasted_iota(jnp.int32, (1, SLOTS), 1) < r.seen[data(k), 4 * i, 0:1].reshape(1, 1)
+            r.pz[k - 1, i] = probabilities(r.kz[data(k), i], keep, 256, HEAD, e_scale)
+
     arrive(got_w1)
     got_z1 = dec_sums(r.w1o, r.w1r, r.z1s, r.z1r)
 
     gain_sum = jnp.zeros((1, 512), F32)
     token_sum = jnp.zeros((1, 512), F32)
     sent_on = []
-    got_dec = []
     for i in pair:
         arrive(got[i])
-        if i == 1:
-            for a, k in plane:
-                to = lax.rem(s + a, 2) * 4 + model(k)
-                got_dec.append(send(r.ds.at[to], r.dr.at[rank], to_plane(a, k)))
-            r.dr[rank] = r.ds[rank]
+        if i == 0:
+            got_nm.append(relay(r.nz, 1))
         at = slice(i * 256, (i + 1) * 256)
         grad_low = r.dgm[i]
         grad_context = dot(grad_low, r.v_d_out[...], 1, 0).astype(BF16)
@@ -1133,10 +1145,16 @@
         arrive(sent_on[i])
         r.sg[i] = summed(r.s5.at[i], r.r5.at[i], SHARD).astype(BF16)
         back.start(i)
+    got_dec = []
+    for a, k in plane:
+        to = lax.rem(s + a, 2) * 4 + model(k)
+        got_dec.append(send(r.ds.at[to], r.dr.at[rank], to_plane(a, k)))
+    r.dr[rank] = r.ds[rank]
     dec_weights(r.dn1, r.dgq, r.w2o, r.w2s, 0)
     dec_weights(r.dgm.reshape(512, 512), r.dctx, r.w2o, r.w2s, 384)
     got_w2 = [send(r.w2s, r.w2r, to_plane(1, 0))]
-    upper_of(3)
+    upper_of(1)
+    probs_of(1)
 
     sent_on = []
     for i in pair:
@@ -1148,6 +1166,7 @@
     got_sz = [
         send(r.sz.at[d, :, m], r.sz.at[d, :, m], {"dp": data(k)}) for k in (1, 2, 3)
     ]
+    probs_of(2)
     arrive(got_w2)
     got_z2 = dec_sums(r.w2o, r.w2r, r.z2s, r.z2r)
     got = []
@@ -1163,6 +1182,8 @@
         got.append(gather(r.gm.at[i], SHARD))
     r.vec[2:3, :] = gain_two[:, :512]
     r.vec[3:4, :] = gain_two[:, 512:]
+    probs_of(3)
+    back.left()
     arrive(got_sz)
     got_sm = relay(r.sz, 0) + relay(r.sz, 1)
     gain_one = jnp.zeros((1, WIDTH), F32)
@@ -1174,9 +1195,10 @@
             got_x4 = send_columns(1)
         grad_low = r.gm[i]
         grad_context = dot(grad_low, r.v_w_out[...], 1, 0).astype(BF16)
-        part = attention_back(r.qkv[i], r.probs[i], grad_context, 64, 256, HEAD, e_scale)
-        r.qz[d, i] = part
-        got_q += [send(r.qz.at[d, i], r.qz.at[d, i], {"dp": data(k)}) for k in (1, 2, 3)]
+        r.gz[d, i] = grad_context
+        got_q += [send(r.gz.at[d, i], r.gz.at[d, i], {"dp": data(k)}) for k in (1, 2, 3)]
+        part = attention_back(r.kz[d, i], r.probs[i], grad_context, 64, 256, HEAD, e_scale)
+        r.qa[d, i] = part
         terms = dot(part, r.v_w_qkv[...], 1, 1)
         normal, inverse = norm_rows(r.xf[i].astype(F32))
         gain_one += jnp.sum(terms * normal, axis=0, keepdims=True)
@@ -1211,7 +1233,7 @@
     got_p = [send(r.ps, r.pr, to_plane(1, 0))]
 
     r.ga[...] = dot(grad_all, r.v_w_proj[...], 1, 1).astype(BF16)
-    grad_upper = (dot(r.ga[...], r.v_w_down[...], 1, 0) * r.sa[...].astype(F32)).astype(BF16)
+    grad_upper = (dot(r.ga[...], r.v_w_down[...], 1, 0) * r.sa[...].reshape(512, WIDTH).astype(F32)).astype(BF16)
     columns = []
     for a in (0, 1):
         block = lax.rem(s + a, 2) * 4 + d
@@ -1221,10 +1243,17 @@
     half_rows = pl.ds(pl.multiple_of(s * 128, 128), 128)
     r.pa[m, s] = (r.ps[half_rows, :].astype(F32) + r.pr[half_rows, :].astype(F32)).astype(BF16)
     got_pa = [send(r.pa.at[m, s], r.pa.at[m, s], {"mp": model(k)}) for k in (1, 2, 3)]
-    got_w = [enc_weights(lefts, r.ha[...], 2048, r.v_o_down)]
+    got_w = [enc_weights(lefts, r.ha[...].reshape(512, WIDTH), 2048, r.v_o_down)]
     lefts = [r.nz[:, :, :, :, at].reshape(512, 128) for at in columns]
     got_w.append(enc_weights(lefts, grad_upper, 1024, r.v_o_up))
 
+    arrive(got_q)
+    for k in (1, 2, 3):
+        for i in pair:
+            at = data(k)
+            r.qa[at, i] = attention_back(
+                r.kz[at, i], r.pz[k - 1, i], r.gz[at, i], 64, 256, HEAD, e_scale
+            )
     arrive(got_z1)
     mine64 = pl.ds(pl.multiple_of(d * 64, 64), 64)
     total = r.w1o[mine64, :]
@@ -1275,8 +1304,7 @@
     arrive(got_x4)
     got_w.append(enc_weights(cut_rows(1), r.cz[...].reshape(512, 256), 768, r.v_o_out))
     arrive(got_x1)
-    arrive(got_q)
-    got_w.append(enc_weights(cut_rows(0), r.qz[...].reshape(512, 768), 0, r.own_qkv))
+    got_w.append(enc_weights(cut_rows(0), r.qa[...].reshape(512, 768), 0, r.own_qkv))
     arrive(got_vz)
     total = r.vz[0] + r.vz[1] + r.vz[2] + r.vz[3]
     r.o_v1[...] = jnp.concatenate([total[0:1], total[1:2]], axis=1).reshape(WIDTH)
@@ -1286,7 +1314,7 @@
     firsts = [(2048, 1024), (1024, 1024), (768, 256), (0, 768)]
     names = ["o_down", "o_up", "o_out", "o_qkv"]
     for made, (first, size), name in zip(got_w, firsts, names):
-        made.wait_recv()
+        arrive([made])
         more = r.wer[:, first : first + size].astype(F32)
         if name == "o_qkv":
             for c in range(3):
@@ -1296,10 +1324,6 @@
             out = getattr(r, "v_" + name)
             out[...] = out[...] + more
         store(name)
-    for made in started:
-        made.wait_send()
-    for leave in (info, sent, back):
-        leave.left()
     for made in stores:
         made.wait()
     assert used[0] <= COPIES

time: 126 us -> 118 us (0.937)
  Pallas kernels: 125 us -> 117 us
    pallas_call x1, Pallas kernels: 120 us -> 112 us  [with_kernel(): pl.pallas_call(kernel, out_shape=shapes, in_specs=[vmem, smem, vmem, smem...]
where the time goes in v5:
time: 118 us
  Pallas kernels  117 us (99%)
    pallas_call x1, Pallas kernels, with_kernel(): pl.pallas_call(kernel, out_shape=shapes, in_specs=[vmem, smem, vmem, smem...  112 us
    pallas_call x1, Pallas kernels, with_kernel(): pl.pallas_call(hand_over, out_shape=shapes, in_specs=[hbm] * len(shapes),...  4.85 us

profile of v5, /device:TPU:0, one launch (start us, length us, event | category | flops | bytes accessed | tf_op | source)
XLA Modules:
  0.0 118.1 jit_solution(1017806568894733666)
XLA Ops:
  0.7 112.4 %layer_pair.1 = (f32[4,64,196]{2,1,0:T(8,128)}, f32[64,4,128]{2,1,0:T(4,128)}, f32[3,128,256]{2,1,0:T(8,128)}, f32[128,256]{1,0:T(8,128)}, f32[128,1024]{1,0:T(8...) custom-call(bf16[16,4,1024]{2,1,0:T(4,128)(2,1)} %refs_0_.1, ...), custom_call_target="tpu_custom_call" | custom-call | tf_op jit(solution)/shard_map/layer_pair/pallas_call | solution.py:1382
  113.1 4.9 %hand_over.1 = (f32[4,64,196]{2,1,0:T(8,128)}, f32[64,4,128]{2,1,0:T(4,128)}, f32[3,128,256]{2,1,0:T(8,128)}, f32[128,256]{1,0:T(8,128)}, f32[128,1024]{1,0:T(8,...) custom-call(f32[4,64,196]{2,1,0:T(8,128)} %get-tuple-element.48.refs, ...), custom_call_target="tpu_custom_call" | custom-call | tf_op jit(solution)/shard_map/hand_over/pallas_call | solution.py:1402

commit v6 on v5

--- a/solution.py
+++ b/solution.py
@@ -518,7 +518,7 @@
     scores = dot(queries, qkv[:, width : 2 * width], 1, 1) * scale
     scores = jnp.where(keep, scores, -1e30)
     weights = jnp.exp(scores - jnp.max(scores, axis=-1, keepdims=True))
-    return weights / jnp.sum(weights, axis=-1, keepdims=True)
+    return weights * (1.0 / jnp.sum(weights, axis=-1, keepdims=True))
 
 
 def attention(qkv, keep, rows, width, head, scale):
@@ -686,6 +686,10 @@
 )
 
 
+def kind_of(name):
+    return BF16 if name == "o_proj" else F32
+
+
 class Refs:
     pass
 
@@ -922,9 +926,7 @@
     contexts, normeds = [], []
     for i in pair:
         arrive(got[i])
-    got_dg = []
-    for i in pair:
-        got_dg += gather(r.dgf.at[i], ROWS)
+    for i in pair:
         normal, _ = norm_rows(r.xf[i].astype(F32))
         normed = (normal * e_g1).astype(BF16)
         part = dot(normed, r.v_w_qkv[...], 1, 0).astype(BF16)
@@ -983,9 +985,6 @@
         r.gp[i] = slope
         r.s2[i] = dot(hidden.astype(BF16), r.v_w_down[...], 1, 1).astype(BF16)
         sent_on.append(scatter(r.s2.at[i], r.r2.at[i], SHARD))
-    arrive(got_dg)
-    loaded("d_down")
-    r.dgh[...] = dot(r.dgf[...].reshape(512, 512), r.v_d_down[...], 1, 0)
     sent = exchange(lambda i: r.sent.at[i], slot_rows(r.arr), put_rows(r.arr))
     for i in pair:
         arrive(sent_on[i])
@@ -993,6 +992,7 @@
         r.eo[i] = out_low
         r.sent[i] = dot(out_low, r.v_w_proj[...], 1, 0).astype(BF16)
         sent.start(i)
+    got_dg = gather(r.dgf.at[0], ROWS) + gather(r.dgf.at[1], ROWS)
     r.ez[d, :, own16] = r.eo[:, :, pl.ds(pl.multiple_of(m * 256, 256), 256)]
     got_eo = []
     for k in (1, 2, 3):
@@ -1046,6 +1046,9 @@
         r.ha[:, i] = hidden.astype(BF16).reshape(4, 64, WIDTH)
         r.sa[:, i] = slope.astype(BF16).reshape(4, 64, WIDTH)
 
+    arrive(got_dg)
+    loaded("d_down")
+    r.dgh[...] = dot(r.dgf[...].reshape(512, 512), r.v_d_down[...], 1, 0)
     upper_of(0)
     sent_on = []
     for i in pair:
@@ -1127,11 +1130,11 @@
         r.dgq[at, :] = part
         terms = dot(part, r.v_d_qkv[...], 1, 1)
         normal, inverse = norm_rows(r.grid[i])
-        gain_sum += jnp.sum(terms * normal, axis=0, keepdims=True)
         back = rows_back(normal, inverse, d_g1, terms) + 0.25 * grad_low.astype(F32)
-        token_sum += jnp.sum(back * r.free[i], axis=0, keepdims=True)
         r.s5[i] = dot(r.hot[i], back.astype(BF16), 0, 0).astype(BF16)
         sent_on.append(scatter(r.s5.at[i], r.r5.at[i], SHARD))
+        gain_sum += jnp.sum(terms * normal, axis=0, keepdims=True)
+        token_sum += jnp.sum(back * r.free[i], axis=0, keepdims=True)
     r.vec[4:5, :] = gain_sum
     r.vec[6:7, :] = token_sum
 
@@ -1186,17 +1189,26 @@
     back.left()
     arrive(got_sz)
     got_sm = relay(r.sz, 0) + relay(r.sz, 1)
+    arrive(got_dec)
+    token_at = padded_row(lax.broadcasted_iota(jnp.int32, (1024, 196), 1))
+    row_at = lax.rem(lax.broadcasted_iota(jnp.int32, (1024, 1), 0), 256)
+    kept = (row_at == token_at).astype(F32).astype(BF16)
+    for a in (0, 1):
+        total = dot(r.dr[4 * a : 4 * a + 4].reshape(1024, 128), kept, 0, 0)
+        for i in pair:
+            r.v_o_dec[PAIR * a + i] = total[i * 64 : (i + 1) * 64]
+    store("o_dec")
     gain_one = jnp.zeros((1, WIDTH), F32)
     got_f, got_q = [], []
     for i in pair:
         arrive(got[i])
+        grad_low = r.gm[i]
+        grad_context = dot(grad_low, r.v_w_out[...], 1, 0).astype(BF16)
+        r.gz[d, i] = grad_context
+        got_q.append([send(r.gz.at[d, i], r.gz.at[d, i], {"dp": data(k)}) for k in (1, 2, 3)])
         if i == 1:
             block_columns(1, [r.gm[0], r.gm[1]])
             got_x4 = send_columns(1)
-        grad_low = r.gm[i]
-        grad_context = dot(grad_low, r.v_w_out[...], 1, 0).astype(BF16)
-        r.gz[d, i] = grad_context
-        got_q += [send(r.gz.at[d, i], r.gz.at[d, i], {"dp": data(k)}) for k in (1, 2, 3)]
         part = attention_back(r.kz[d, i], r.probs[i], grad_context, 64, 256, HEAD, e_scale)
         r.qa[d, i] = part
         terms = dot(part, r.v_w_qkv[...], 1, 1)
@@ -1247,9 +1259,9 @@
     lefts = [r.nz[:, :, :, :, at].reshape(512, 128) for at in columns]
     got_w.append(enc_weights(lefts, grad_upper, 1024, r.v_o_up))
 
-    arrive(got_q)
-    for k in (1, 2, 3):
-        for i in pair:
+    for i in pair:
+        arrive(got_q[i])
+        for k in (1, 2, 3):
             at = data(k)
             r.qa[at, i] = attention_back(
                 r.kz[at, i], r.pz[k - 1, i], r.gz[at, i], 64, 256, HEAD, e_scale
@@ -1278,15 +1290,6 @@
     got_vz = along(r.vz)
     arrive(got_pa)
     got_ps = [send(r.pa.at[:, s], r.pa.at[:, s], to_plane(1, 0))]
-    arrive(got_dec)
-    token_at = padded_row(lax.broadcasted_iota(jnp.int32, (1024, 196), 1))
-    row_at = lax.rem(lax.broadcasted_iota(jnp.int32, (1024, 1), 0), 256)
-    kept = (row_at == token_at).astype(F32).astype(BF16)
-    for a in (0, 1):
-        total = dot(r.dr[4 * a : 4 * a + 4].reshape(1024, 128), kept, 0, 0)
-        for i in pair:
-            r.v_o_dec[PAIR * a + i] = total[i * 64 : (i + 1) * 64]
-    store("o_dec")
     arrive(got_f)
     for a in (0, 1):
         total = r.fr[4 * a].astype(F32)
@@ -1298,7 +1301,7 @@
     for a in range(4):
         for b in range(2):
             at = a * 256 + b * 128
-            r.v_o_proj[at : at + 128, :] = r.pa[a, b].astype(F32)
+            r.v_o_proj[at : at + 128, :] = r.pa[a, b]
     store("o_proj")
     arrive(got_c)
     arrive(got_x4)
@@ -1375,18 +1378,19 @@
     )
     shapes = dict(STORED, o_pat=(SLOTS, 4, 128), o_v1=(WIDTH,), o_v2=(WIDTH,))
     shapes.update(o_v3=(DEC_WIDTH,), o_v4=(DEC_WIDTH,), o_v5=(DEC_WIDTH,))
+    given = [jax.ShapeDtypeStruct(shapes[name], kind_of(name)) for name in OUT_NAMES]
     shapes = [jax.ShapeDtypeStruct(shapes[name], F32) for name in OUT_NAMES]
     vmem = pl.BlockSpec(memory_space=pltpu.VMEM)
     smem = pl.BlockSpec(memory_space=pltpu.SMEM)
     hbm = pl.BlockSpec(memory_space=pl.ANY)
     outs = pl.pallas_call(
         kernel,
-        out_shape=shapes,
+        out_shape=given,
         in_specs=[vmem, smem, vmem, smem] + [vmem] * 6 + [hbm] * len(LOADED),
         out_specs=[hbm if name in STORED else vmem for name in OUT_NAMES],
         scratch_shapes=[pltpu.VMEM(shape, kind) for shape, kind in BUFFERS.values()]
         + [pltpu.VMEM(shape, BF16) for shape in LOADED.values()]
-        + [pltpu.VMEM(shape, F32) for shape in STORED.values()]
+        + [pltpu.VMEM(shape, kind_of(name)) for name, shape in STORED.items()]
         + [
             pltpu.SemaphoreType.DMA((len(LOADED) + 4,)),
             pltpu.SemaphoreType.DMA((len(STORED),)),
@@ -1405,6 +1409,7 @@
             in_specs=[hbm] * len(shapes),
             out_specs=[hbm] * len(shapes),
             scratch_shapes=[pltpu.VMEM(shape.shape, F32) for shape in shapes]
+            + [pltpu.VMEM((WIDTH, DEC_WIDTH), BF16)]
             + [pltpu.SemaphoreType.DMA((len(shapes),))] * 2,
             compiler_params=pltpu.CompilerParams(vmem_limit_bytes=60 * 2**20),
             name="hand_over",
@@ -1419,16 +1424,22 @@
 def hand_over(*refs):
     count = len(OUT_NAMES)
     given, returned, held = (refs[i * count : (i + 1) * count] for i in range(3))
-    come, go = refs[3 * count :]
-    arriving = [pltpu.make_async_copy(given[i], held[i], come.at[i]) for i in range(count)]
-    leaving = [pltpu.make_async_copy(held[i], returned[i], go.at[i]) for i in range(count)]
-    for made in arriving:
-        made.start()
-    for first, second in zip(arriving, leaving):
-        first.wait()
-        second.start()
-    for made in leaving:
-        made.wait()
+    low, come, go = refs[3 * count :]
+    wide = OUT_NAMES.index("o_proj")
+    order = [wide] + [i for i in range(count) if i != wide]
+    arriving, leaving = {}, {}
+    for i in order:
+        landing = low if i == wide else held[i]
+        arriving[i] = pltpu.make_async_copy(given[i], landing, come.at[i])
+        leaving[i] = pltpu.make_async_copy(held[i], returned[i], go.at[i])
+        arriving[i].start()
+    for i in order:
+        arriving[i].wait()
+        if i == wide:
+            held[i][...] = low[...].astype(F32)
+        leaving[i].start()
+    for i in order:
+        leaving[i].wait()
 
 
 def fits_kernel(mesh, shapes):

time: 118 us -> 116 us (0.983)
  Pallas kernels: 117 us -> 115 us
    pallas_call x1, Pallas kernels: 112 us -> 111 us  [with_kernel(): pl.pallas_call(kernel, out_shape=given, in_specs=[vmem, smem, vmem, smem]...]
where the time goes in v6:
time: 116 us; the launch traced here: 115 us
  Pallas kernels  115 us (99%)
    pallas_call x1, Pallas kernels, with_kernel(): pl.pallas_call(kernel, out_shape=given, in_specs=[vmem, smem, vmem, smem]...  111 us
    pallas_call x1, Pallas kernels, with_kernel(): pl.pallas_call(hand_over, out_shape=shapes, in_specs=[hbm] * len(shapes),...  3.75 us

profile of v6, /device:TPU:0, one launch (start us, length us, event | category | flops | bytes accessed | tf_op | source)
XLA Modules:
  0.0 115.4 jit_solution(3873902705948196270)
XLA Ops:
  0.7 110.8 %layer_pair.1 = (f32[4,64,196]{2,1,0:T(8,128)}, f32[64,4,128]{2,1,0:T(4,128)}, f32[3,128,256]{2,1,0:T(8,128)}, f32[128,256]{1,0:T(8,128)}, f32[128,1024]{1,0:T(8...) custom-call(bf16[16,4,1024]{2,1,0:T(4,128)(2,1)} %refs_0_.1, ...), custom_call_target="tpu_custom_call" | custom-call | tf_op jit(solution)/shard_map/layer_pair/pallas_call | solution.py:1386
  111.5 3.8 %hand_over.1 = (f32[4,64,196]{2,1,0:T(8,128)}, f32[64,4,128]{2,1,0:T(4,128)}, f32[3,128,256]{2,1,0:T(8,128)}, f32[128,256]{1,0:T(8,128)}, f32[128,1024]{1,0:T(8,...) custom-call(f32[4,64,196]{2,1,0:T(8,128)} %get-tuple-element.48.refs, ...), custom_call_target="tpu_custom_call" | custom-call | tf_op jit(solution)/shard_map/hand_over/pallas_call | solution.py:1406

commit v7 on v6

--- a/solution.py
+++ b/solution.py
@@ -1410,7 +1410,7 @@
             out_specs=[hbm] * len(shapes),
             scratch_shapes=[pltpu.VMEM(shape.shape, F32) for shape in shapes]
             + [pltpu.VMEM((WIDTH, DEC_WIDTH), BF16)]
-            + [pltpu.SemaphoreType.DMA((len(shapes),))] * 2,
+            + [pltpu.SemaphoreType.DMA((len(shapes) + 3,))] * 2,
             compiler_params=pltpu.CompilerParams(vmem_limit_bytes=60 * 2**20),
             name="hand_over",
         )(*outs)
@@ -1433,12 +1433,21 @@
         arriving[i] = pltpu.make_async_copy(given[i], landing, come.at[i])
         leaving[i] = pltpu.make_async_copy(held[i], returned[i], go.at[i])
         arriving[i].start()
-    for i in order:
+    arriving[wide].wait()
+    parts = []
+    for part in range(4):
+        rows = pl.ds(part * 256, 256)
+        held[wide][rows, :] = low[rows, :].astype(F32)
+        at = go.at[wide] if part == 0 else go.at[count + part - 1]
+        made = pltpu.make_async_copy(held[wide].at[rows], returned[wide].at[rows], at)
+        made.start()
+        parts.append(made)
+    for i in order[1:]:
         arriving[i].wait()
-        if i == wide:
-            held[i][...] = low[...].astype(F32)
         leaving[i].start()
-    for i in order:
+    for made in parts:
+        made.wait()
+    for i in order[1:]:
         leaving[i].wait()
 
 

time: 116 us -> 116 us (level)
  no operation moved by 1% of the time
where the time goes in v7:
time: 116 us; the launch traced here: 115 us
  Pallas kernels  115 us (99%)
    pallas_call x1, Pallas kernels, with_kernel(): pl.pallas_call(kernel, out_shape=given, in_specs=[vmem, smem, vmem, smem]...  111 us
    pallas_call x1, Pallas kernels, with_kernel(): pl.pallas_call(hand_over, out_shape=shapes, in_specs=[hbm] * len(shapes),...  3.71 us

profile of v7, /device:TPU:0, one launch (start us, length us, event | category | flops | bytes accessed | tf_op | source)
XLA Modules:
  0.0 115.4 jit_solution(356520728943517046)
XLA Ops:
  0.7 110.8 %layer_pair.1 = (f32[4,64,196]{2,1,0:T(8,128)}, f32[64,4,128]{2,1,0:T(4,128)}, f32[3,128,256]{2,1,0:T(8,128)}, f32[128,256]{1,0:T(8,128)}, f32[128,1024]{1,0:T(8...) custom-call(bf16[16,4,1024]{2,1,0:T(4,128)(2,1)} %refs_0_.1, ...), custom_call_target="tpu_custom_call" | custom-call | tf_op jit(solution)/shard_map/layer_pair/pallas_call | solution.py:1386
  111.5 3.7 %hand_over.1 = (f32[4,64,196]{2,1,0:T(8,128)}, f32[64,4,128]{2,1,0:T(4,128)}, f32[3,128,256]{2,1,0:T(8,128)}, f32[128,256]{1,0:T(8,128)}, f32[128,1024]{1,0:T(8,...) custom-call(f32[4,64,196]{2,1,0:T(8,128)} %get-tuple-element.48.refs, ...), custom_call_target="tpu_custom_call" | custom-call | tf_op jit(solution)/shard_map/hand_over/pallas_call | solution.py:1406
